TPU v7x, 32 devices: a whole 2x2x4 slice. The times are simulated.
32 devices in a mesh: seq: 16 (over z, y, x), row: 2 (over core).
Axes of the slice: x: 2, y: 2, z: 4, core: 2. Of those that a mesh axis runs over, the one named last changes fastest.
Arguments:
- tokens: bfloat16 [4, 2048, 768], P('row', 'seq'), may hold values from -6 to 6
- cotangent: bfloat16 [4, 2048, 768], P('row', 'seq'), may hold values from -6 to 6
- doc_lengths: int32 [4, 8], P('row'), may hold values from 1 to 2041, as said below
- attn_gain: float32 [768], replicated, may hold values from 0.5 to 1.5
- ema_beta: float32 [16, 768], replicated, may hold values from -6 to 6
- alpha_raw: float32 [16, 768], replicated, may hold values from -12 to 1.5
- delta_raw: float32 [16, 768], replicated, may hold values from -12 to 0
- ema_eta: float32 [16, 768], replicated, may hold values from -1.5 to 1.5
- ema_omega: float32 [768], replicated, may hold values from -6 to 6
- w_value: bfloat16 [768, 1536], replicated, may hold values from -0.21875 to 0.21875
- w_mix: bfloat16 [768, 3200], replicated, may hold values from -0.21875 to 0.21875
- query_gain: float32 [128], replicated, may hold values from -16 to 16
- query_bias: float32 [128], replicated, may hold values from -6 to 6
- key_gain: float32 [128], replicated, may hold values from -16 to 16
- w_out: bfloat16 [1536, 768], replicated, may hold values from -0.625 to 0.625
- ffn_gain: float32 [768], replicated, may hold values from 0.5 to 1.5
- w_up: bfloat16 [768, 1536], replicated, may hold values from -0.21875 to 0.21875
- w_down: bfloat16 [1536, 768], replicated, may hold values from -0.15625 to 0.15625
Outputs:
- output: bfloat16 [4, 2048, 768], P('row', 'seq')
- grad_tokens: float32 [4, 2048, 768], P('row', 'seq')
- grad_attn_gain: float32 [768], replicated
- grad_ema_beta: float32 [16, 768], replicated
- grad_alpha_raw: float32 [16, 768], replicated
- grad_delta_raw: float32 [16, 768], replicated
- grad_ema_eta: float32 [16, 768], replicated
- grad_ema_omega: float32 [768], replicated
- grad_w_value: float32 [768, 1536], replicated
- grad_w_mix: float32 [768, 3200], replicated
- grad_query_gain: float32 [128], replicated
- grad_query_bias: float32 [128], replicated
- grad_key_gain: float32 [128], replicated
- grad_w_out: float32 [1536, 768], replicated
- grad_ffn_gain: float32 [768], replicated
- grad_w_up: float32 [768, 1536], replicated
- grad_w_down: float32 [1536, 768], replicated
Inputs may be any that keep to these rules, and one draw needn't show every extreme that they name: `doc_lengths`: each row's 8 lengths sum to 2048; in every row one document, at a place drawn from the seed, starts within the first 128 positions and ends within the last 128. In the first row all other documents have length 1.
All inputs are finite; a program needn't handle non-finite values.
Results may differ from a plain program's by a relative error of at most 0.028.
The roundings to bfloat16 on the way count: a program that leaves them out, or rounds other values in their place, can miss the bound.
Values may be sent and summed in bfloat16 or wider, within the bound.
No kernel may reach another device: no remote copies, remote signals or barrier semaphores. Data moves between devices by JAX's collectives and lax.ppermute only.
A program may use at most 320 MiB of HBM per device.

v0:
```python
import functools

import jax
import jax.numpy as jnp
from jax import lax
from jax.experimental import pallas as pl
from jax.experimental.pallas import tpu as pltpu
from jax.sharding import Mesh
from jax.sharding import PartitionSpec as P

EPSILON = 1e-05
MASKED_SCORE = -1e30
BF16 = jnp.bfloat16
F32 = jnp.float32
EVERY = ("g", "s", "core")
MIB = 1024 * 1024
BRIEF = pl.CostEstimate(flops=1, bytes_accessed=1, transcendentals=0)


def logistic(inputs):
    return 0.5 * jnp.tanh(0.5 * inputs) + 0.5


def silu_slope(inputs):
    gate = logistic(inputs)
    return gate * (1.0 + inputs * (1.0 - gate))


def norm_parts(inputs):
    centred = inputs - jnp.mean(inputs, axis=-1, keepdims=True)
    inverse = lax.rsqrt(jnp.mean(centred * centred, axis=-1, keepdims=True) + EPSILON)
    return (centred * inverse, inverse)


def norm_back(upstream, normed, inverse, gain):
    scaled = upstream * gain
    first_mean = jnp.mean(scaled, axis=-1, keepdims=True)
    second_mean = jnp.mean(scaled * normed, axis=-1, keepdims=True)
    return (
        inverse * (scaled - first_mean - normed * second_mean),
        jnp.sum(upstream * normed, axis=0),
    )


def dot(left, right, contract):
    return lax.dot_general(left, right, (contract, ((), ())), preferred_element_type=F32)


SMEM = functools.partial(pl.BlockSpec, memory_space=pltpu.SMEM)


def whole(*shape):
    return pl.BlockSpec(shape, lambda *_: (0,) * len(shape))


def first_kernel(keep_ref, x_ref, gain_ref, decay_ref, feed_ref, normed_ref, last_ref):
    segs, length, width = x_ref.shape
    for i in range(segs):
        normed_ref[i] = norm_parts(x_ref[i].astype(F32))[0] * gain_ref[...]
    part = width // 2
    for c in range(0, width, part):
        cols = slice(c, c + part)
        decay, feed = decay_ref[:, cols], feed_ref[:, cols]

        def eight(block, states):
            at = pl.multiple_of(block * 8, 8)
            rows = [normed_ref[i, pl.ds(at, 8), cols] for i in range(segs)]
            for u in range(8):
                states = tuple(
                    state * (decay * keep_ref[i, at + u]) + feed * rows[i][u : u + 1]
                    for i, state in enumerate(states)
                )
            return states

        zero = jnp.zeros(decay.shape, F32)
        states = lax.fori_loop(0, length // 8, eight, (zero,) * segs)
        for i in range(segs):
            last_ref[i, :, cols] = states[i]


def ema_first(keep, x, gain, decay, feed):
    segs, length, width = x.shape
    return pl.pallas_call(
        first_kernel,
        out_shape=(
            jax.ShapeDtypeStruct(x.shape, F32),
            jax.ShapeDtypeStruct((segs, *decay.shape), F32),
        ),
        in_specs=[SMEM()] + [pl.BlockSpec(memory_space=pltpu.VMEM)] * 4,
        out_specs=(pl.BlockSpec(memory_space=pltpu.VMEM),) * 2,
        compiler_params=pltpu.CompilerParams(vmem_limit_bytes=8 * MIB),
        cost_estimate=BRIEF,
        name="ema_first",
    )(keep, x, gain, decay, feed)


def second_kernel(
    place_ref, slot_ref, pass_ref, keep_ref, normed_ref, ends_ref, long_ref, decay_ref, feed_ref, eta_ref, omega_ref,
    smoothed_ref, mixed_ref, enter_ref,
):
    segs, length, width = normed_ref.shape
    for i in range(segs):

        def hop(p, state):
            return state * (long_ref[...] * pass_ref[p]) + ends_ref[slot_ref[p]]

        enter_ref[i] = lax.fori_loop(0, place_ref[i], hop, jnp.zeros(decay_ref.shape, F32))

    part = width // 2
    for c in range(0, width, part):
        cols = slice(c, c + part)
        decay, feed, eta = decay_ref[:, cols], feed_ref[:, cols], eta_ref[:, cols]
        omega = omega_ref[:, cols]

        def eight(block, states):
            at = pl.multiple_of(block * 8, 8)
            rows = [normed_ref[i, pl.ds(at, 8), cols] for i in range(segs)]
            sums = [[] for _ in range(segs)]
            for u in range(8):
                following = []
                for i, state in enumerate(states):
                    state = state * (decay * keep_ref[i, at + u]) + feed * rows[i][u : u + 1]
                    sums[i].append(jnp.sum(eta * state, axis=0, keepdims=True))
                    following.append(state)
                states = tuple(following)
            for i in range(segs):
                smooth = jnp.concatenate(sums[i], axis=0) + omega * rows[i]
                smoothed_ref[i, pl.ds(at, 8), cols] = smooth
            return states

        lax.fori_loop(0, length // 8, eight, tuple(enter_ref[i, :, cols] for i in range(segs)))
    smoothed = smoothed_ref[...]
    mixed_ref[...] = (smoothed * logistic(smoothed)).astype(BF16)


VMEM = functools.partial(pl.BlockSpec, memory_space=pltpu.VMEM)


def ema_second(place, slots, passes, keep, normed, ends, long_decay, decay, feed, eta, omega):
    segs, length, width = normed.shape
    return pl.pallas_call(
        second_kernel,
        out_shape=(
            jax.ShapeDtypeStruct(normed.shape, F32),
            jax.ShapeDtypeStruct(normed.shape, BF16),
            jax.ShapeDtypeStruct((segs, *decay.shape), F32),
        ),
        in_specs=[SMEM()] * 4 + [VMEM()] * 7,
        out_specs=(VMEM(),) * 3,
        compiler_params=pltpu.CompilerParams(vmem_limit_bytes=12 * MIB),
        cost_estimate=BRIEF,
        name="ema_second",
    )(place, slots, passes, keep, normed, ends, long_decay, decay, feed, eta, omega)


def fourth_kernel(
    place_ref, slot_ref, pass_ref, keep_ref, next_ref, d_ref, normed_ref, enter_ref, heads_ref, long_ref,
    decay_ref, feed_ref, eta_ref, omega_ref, alpha_ref, delta_ref, beta_ref, omega_grad_ref, grad_ref, rates_ref, before_ref,
):
    segs, length, width = normed_ref.shape
    n_heads = decay_ref.shape[0]
    half = width // 2
    for c in range(0, width, half):
        cols = slice(c, c + half)
        decay, feed = decay_ref[:, cols], feed_ref[:, cols]

        def again(block, states):
            at = pl.multiple_of(block * 8, 8)
            rows = [normed_ref[i, pl.ds(at, 8), cols] for i in range(segs)]
            for u in range(8):
                following = []
                for i, state in enumerate(states):
                    state = state * keep_ref[i, at + u]
                    before_ref[i, at + u, :, cols] = state
                    following.append(state * decay + feed * rows[i][u : u + 1])
                states = tuple(following)
            return states

        lax.fori_loop(0, length // 8, again, tuple(enter_ref[i, :, cols] for i in range(segs)))

    count = slot_ref.shape[0]
    part = width // 3
    for c in range(0, width, part):
        cols = slice(c, c + part)
        decay, feed, eta = decay_ref[:, cols], feed_ref[:, cols], eta_ref[:, cols]
        omega = omega_ref[:, cols]
        entering = []
        for i in range(segs):

            def hop(back, grad):
                p = count - 1 - back
                return grad * (long_ref[:, cols] * pass_ref[p]) + heads_ref[slot_ref[p], :, cols]

            entering.append(lax.fori_loop(0, count - 1 - place_ref[i], hop, jnp.zeros(decay.shape, F32)))

        def eight(block, carried):
            grads, kept, decayed, fed = carried
            at = pl.multiple_of(length - 8 - block * 8, 8)
            rows = [normed_ref[i, pl.ds(at, 8), cols] for i in range(segs)]
            d_rows = [d_ref[i, pl.ds(at, 8), cols] for i in range(segs)]
            sums = [[] for _ in range(segs)]
            for u in reversed(range(8)):
                following = []
                for i, grad in enumerate(grads):
                    d_row = d_rows[i][u : u + 1]
                    grad = grad * (decay * next_ref[i, at + u]) + eta * d_row
                    before = before_ref[i, at + u, :, cols]
                    kept = kept + d_row * before
                    decayed = decayed + grad * before
                    fed = fed + grad * rows[i][u : u + 1]
                    sums[i].insert(0, jnp.sum(feed * grad, axis=0, keepdims=True))
                    following.append(grad)
                grads = tuple(following)
            for i in range(segs):
                grad_ref[i, pl.ds(at, 8), cols] = jnp.concatenate(sums[i], axis=0) + omega * d_rows[i]
            return grads, kept, decayed, fed

        zero = jnp.zeros(decay.shape, F32)
        _, kept, decayed, fed = lax.fori_loop(0, length // 8, eight, (tuple(entering), zero, zero, zero))
        alpha, delta = alpha_ref[:, cols], delta_ref[:, cols]
        made = (
            alpha * fed,
            alpha * (1.0 - alpha) * (beta_ref[:, cols] * fed - delta * decayed),
            -delta * (1.0 - delta) * alpha * decayed,
            decay * kept + feed * omega_grad_ref[:, cols],
        )
        for i, gradient in enumerate(made):
            rates_ref[i * n_heads : (i + 1) * n_heads, cols] = gradient.astype(BF16)


def ema_fourth(
    place, slots, passes, keep, keep_next, d_smoothed, normed, enter, heads_grad, long_decay, decay, feed, eta, omega,
    alpha, delta, beta, omega_grad,
):
    segs, length, width = normed.shape
    return pl.pallas_call(
        fourth_kernel,
        out_shape=(
            jax.ShapeDtypeStruct(normed.shape, F32),
            jax.ShapeDtypeStruct((4 * decay.shape[0], width), BF16),
        ),
        in_specs=[SMEM()] * 5 + [VMEM()] * 13,
        out_specs=(VMEM(),) * 2,
        scratch_shapes=[pltpu.VMEM((segs, length, *decay.shape), F32)],
        compiler_params=pltpu.CompilerParams(vmem_limit_bytes=24 * MIB),
        cost_estimate=BRIEF,
        name="ema_fourth",
    )(
        place, slots, passes, keep, keep_next, d_smoothed, normed, enter, heads_grad, long_decay, decay, feed, eta, omega,
        alpha, delta, beta, omega_grad,
    )


def values_kernel(x_ref, gain_ref, w_ref, normed_ref, values_ref, slope_ref):
    segs, length, width = x_ref.shape
    x = x_ref[...].astype(F32).reshape(segs * length, width)
    normed = (norm_parts(x)[0] * gain_ref[...]).astype(BF16)
    normed_ref[...] = normed
    wide = w_ref.shape[1]
    chunk = wide // 3
    for c in range(0, wide, chunk):
        pre = dot(normed, w_ref[:, c : c + chunk], ((1,), (0,)))
        gate = logistic(pre)
        value = pre * gate
        values_ref[:, c : c + chunk] = value.astype(BF16)
        slope_ref[:, c : c + chunk] = (gate + value * (1.0 - gate)).astype(BF16)


def row_values(x, gain, w_value):
    segs, length, width = x.shape
    wide = w_value.shape[1]
    rows = 2 * length
    count = segs * length
    return pl.pallas_call(
        values_kernel,
        grid=(segs // 2,),
        out_shape=(
            jax.ShapeDtypeStruct((count, width), BF16),
            jax.ShapeDtypeStruct((count, wide), BF16),
            jax.ShapeDtypeStruct((count, wide), BF16),
        ),
        in_specs=[pl.BlockSpec((2, length, width), lambda b: (b, 0, 0)), whole(1, width), whole(width, wide)],
        out_specs=(
            pl.BlockSpec((rows, width), lambda b: (b, 0)),
            pl.BlockSpec((rows, wide), lambda b: (b, 0)),
            pl.BlockSpec((rows, wide), lambda b: (b, 0)),
        ),
        compiler_params=pltpu.CompilerParams(vmem_limit_bytes=16 * MIB),
        cost_estimate=BRIEF,
        name="row_values",
    )(x, gain, w_value)


def values_back_kernel(probs_ref, d_ref, slope_ref, w_ref, pre_ref, near_ref, far_ref):
    wide = d_ref.shape[1]
    chunk = wide // 3
    total = jnp.zeros(near_ref.shape, F32)
    for c in range(0, wide, chunk):
        cols = slice(c, c + chunk)
        d_values = dot(probs_ref[...], d_ref[:, cols], ((0,), (0,)))
        pre = (d_values * slope_ref[:, cols].astype(F32)).astype(BF16)
        pre_ref[:, cols] = pre
        total = total + dot(pre, w_ref[:, cols], ((1,), (1,)))
    step, steps = pl.program_id(0), pl.num_programs(0)

    @pl.when(step < steps // 2)
    def _():
        near_ref[...] = total.astype(BF16)

    @pl.when(step >= steps // 2)
    def _():
        far_ref[...] = total.astype(BF16)


def values_back(probs, d_attended, slope, w_value):
    count, every = probs.shape
    width, wide = w_value.shape
    rows = 256
    half = every // rows // 2
    return pl.pallas_call(
        values_back_kernel,
        grid=(every // rows,),
        out_shape=(
            jax.ShapeDtypeStruct((every, wide), BF16),
            jax.ShapeDtypeStruct((every // 2, width), BF16),
            jax.ShapeDtypeStruct((every // 2, width), BF16),
        ),
        in_specs=[
            pl.BlockSpec((count, rows), lambda b: (0, b)),
            whole(count, wide),
            pl.BlockSpec((rows, wide), lambda b: (b, 0)),
            whole(width, wide),
        ],
        out_specs=(
            pl.BlockSpec((rows, wide), lambda b: (b, 0)),
            pl.BlockSpec((rows, width), lambda b: (jnp.minimum(b, half - 1), 0)),
            pl.BlockSpec((rows, width), lambda b: (jnp.maximum(b - half, 0), 0)),
        ),
        compiler_params=pltpu.CompilerParams(vmem_limit_bytes=16 * MIB),
        cost_estimate=BRIEF,
        name="values_back",
    )(probs, d_attended, slope, w_value)


def attend_kernel(
    scale, at_ref, doc_ref, every_at_ref, every_doc_ref, q_ref, k_ref, v_ref, reset_ref,
    weight_ref, probs_ref, inverse_ref, attended_ref, gated_ref,
):
    count, every = probs_ref.shape
    chunk = 256

    @pl.when(pl.program_id(0) == 0)
    def _():
        def scores(j, highest):
            keys = pl.ds(pl.multiple_of(j * chunk, chunk), chunk)
            raw = dot(q_ref[...], k_ref[keys, :], ((1,), (1,))) * scale
            visible = (every_doc_ref[:, keys] == doc_ref[...]) & (every_at_ref[:, keys] <= at_ref[...])
            raw = jnp.where(visible, raw, MASKED_SCORE)
            weight_ref[:, keys] = raw
            return jnp.maximum(highest, jnp.maximum(raw[:, :128], raw[:, 128:]))

        highest = lax.fori_loop(0, every // chunk, scores, jnp.full((count, 128), MASKED_SCORE, F32))
        highest = jnp.max(highest, axis=1, keepdims=True)

        def weights(j, total):
            keys = pl.ds(pl.multiple_of(j * chunk, chunk), chunk)
            weight = jnp.exp(weight_ref[:, keys] - highest)
            weight_ref[:, keys] = weight
            return total + (weight[:, :128] + weight[:, 128:])

        total = lax.fori_loop(0, every // chunk, weights, jnp.zeros((count, 128), F32))
        inverse = 1.0 / jnp.sum(total, axis=1, keepdims=True)
        inverse_ref[...] = inverse

        def rounded(j, nothing):
            keys = pl.ds(pl.multiple_of(j * chunk, chunk), chunk)
            probs_ref[:, keys] = (weight_ref[:, keys] * inverse).astype(BF16)
            return nothing

        lax.fori_loop(0, every // chunk, rounded, 0)

    attended = dot(probs_ref[...], v_ref[...], ((1,), (0,)))
    attended_ref[...] = attended
    reset = reset_ref[...]
    gated_ref[...] = (reset * logistic(reset) * attended).astype(BF16)


def attend(scale, at, doc, every_at, every_doc, queries, keys, values, reset_pre):
    count, zdim = queries.shape
    every, wide = values.shape
    chunk = 256
    columns = pl.BlockSpec((count, chunk), lambda c: (0, c))
    return pl.pallas_call(
        functools.partial(attend_kernel, scale),
        grid=(wide // chunk,),
        out_shape=(
            jax.ShapeDtypeStruct((count, every), F32),
            jax.ShapeDtypeStruct((count, every), BF16),
            jax.ShapeDtypeStruct((count, 1), F32),
            jax.ShapeDtypeStruct((count, wide), F32),
            jax.ShapeDtypeStruct((count, wide), BF16),
        ),
        in_specs=[
            whole(count, 1), whole(count, 1), whole(1, every), whole(1, every),
            whole(count, zdim), whole(every, zdim), pl.BlockSpec((every, chunk), lambda c: (0, c)), columns,
        ],
        out_specs=(whole(count, every), whole(count, every), whole(count, 1), columns, columns),
        compiler_params=pltpu.CompilerParams(vmem_limit_bytes=(6 + every * 7 // 2048) * MIB),
        cost_estimate=BRIEF,
        name="attend",
    )(at, doc, every_at, every_doc, queries, keys, values, reset_pre)


def middle_kernel(
    gated_ref, attended_ref, reset_ref, update_ref, cand_ref, x_ref, cot_ref, out_w_ref, up_w_ref, down_w_ref, gain_ref,
    output_ref, in_ref, hidden_ref, d_up_ref, d_tail_ref, skip_ref, gain_grad_ref, d_attended_ref, delta_ref,
    after_ref, sum_ref, normed_ref, back_ref,
):
    count, width = x_ref.shape
    wide = gated_ref.shape[1]
    chunk = 256
    for c in range(0, width, chunk):
        cols = slice(c, c + chunk)
        cand = cand_ref[:, cols] + dot(gated_ref[...], out_w_ref[:, cols], ((1,), (0,)))
        sum_ref[:, cols] = cand
        x = x_ref[:, cols].astype(F32)
        after_ref[:, cols] = x + logistic(update_ref[:, cols]) * (cand * logistic(cand) - x)
    gain = gain_ref[...]
    tall = 64
    for r in range(0, count, tall):
        rows = slice(r, r + tall)
        normed = norm_parts(after_ref[rows, :])[0]
        normed_ref[rows, :] = normed
        in_ref[rows, :] = (normed * gain).astype(BF16)
    for c in range(0, wide, chunk):
        cols = slice(c, c + chunk)
        up = dot(in_ref[...], up_w_ref[:, cols], ((1,), (0,)))
        gate = logistic(up)
        high = up * gate
        hidden_ref[:, cols] = high.astype(BF16)
        d_hidden = dot(cot_ref[...], down_w_ref[cols, :], ((1,), (1,)))
        d_up_ref[:, cols] = (d_hidden * (gate + high * (1.0 - gate))).astype(BF16)
    for c in range(0, width, chunk):
        cols = slice(c, c + chunk)
        result = after_ref[:, cols] + dot(hidden_ref[...], down_w_ref[:, cols], ((1,), (0,)))
        output_ref[:, cols] = result.astype(BF16)
        back_ref[:, cols] = dot(d_up_ref[...], up_w_ref[cols, :], ((1,), (1,)))
    gain_grad = jnp.zeros((1, width), F32)
    for r in range(0, count, tall):
        rows = slice(r, r + tall)
        back, normed, old = back_ref[rows, :], normed_ref[rows, :], after_ref[rows, :]
        inverse = norm_parts(old)[1]
        gain_grad = gain_grad + jnp.sum(back * normed, axis=0, keepdims=True)
        scaled = back * gain
        first = jnp.mean(scaled, axis=-1, keepdims=True)
        second = jnp.mean(scaled * normed, axis=-1, keepdims=True)
        d_after = cot_ref[rows, :].astype(F32) + inverse * (scaled - first - normed * second)
        update = logistic(update_ref[rows, :])
        cand = sum_ref[rows, :]
        gate = logistic(cand)
        high = cand * gate
        skip_ref[rows, :] = d_after * (1.0 - update)
        taken = d_after * update
        d_update = taken * (1.0 - update) * (high - x_ref[rows, :].astype(F32))
        d_tail_ref[rows, wide : wide + width] = d_update.astype(BF16)
        d_tail_ref[rows, wide + width :] = (taken * (gate + high * (1.0 - gate))).astype(BF16)
    gain_grad_ref[...] = gain_grad
    delta = jnp.zeros((count, 1), F32)
    for c in range(0, wide, chunk):
        cols = slice(c, c + chunk)
        d_gated = dot(d_tail_ref[:, wide + width :], out_w_ref[cols, :], ((1,), (1,)))
        attended = attended_ref[:, cols]
        reset = reset_ref[:, cols]
        gate = logistic(reset)
        high = reset * gate
        d_tail_ref[:, cols] = (d_gated * attended * (gate + high * (1.0 - gate))).astype(BF16)
        d_attended = (d_gated * high).astype(BF16)
        d_attended_ref[:, cols] = d_attended
        delta = delta + jnp.sum(d_attended.astype(F32) * attended, axis=1, keepdims=True)
    delta_ref[...] = delta


def middle(gated, attended, reset_pre, update_pre, cand_part, x, cot, w_out, w_up, w_down, gain):
    count, width = x.shape
    wide = gated.shape[1]

    def low(*shape):
        return jax.ShapeDtypeStruct(shape, BF16)

    def full(*shape):
        return jax.ShapeDtypeStruct(shape, F32)

    return pl.pallas_call(
        middle_kernel,
        out_shape=(
            low(count, width), low(count, width), low(count, wide), low(count, wide), low(count, wide + 2 * width),
            full(count, width), full(1, width), low(count, wide), full(count, 1),
        ),
        in_specs=[VMEM()] * 11,
        out_specs=(VMEM(),) * 9,
        scratch_shapes=[pltpu.VMEM((count, width), F32)] * 4,
        compiler_params=pltpu.CompilerParams(vmem_limit_bytes=28 * MIB),
        cost_estimate=BRIEF,
        name="middle",
    )(gated, attended, reset_pre, update_pre, cand_part, x, cot, w_out, w_up, w_down, gain)


def scores_back_kernel(scale, weight_ref, inverse_ref, delta_ref, d_ref, v_ref, q_ref, k_ref, near_ref, far_ref, dq_ref):
    step, steps = pl.program_id(0), pl.num_programs(0)
    d_probs = dot(d_ref[...], v_ref[...], ((1,), (1,)))
    probs = weight_ref[...] * inverse_ref[...]
    d_score = (probs * (d_probs - delta_ref[...]) * scale).astype(BF16)
    d_keys = dot(d_score, q_ref[...], ((0,), (0,))).astype(BF16)

    @pl.when(step < steps // 2)
    def _():
        near_ref[...] = d_keys

    @pl.when(step >= steps // 2)
    def _():
        far_ref[...] = d_keys

    d_queries = dot(d_score, k_ref[...], ((1,), (0,)))

    @pl.when(step == 0)
    def _():
        dq_ref[...] = d_queries

    @pl.when(step > 0)
    def _():
        dq_ref[...] += d_queries


def scores_back(scale, weight, inverse, delta, d_attended, values, queries, keys):
    count, every = weight.shape
    zdim, wide = queries.shape[1], values.shape[1]
    rows = 256
    half = every // rows // 2
    return pl.pallas_call(
        functools.partial(scores_back_kernel, scale),
        grid=(every // rows,),
        out_shape=(
            jax.ShapeDtypeStruct((every // 2, zdim), BF16),
            jax.ShapeDtypeStruct((every // 2, zdim), BF16),
            jax.ShapeDtypeStruct((count, zdim), F32),
        ),
        in_specs=[
            pl.BlockSpec((count, rows), lambda b: (0, b)), whole(count, 1), whole(count, 1), whole(count, wide),
            pl.BlockSpec((rows, wide), lambda b: (b, 0)), whole(count, zdim), pl.BlockSpec((rows, zdim), lambda b: (b, 0)),
        ],
        out_specs=(
            pl.BlockSpec((rows, zdim), lambda b: (jnp.minimum(b, half - 1), 0)),
            pl.BlockSpec((rows, zdim), lambda b: (jnp.maximum(b - half, 0), 0)),
            whole(count, zdim),
        ),
        compiler_params=pltpu.CompilerParams(vmem_limit_bytes=10 * MIB),
        cost_estimate=BRIEF,
        name="scores_back",
    )(weight, inverse, delta, d_attended, values, queries, keys)


def third_kernel(
    next_ref, dq_ref, z_ref, query_ref, key_ref, d_tail_ref, w_ref, mixed_ref, smoothed_ref, normed_ref, decay_ref,
    eta_ref, *refs
):
    *part_refs, dz_ref, zw_ref, d_ref, head_ref, omega_ref, small_ref = refs
    segs, length, width = d_ref.shape
    zdim = dq_ref.shape[1]
    d_keys = sum(part_ref[...].astype(F32) for part_ref in part_refs)
    z, d_queries = z_ref[...], dq_ref[...]
    gate = logistic(z)
    shared = z * gate
    small_ref[0:1, :] = jnp.sum(d_queries * shared, axis=0, keepdims=True)
    small_ref[1:2, :] = jnp.sum(d_queries, axis=0, keepdims=True)
    small_ref[2:3, :] = jnp.sum(d_keys * shared, axis=0, keepdims=True)
    d_shared = d_queries * query_ref[...] + d_keys * key_ref[...]
    dz_ref[...] = (d_shared * (gate + shared * (1.0 - gate))).astype(BF16)
    zw_ref[...] = dot(dz_ref[...], mixed_ref[...], ((0,), (0,))).astype(BF16)
    part = 256
    for c in range(0, width, part):
        cols = slice(c, c + part)
        back = dot(dz_ref[...], w_ref[cols, :zdim], ((1,), (1,))) + dot(d_tail_ref[...], w_ref[cols, zdim:], ((1,), (1,)))
        omega = jnp.zeros((1, part), F32)
        for i in range(segs):
            smoothed = smoothed_ref[i, :, cols]
            gate = logistic(smoothed)
            slope = gate * (1.0 + smoothed * (1.0 - gate))
            d_smoothed = back[i * length : (i + 1) * length] * slope
            d_ref[i, :, cols] = d_smoothed
            omega = omega + jnp.sum(d_smoothed * normed_ref[i, :, cols], axis=0, keepdims=True)
        omega_ref[:, cols] = omega
    part = width // 2
    for c in range(0, width, part):
        cols = slice(c, c + part)
        decay, eta = decay_ref[:, cols], eta_ref[:, cols]

        def eight(block, grads):
            at = pl.multiple_of(length - 8 - block * 8, 8)
            rows = [d_ref[i, pl.ds(at, 8), cols] for i in range(segs)]
            for u in reversed(range(8)):
                grads = tuple(
                    grad * (decay * next_ref[i, at + u]) + eta * rows[i][u : u + 1]
                    for i, grad in enumerate(grads)
                )
            return grads

        zero = jnp.zeros(decay.shape, F32)
        grads = lax.fori_loop(0, length // 8, eight, (zero,) * segs)
        for i in range(segs):
            head_ref[i, :, cols] = grads[i]


def ema_third(
    keep_next, d_queries, z_pre, query_gain, key_gain, d_tail, w_mix, mixed_in, smoothed, normed, decay, eta, *parts
):
    segs, length, width = normed.shape
    count, zdim = z_pre.shape
    return pl.pallas_call(
        third_kernel,
        out_shape=(
            jax.ShapeDtypeStruct((count, zdim), BF16),
            jax.ShapeDtypeStruct((zdim, width), BF16),
            jax.ShapeDtypeStruct(normed.shape, F32),
            jax.ShapeDtypeStruct((segs, *decay.shape), F32),
            jax.ShapeDtypeStruct((1, width), F32),
            jax.ShapeDtypeStruct((3, zdim), F32),
        ),
        in_specs=[SMEM()] + [VMEM()] * (11 + len(parts)),
        out_specs=(VMEM(),) * 6,
        compiler_params=pltpu.CompilerParams(vmem_limit_bytes=20 * MIB),
        cost_estimate=BRIEF,
        name="ema_third",
    )(keep_next, d_queries, z_pre, query_gain, key_gain, d_tail, w_mix, mixed_in, smoothed, normed, decay, eta, *parts)


def half_kernel(halved, half_ref, slot_ref, *refs):
    *refs, low_ref, high_ref = refs
    half = low_ref.shape[0]
    blocks = 2 * half
    at = 0
    for i, kind in enumerate(halved):
        left_ref, right_ref = refs[2 * i], refs[2 * i + 1]
        (count, tall), wide = left_ref.shape, right_ref.shape[1]
        piece = min(count, 2048)
        own_left = slice(None)
        if kind == "left":
            tall //= 2
            own_left = pl.ds(pl.multiple_of(half_ref[0] * tall, 128), tall)
        else:
            wide //= 2
        rows = tall // blocks
        chunk = 384
        for c in range(0, wide, chunk):
            own_right = slice(c, c + chunk)
            if kind == "right":
                own_right = pl.ds(pl.multiple_of(half_ref[0] * wide + c, 128), chunk)
            part = sum(
                dot(left_ref[k : k + piece, own_left], right_ref[k : k + piece, own_right], ((0,), (0,)))
                for k in range(0, count, piece)
            )
            for b in range(blocks):
                slot = slot_ref[b]
                own = part[b * rows : (b + 1) * rows].astype(BF16)

                @pl.when(slot < half)
                def _():
                    low_ref[slot, at : at + rows, c : c + chunk] = own

                @pl.when(slot >= half)
                def _():
                    high_ref[slot - half, at : at + rows, c : c + chunk] = own

        at += rows


def grad_half(half, slots, halved, *pairs):
    blocks = slots.shape[0]
    rows, held = 0, 0
    for i, kind in enumerate(halved):
        left, right = pairs[2 * i], pairs[2 * i + 1]
        rows += left.shape[1] // (2 if kind == "left" else 1) // blocks
        held += 2 * (left.size + right.size) + left.shape[1] * right.shape[1]
        wide = right.shape[1] // (1 if kind == "left" else 2)
    return pl.pallas_call(
        functools.partial(half_kernel, halved),
        out_shape=(jax.ShapeDtypeStruct((blocks // 2, rows, wide), BF16),) * 2,
        in_specs=[SMEM()] * 2 + [VMEM()] * len(pairs),
        out_specs=(VMEM(),) * 2,
        compiler_params=pltpu.CompilerParams(vmem_limit_bytes=held + 8 * MIB),
        cost_estimate=BRIEF,
        name="grad_half",
    )(half, slots, *pairs)


def place_kernel(halved, lead, step, core_ref, slot_ref, near_ref, far_ref, near_other_ref, far_other_ref, *out_refs):
    half, _, wide = near_ref.shape
    core = core_ref[0]
    for b in range(step):
        slot = slot_ref[pl.program_id(0) * step + b]

        def put(own, other):
            at = 0
            for kind, out_ref in zip(halved, out_refs, strict=True):
                if kind == "right":
                    rows = out_ref.shape[1]
                    mine = pl.ds(pl.multiple_of(core * wide, 128), wide)
                    others = pl.ds(pl.multiple_of((1 - core) * wide, 128), wide)
                    out_ref[b, :, mine] = own[at : at + rows].astype(F32)
                    out_ref[b, :, others] = other[at : at + rows].astype(F32)
                else:
                    rows = out_ref.shape[2]
                    if lead:
                        out_ref[:, b, :, :lead] = jnp.zeros((2, rows, lead), F32)
                    out_ref[core, b, :, lead:] = own[at : at + rows].astype(F32)
                    out_ref[1 - core, b, :, lead:] = other[at : at + rows].astype(F32)
                at += rows

        @pl.when(slot < half)
        def _():
            put(near_ref[slot], near_other_ref[slot])

        @pl.when(slot >= half)
        def _():
            put(far_ref[slot - half], far_other_ref[slot - half])


def put_in_place(core, slots, halved, talls, lead, near, far, near_other, far_other):
    half, rows, wide = near.shape
    blocks = 2 * half
    step = 2
    shapes, specs = [], []
    for kind, tall in zip(halved, talls, strict=True):
        if kind != "left":
            each = tall // blocks
            shapes.append(jax.ShapeDtypeStruct((blocks, each, 2 * wide), F32))
            specs.append(pl.BlockSpec((step, each, 2 * wide), lambda b: (b, 0, 0)))
        else:
            each = tall // 2 // blocks
            shapes.append(jax.ShapeDtypeStruct((2, blocks, each, lead + wide), F32))
            specs.append(pl.BlockSpec((2, step, each, lead + wide), lambda b: (0, b, 0, 0)))
    outs = pl.pallas_call(
        functools.partial(place_kernel, halved, lead, step),
        grid=(blocks // step,),
        out_shape=shapes,
        in_specs=[SMEM()] * 2 + [whole(half, rows, wide)] * 4,
        out_specs=specs,
        compiler_params=pltpu.CompilerParams(vmem_limit_bytes=20 * MIB),
        cost_estimate=BRIEF,
        name="put_in_place",
    )(core, slots, near, far, near_other, far_other)
    return [out.reshape(tall, -1) for out, tall in zip(outs, talls, strict=True)]


def after(value, *others):
    return lax.optimization_barrier((value, *others))[0]


def added(one, two):
    return (one.astype(F32) + two.astype(F32)).astype(one.dtype)


CORES = [(0, 1), (1, 0)]


def swapped(part):
    return lax.ppermute(part, "core", CORES)


def across(part, bit):
    chips = lax.axis_size("g") * lax.axis_size("s")
    return lax.ppermute(part, ("g", "s"), [(i, i ^ (1 << bit)) for i in range(chips)])


class Lane:
    def __init__(self, order, back, halved):
        chips = lax.axis_size("g") * lax.axis_size("s")
        bits = chips.bit_length() - 1
        order = list(order) + [bit for bit in range(bits) if bit not in order]
        self.cut, self.rest, self.halved = order[:3], order[3:], halved
        chip = lax.axis_index(("g", "s"))
        self.core = lax.axis_index("core").reshape(1)
        block = jnp.arange(1 << len(self.cut), dtype=jnp.int32)
        count = len(self.cut)
        self.slots = block ^ sum(((chip >> bit) & 1) << (count - 1 - t) for t, bit in enumerate(self.cut))
        self.back = [bit for bit in back if bit in self.cut]
        self.back_slots = sum(
            (((block >> (count - 1 - t)) ^ (chip >> bit)) & 1) << self.back.index(bit) for t, bit in enumerate(self.cut)
        )

    def theirs(self, *pairs):
        self.talls = [left.shape[1] for left in pairs[::2]]
        low, high = grad_half(1 - self.core, self.slots, self.halved, *pairs)
        self.received, self.received_low = swapped(high), swapped(low)
        return high

    def mine(self, *pairs):
        self.low, self.kept = grad_half(self.core, self.slots, self.halved, *pairs)
        self.turn = 0
        return self.kept

    def more(self):
        return self.turn < 2 * len(self.cut) + len(self.rest)

    def near_end(self):
        return self.turn >= 2 * len(self.cut) + len(self.rest) - 1

    def step(self, *others):
        received = after(self.received, *others)
        cut, rest = self.cut, self.rest
        doubled = self.turn - len(cut) - len(rest)
        if self.turn == 0:
            self.sent = added(self.kept, received)
            self.kept = added(self.low, after(self.received_low, self.sent))
            bit = cut[0]
        elif self.turn < len(cut):
            half = self.kept.shape[0] // 2
            self.sent = added(self.kept[half:], received[half:])
            self.kept = added(self.kept[:half], received[:half])
            bit = cut[self.turn]
        elif doubled < 0:
            self.sent = self.kept = added(self.kept, received)
            bit = rest[self.turn - len(cut)]
        elif doubled == 0:
            self.sent = added(self.kept, received)
            bit = self.back[0]
        else:
            self.sent = jnp.concatenate([self.sent, received])
            bit = self.back[doubled]
        self.received = across(self.sent, bit)
        self.turn += 1
        return self.sent

    def arrive(self, *others):
        self.received = after(self.received, *others)
        self.others = swapped(after(self.sent, self.received)), swapped(self.received)
        return self.received

    def end(self, last, lead=0):
        return put_in_place(
            self.core, self.back_slots, self.halved, self.talls, lead,
            self.sent, self.received, *after(self.others, last),
        )


def local(
    tokens,
    cotangent,
    doc_lengths,
    attn_gain,
    ema_beta,
    alpha_raw,
    delta_raw,
    ema_eta,
    ema_omega,
    w_value,
    w_mix,
    query_gain,
    query_bias,
    key_gain,
    w_out,
    ffn_gain,
    w_up,
    w_down,
):
    held, seg_len, width = tokens.shape
    planes, around = lax.axis_size("g"), lax.axis_size("s")
    g, s, core = lax.axis_index("g"), lax.axis_index("s"), lax.axis_index("core")
    odd = g % 2
    count = 2 * seg_len
    zdim = query_gain.shape[0]
    vdim = w_value.shape[1]
    scale_factor = zdim ** (-0.5)

    def number(z, x, c):
        return (z * around + x) * 2 + c

    routes = [
        [
            (number(z, x, c), number(2 * c + ((z % 2) ^ a), x, z // 2))
            for z in range(planes)
            for x in range(around)
            for c in range(2)
        ]
        for a in range(2)
    ]

    def to_planes(rows):
        return jnp.concatenate(
            [
                lax.ppermute(lax.dynamic_slice_in_dim(rows, odd ^ a, 1, 0), EVERY, routes[a])
                for a in range(2)
            ]
        )

    def from_planes(segs):
        return [
            lax.ppermute(segs[a : a + 1], EVERY, [(b, a_) for a_, b in routes[a]])
            for a in range(2)
        ]

    def in_order(back):
        return jnp.concatenate(
            [jnp.where(odd == 0, back[0], back[1]), jnp.where(odd == 0, back[1], back[0])]
        )

    def nearby(part, k):
        return lax.ppermute(part, "s", [(i, i ^ k) for i in range(around)])

    def gathered_near(part):
        return jnp.concatenate([part] + [nearby(part, k) for k in range(1, around)])

    def gathered(part):
        near = gathered_near(part)
        return jnp.concatenate([near, swapped(near)])

    hops = range(around.bit_length() - 1)

    def hop_gather(part, hop):
        return jnp.concatenate([part, nearby(part, 1 << hop)])

    def hop_send(parts, hop):
        half = parts.shape[0] // 2
        return parts[:half], nearby(parts[half:], 1 << hop)

    def scattered_near(parts, received):
        mine = added(parts, received).reshape(around, parts.shape[0] // around, *parts.shape[1:])
        return mine, [nearby(mine[k], k) for k in range(1, around)]

    def scattered_sum(mine, received):
        total = mine[0].astype(F32)
        for part in received:
            total = total + part.astype(F32)
        return total

    x_rows = to_planes(tokens)

    other = lax.ppermute(doc_lengths, "core", [(0, 1), (1, 0)])
    lengths = jnp.where(g // 2 == core, doc_lengths[odd], other[odd])
    docs = lengths.shape[0]
    before_it = jnp.arange(docs)[:, None] > jnp.arange(docs)[None, :]
    starts = jnp.sum(jnp.where(before_it, lengths[None, :], 0), axis=1)

    def doc_of(positions):
        return jnp.sum((starts[:, None] <= positions[None, :]).astype(jnp.int32), axis=0) - 1

    def kept_at(positions):
        return 1.0 - jnp.any(starts[:, None] == positions[None, :], axis=0).astype(F32)

    def blocks_of(s_of, core_of):
        return [(2 * core_of + (odd ^ i)) * around + s_of for i in range(2)]

    place = jnp.stack(blocks_of(s, core))
    order = jnp.stack(
        [block for c in range(2) for k in range(around) for block in blocks_of(s ^ k, core ^ c)]
    )
    n_segs = order.shape[0]
    block = jnp.arange(n_segs, dtype=jnp.int32)
    other_core = (block // around // 2) ^ core
    near_slots = (other_core * around + ((block % around) ^ s)) * 2 + ((block // around % 2) ^ odd)
    within = jnp.arange(seg_len, dtype=jnp.int32)
    local_pos = (place[:, None] * seg_len + within).reshape(-1)
    every_pos = (order[:, None] * seg_len + within).reshape(-1)
    keep = kept_at(local_pos).reshape(2, seg_len)
    keep_next = kept_at(local_pos + 1).reshape(2, seg_len)
    row_keep = kept_at(jnp.arange(n_segs * seg_len + 1, dtype=jnp.int32))
    passes = jnp.min(row_keep[:-1].reshape(n_segs, seg_len), axis=1)
    passes_back = jnp.min(row_keep[1:].reshape(n_segs, seg_len), axis=1)

    ema_alpha = jax.nn.sigmoid(alpha_raw)
    ema_delta = jax.nn.sigmoid(delta_raw)
    decay = 1.0 - ema_alpha * ema_delta
    feed_gain = ema_alpha * ema_beta
    long_decay = decay
    reach = 1
    while reach < seg_len:
        long_decay = long_decay * long_decay
        reach *= 2
    gain_row, omega_row = attn_gain[None], ema_omega[None]

    normed_rows, ends = ema_first(keep, x_rows, gain_row, decay, feed_gain)
    near_ends = gathered_near(ends)
    every_end = jnp.concatenate([near_ends, swapped(near_ends)])
    every_x = gathered(after(x_rows, near_ends))
    cot_rows = to_planes(after(cotangent, near_ends))
    smoothed, mixed_in, states_enter = ema_second(
        place, near_slots, passes, keep, normed_rows, every_end, long_decay, decay, feed_gain, ema_eta, omega_row
    )
    mixed_in = mixed_in.reshape(count, width)

    z_pre = dot(mixed_in, w_mix[:, :zdim], ((1,), (0,)))
    shared = jax.nn.silu(z_pre)
    queries = (shared * query_gain + query_bias).astype(BF16)
    keys = (shared * key_gain).astype(BF16)
    every_key = gathered(keys)
    every_normed, values, value_slope = row_values(after(every_x, keys), gain_row, w_value)
    mixed_here = after(mixed_in, keys)
    reset_pre = dot(mixed_here, w_mix[:, zdim : zdim + vdim], ((1,), (0,)))
    update_pre = dot(mixed_here, w_mix[:, zdim + vdim : zdim + vdim + width], ((1,), (0,)))
    cand_part = dot(mixed_here, w_mix[:, zdim + vdim + width :], ((1,), (0,)))

    inputs_x = x_rows.reshape(count, width)
    weight, probs_low, inverse, attended, gated = attend(
        scale_factor, local_pos[:, None], doc_of(local_pos)[:, None], every_pos[None], doc_of(every_pos)[None],
        queries, every_key, values, reset_pre,
    )
    cot_flat = cot_rows.reshape(count, width)
    result, ffn_in, hidden, d_up, d_tail, d_skip, grad_ffn_gain, d_attended, delta_row = middle(
        gated, attended, reset_pre, update_pre, cand_part, inputs_x, cot_flat, w_out, w_up, w_down, ffn_gain[None]
    )
    d_cand = d_tail[:, vdim + width :]

    one, two = Lane((2, 0, 1, 3), (2, 1, 0), ("left", "right")), Lane((1, 0, 2, 3), (0, 1, 2), ("right",))
    three, four = Lane((2, 1, 0, 3), (0, 2, 1), ("left",)), Lane((0, 1, 2, 3), (0, 1, 2), ("left",))

    def all_step(last, *lanes):
        for lane in lanes:
            if lane.more():
                last = lane.step(last)
        return last

    last = one.theirs(gated, d_cand, ffn_in, d_up)
    last = three.theirs(after(mixed_in, last), d_tail)
    keys_sums, keys_far, d_queries = scores_back(
        scale_factor, weight, inverse, after(delta_row, last), d_attended, values, queries, every_key
    )
    keys_swapped = swapped(keys_far)
    last = one.mine(gated, d_cand, after(ffn_in, d_queries), d_up)
    last = one.step(last)
    keys_sums = added(keys_sums, after(keys_swapped, last))
    last = keys_sums
    for hop in reversed(hops):
        keys_kept, keys_near = hop_send(keys_sums, hop)
        if hop == hops[-1]:
            last = three.mine(after(mixed_in, last), d_tail)
            last = three.step(last)
            last = four.theirs(hidden, after(cot_flat, last))
        if hop > 0:
            keys_sums = added(keys_kept, after(keys_near, last))
            last = keys_sums
    last = four.mine(hidden, after(cot_flat, last))
    last = four.step(last)
    d_value_pre, normed_near_part, normed_far = values_back(
        after(probs_low, last), d_attended, value_slope, w_value
    )
    d_z_pre, grad_z, d_smoothed, grad_heads, grad_omega, grad_z_small = ema_third(
        keep_next, d_queries, z_pre, query_gain[None], key_gain[None], d_tail, w_mix, mixed_in, smoothed, normed_rows,
        decay, ema_eta, keys_kept, after(keys_near, d_value_pre),
    )
    heads = grad_heads
    for hop in hops:
        near = nearby(heads, 1 << hop)
        if hop == 0:
            last = two.theirs(every_normed, after(d_value_pre, heads))
            last = four.step(last)
            near = after(near, last)
        if hop == hops[-1]:
            last = two.mine(every_normed, after(d_value_pre, heads))
            near = after(near, last)
        heads = jnp.concatenate([heads, near])
    far = swapped(heads)
    normed_swapped = swapped(after(normed_far, heads))
    last = one.step(heads)
    last = two.step(last)
    every_head = jnp.concatenate([heads, after(far, last)])
    normed_sums = added(normed_near_part, after(normed_swapped, every_head))
    ema_normed, grad_rates = ema_fourth(
        place, near_slots, passes_back, keep, keep_next, d_smoothed, normed_rows, states_enter, every_head,
        long_decay, decay, feed_gain, ema_eta, omega_row, ema_alpha, ema_delta, ema_beta, grad_omega,
    )
    output = from_planes(after(result, grad_rates).reshape(2, seg_len, width))
    last = all_step(grad_rates, three, four, two, one)
    normed_kept, normed_near = hop_send(after(normed_sums, last, *output), hops[-1])
    output = in_order(output)
    last = all_step(last, three, four, two, one)
    for hop in reversed(hops[:-1]):
        last = added(normed_kept, after(normed_near, last))
        normed_kept, normed_near = hop_send(last, hop)
    last = all_step(last, three, four, two, one)
    d_normed = normed_kept.astype(F32) + after(normed_near, last).astype(F32)
    normed_one, inverse_one = norm_parts(inputs_x.astype(F32))
    d_norm_one, grad_attn_gain = norm_back(
        d_normed + ema_normed.reshape(count, width), normed_one, inverse_one, attn_gain
    )
    back = (d_skip + d_norm_one).astype(BF16)
    gains = jnp.concatenate(
        [
            grad_attn_gain[None],
            grad_omega,
            grad_ffn_gain,
            jnp.pad(grad_z_small.reshape(1, -1), ((0, 0), (0, width - 3 * zdim))),
            jnp.zeros((12, width), F32),
        ]
    )
    small = jnp.concatenate([grad_rates, gains.astype(BF16), grad_z])
    tall = small.shape[0] // 2
    small_far = lax.dynamic_slice_in_dim(small, (1 - core) * tall, tall)
    small_own = lax.dynamic_slice_in_dim(small, core * tall, tall)
    small, last = small_own, (small_far,)
    for bit in [None] + list(range((planes * around).bit_length() - 1)):
        small_near = swapped(small_far) if bit is None else across(after(small, *last), bit)
        last = all_step(small, *(lane for lane in (one, three, four, two) if not lane.near_end()))
        small = added(small, after(small_near, last))
        last = (small,)
        if bit == 0:
            sent_back = from_planes(after(back, small).reshape(2, seg_len, width))
        if bit == 1:
            last = (small, *sent_back)
    grad_tokens = in_order(sent_back).astype(F32)
    small_near = swapped(after(small, *last))
    last = small
    while not all(lane.near_end() for lane in (one, two, three, four)):
        last = all_step(last, *(lane for lane in (one, three, four, two) if not lane.near_end()))
    order_of_end = four, one, two, three
    last = all_step(last, *order_of_end)
    ended = {}
    for lane in order_of_end:
        last = lane.arrive(last)
    for lane in order_of_end:
        ended[lane] = lane.end(last, zdim if lane is three else 0)
        last = ended[lane][0]
    small_near = after(small_near, last)
    small = jnp.where(core == 0, jnp.concatenate([small, small_near]), jnp.concatenate([small_near, small]))
    small = small.astype(F32)
    (grad_wout, grad_up), (grad_value,), (grad_mix,), (grad_down,) = (ended[lane] for lane in (one, two, three, four))
    grad_mix = lax.dynamic_update_slice(grad_mix, small[-zdim:].T, (0, 0))
    n_heads = decay.shape[0]
    grad_beta, grad_alpha, grad_delta, grad_eta = (small[i * n_heads : (i + 1) * n_heads] for i in range(4))
    grad_attn_gain, grad_omega, grad_ffn_gain, last = (small[4 * n_heads + i] for i in range(4))
    grad_qgain, grad_qbias, grad_kgain = (last[i * zdim : (i + 1) * zdim] for i in range(3))
    return (
        output,
        grad_tokens,
        grad_attn_gain,
        grad_beta,
        grad_alpha,
        grad_delta,
        grad_eta,
        grad_omega,
        grad_value,
        grad_mix,
        grad_qgain,
        grad_qbias,
        grad_kgain,
        grad_wout,
        grad_ffn_gain,
        grad_up,
        grad_down,
    )


def solution(mesh):
    devices = mesh.devices
    finer = Mesh(devices.reshape(4, devices.shape[0] // 4, 2), EVERY)
    split = P("core", ("g", "s"), None)
    placed = (split, split, P("core", None)) + (P(),) * 15
    return jax.shard_map(
        local,
        mesh=finer,
        in_specs=placed,
        out_specs=(split, split) + (P(),) * 15,
        check_vma=False,
    )
```

profile of v0, /device:TPU:0, one launch (start us, length us, event | category | flops | bytes accessed | tf_op | source)
XLA Modules:
  0.0 359.3 jit_solution(8470255267817712718)
XLA Ops:
  2.2 2.7 collective-permute-start.2
  11.7 2.7 ema_first.1
  14.4 2.5 collective-permute-start.5
  18.0 4.1 %collective-permute-done.3 = f32[2,16,768]{2,1,0:T(8,128)S(1)} collective-permute-done((f32[2,16,768]{2,1,0:T(8,128)S(1)}, f32[2,16,768]{2,1,0:T(8,128)S(1)}, u32[]{:S(2)}, u32[]{:S(2)}) %collective-permute-start.3) | collective-permute-done | bytes 98336 | tf_op jit(solution)/shard_map/ppermute | solution.py:907
  22.1 3.4 collective-permute-start.6
  30.7 2.7 collective-permute-done.16
  33.6 5.1 %ema_second.1 = (f32[2,128,768]{2,1,0:T(8,128)S(1)}, bf16[2,128,768]{2,1,0:T(8,128)(2,1)S(1)}, f32[2,16,768]{2,1,0:T(8,128)S(1)}) custom-call(s32[2]{0:T(128)S(1)} %get-tuple-element.309.place_ref, s32[16]{0:T(128)S(1)} %fusion.18.slot_ref, f32[16]{0:T(128)S(1)} %get-tuple-element.300.pass_ref, f32[2,128]{1,0:T(2,128)S(1)} %subtract_bitcast_fusion.1.keep_ref, ...), custom_call_target="tpu_custom_call" | custom-call | flops 1 | bytes 1 | tf_op jit(solution)/shard_map/ema_second/pallas_call | solution.py:141
  39.1 1.6 collective-permute-start.9
  42.6 6.2 %collective-permute-done.12 = bf16[2,128,768]{2,1,0:T(8,128)(2,1)S(1)} collective-permute-done((bf16[2,128,768]{2,1,0:T(8,128)(2,1)S(1)}, bf16[2,128,768]{2,1,0:T(8,128)(2,1)S(1)}, u32[]{:S(2)}, u32[]{:S(2)}) %collective-permute-start.12) | collective-permute-done | bytes 393248 | tf_op jit(solution)/shard_map/ppermute | solution.py:907
  54.1 1.7 copy-done.5
  55.8 10.2 %row_values.1 = (bf16[2048,768]{1,0:T(8,128)(2,1)S(1)}, bf16[2048,1536]{1,0:T(8,128)(2,1)S(1)}, bf16[2048,1536]{1,0:T(8,128)(2,1)S(1)}) custom-call(bf16[16,128,768]{2,1,0:T(8,128)(2,1)S(1)} %constant_dynamic-update-slice_fusion.16.x_ref, f32[1,768]{1,0:T(1,128)S(1)} %broadcast_in_dim.32.gain_ref, bf16[768,1536]{1,0:T(8,128)(2,1)S(1)} %copy-done.5), custom_call_target="tpu_custom_call" | custom-call | flops 1 | bytes 1 | tf_op jit(solution)/shard_map/row_values/pallas_call | solution.py:274
  66.0 1.7 copy-done.2
  67.7 2.7 copy-done.9
  70.4 6.0 %attend.1 = (f32[256,2048]{1,0:T(8,128)S(1)}, bf16[256,2048]{1,0:T(8,128)(2,1)S(1)}, f32[256,1]{1,0:T(8,128)S(1)}, f32[256,1536]{1,0:T(8,128)S(1)}, bf16[256,1536]{1,0:T(8,128)(2,1)S(1)}) custom-call(s32[256,1]{1,0:T(8,128)S(1)} %copy.39.at_ref, s32[256,1]{1,0:T(8,128)S(1)} %copy.40.doc_ref, s32[1,2048]{1,0:T(1,128)S(1)} %bitcast.101, ...), custom_call_target="tpu_custom_call" | custom-call | flops 1 | bytes 1 | tf_op jit(solution)/shard_map/attend/pallas_call | solution.py:393
  79.4 6.1 %middle.1 = (bf16[256,768]{1,0:T(8,128)(2,1)S(1)}, bf16[256,768]{1,0:T(8,128)(2,1)S(1)}, bf16[256,1536]{1,0:T(8,128)(2,1)S(1)}, bf16[256,1536]{1,0:T(8,128)(2,1)...) custom-call(bf16[256,1536]{1,0:T(8,128)(2,1)S(1)} %get-tuple-element, ...), custom_call_target="tpu_custom_call" | custom-call | flops 1 | bytes 1 | tf_op jit(solution)/shard_map/middle/pallas_call | solution.py:493
  87.8 3.7 %grad_half.8 = (bf16[4,192,768]{2,1,0:T(8,128)(2,1)S(1)}, bf16[4,192,768]{2,1,0:T(8,128)(2,1)}) custom-call(s32[1]{0:T(128)S(6)} %sub.95.half_ref, s32[8]{0:T(128)S(1)} %copy-done.67, bf16[256,1536]{1,0:T(8,128)(2,1)S(1)} %get-tuple-element.162.gated_ref.refs_0_, bf16[256,768]{1,0:T(8,128)(2,1)S(1)} %slice.217.refs_1_, ...), custom_call_target="tpu_custom_call" | custom-call | flops 1 | bytes 1 | tf_op jit(solution)/shard_map/grad_half/pallas_call | solution.py:684
  94.8 4.0 %grad_half.9 = (bf16[4,48,3072]{2,1,0:T(8,128)(2,1)S(1)}, bf16[4,48,3072]{2,1,0:T(8,128)(2,1)S(1)}) custom-call(s32[1]{0:T(128)S(6)} %sub.95.half_ref, s32[8]{0:T(128)S(1)} %copy-done.64, bf16[256,768]{1,0:T(8,128)(2,1)S(1)} %bitcast.93, bf16[256,3072]{1,0:T(8,128)(2,1)S(1)} %get-tuple-element.169.refs_1_.d_tail_ref), custom_call_target="tpu_custom_call" | custom-call | flops 1 | bytes 1 | tf_op jit(solution)/shard_map/grad_half/pallas_call | solution.py:684
  100.4 2.8 copy-done.1
  104.8 7.5 %scores_back.1 = (bf16[1024,128]{1,0:T(8,128)(2,1)S(1)}, bf16[1024,128]{1,0:T(8,128)(2,1)S(1)}, f32[256,128]{1,0:T(8,128)S(1)}) custom-call(f32[256,2048]{1,0:T(8,128)S(1)} %copy-done.24, f32[256,1]{1,0:T(8,128)S(1)} %copy-done.53, f32[256,1]{1,0:T(8,128)S(1)} %copy-done.55, bf16[256,1536]{1,0:T(8,128)(2,1)S(1)} %copy-done.13, ...), custom_call_target="tpu_custom_call" | custom-call | flops 1 | bytes 1 | tf_op jit(solution)/shard_map/scores_back/pallas_call | solution.py:539
  112.4 2.7 grad_half.10
  117.3 2.1 collective-permute-start.30
  119.4 3.7 %grad_half.11 = (bf16[4,48,3072]{2,1,0:T(8,128)(2,1)S(1)}, bf16[4,48,3072]{2,1,0:T(8,128)(2,1)S(1)}) custom-call(s32[1]{0:T(128)} %bitcast.30.half_ref.core_ref, s32[8]{0:T(128)S(1)} %copy-done.65, bf16[256,768]{1,0:T(8,128)(2,1)S(1)} %bitcast.94, bf16[256,3072]{1,0:T(8,128)(2,1)S(1)} %get-tuple-element.169.refs_1_.d_tail_ref), custom_call_target="tpu_custom_call" | custom-call | flops 1 | bytes 1 | tf_op jit(solution)/shard_map/grad_half/pallas_call | solution.py:684
  127.2 1.9 collective-permute-done.19
  129.1 2.0 grad_half.13
  135.4 10.1 %values_back.1 = (bf16[2048,1536]{1,0:T(8,128)(2,1)S(1)}, bf16[1024,768]{1,0:T(8,128)(2,1)S(1)}, bf16[1024,768]{1,0:T(8,128)(2,1)S(1)}) custom-call(bf16[256,2048]{1,0:T(8,128)(2,1)S(1)} %copy-done.30, bf16[256,1536]{1,0:T(8,128)(2,1)S(1)} %copy-done.13, bf16[2048,1536]{1,0:T(8,128)(2,1)S(1)} %bitcast.100, bf16[768,1536]{1,0:T(8,128)(2,1)S(1)} %copy-done.6), custom_call_target="tpu_custom_call" | custom-call | flops 1 | bytes 1 | tf_op jit(solution)/shard_map/values_back/pallas_call | solution.py:320
  145.7 4.8 %ema_third.1 = (bf16[256,128]{1,0:T(8,128)(2,1)}, bf16[128,768]{1,0:T(8,128)(2,1)S(1)}, f32[2,128,768]{2,1,0:T(8,128)S(1)}, f32[2,16,768]{2,1,0:T(8,128)S(1)}, f...) custom-call(f32[2,128]{1,0:T(2,128)S(1)} %subtract_bitcast_fusion.next_ref, f32[256,128]{1,0:T(8,128)S(1)} %get-tuple-element.177.dq_ref, ...), custom_call_target="tpu_custom_call" | custom-call | flops 1 | bytes 1 | tf_op jit(solution)/shard_map/ema_third/pallas_call | solution.py:618
  151.0 4.4 %grad_half.14 = (bf16[4,96,768]{2,1,0:T(8,128)(2,1)S(1)}, bf16[4,96,768]{2,1,0:T(8,128)(2,1)S(1)}) custom-call(s32[1]{0:T(128)S(6)} %sub.95.half_ref, s32[8]{0:T(128)S(1)} %iota_xor_fusion.slot_ref, bf16[2048,768]{1,0:T(8,128)(2,1)S(1)} %copy-done.3, bf16[2048,1536]{1,0:T(8,128)(2,1)S(1)} %get-tuple-element.211.refs_1_), custom_call_target="tpu_custom_call" | custom-call | flops 1 | bytes 1 | tf_op jit(solution)/shard_map/grad_half/pallas_call | solution.py:684
  158.6 4.4 %grad_half.15 = (bf16[4,96,768]{2,1,0:T(8,128)(2,1)S(1)}, bf16[4,96,768]{2,1,0:T(8,128)(2,1)S(1)}) custom-call(s32[1]{0:T(128)} %bitcast.30.half_ref.core_ref, s32[8]{0:T(128)S(1)} %iota_xor_fusion.slot_ref, bf16[2048,768]{1,0:T(8,128)(2,1)S(1)} %copy-done.3, bf16[2048,1536]{1,0:T(8,128)(2,1)S(1)} %get-tuple-element.211.refs_1_), custom_call_target="tpu_custom_call" | custom-call | flops 1 | bytes 1 | tf_op jit(solution)/shard_map/grad_half/pallas_call | solution.py:684
  168.0 10.3 %ema_fourth.1 = (f32[2,128,768]{2,1,0:T(8,128)S(1)}, bf16[64,768]{1,0:T(8,128)(2,1)S(1)}) custom-call(s32[2]{0:T(128)S(1)} %copy-done.59, s32[16]{0:T(128)S(1)} %fusion.18.slot_ref, f32[16]{0:T(128)S(1)} %copy-done.66, f32[2,128]{1,0:T(2,128)S(1)} %subtract_bitcast_fusion.1.keep_ref, f32[2,128]{1,0:T(2,128)S(1)} %subtract_bitcast_fusion.next_ref, ...), custom_call_target="tpu_custom_call" | custom-call | flops 1 | bytes 1 | tf_op jit(solution)/shard_map/ema_fourth/pallas_call | solution.py:236
  180.2 1.7 collective-permute-start.43
  181.9 3.9 %collective-permute-done.36 = bf16[4,96,768]{2,1,0:T(8,128)(2,1)S(1)} collective-permute-done((bf16[4,96,768]{2,1,0:T(8,128)(2,1)S(1)}, bf16[4,96,768]{2,1,0:T(8,128)(2,1)S(1)}, u32[]{:S(2)}, u32[]{:S(2)}) %collective-permute-start.36) | collective-permute-done | bytes 589856 | tf_op jit(solution)/shard_map/ppermute | solution.py:771
  186.8 1.7 collective-permute-start.32
  188.6 8.9 %collective-permute-done.44 = bf16[2,48,3072]{2,1,0:T(8,128)(2,1)S(1)} collective-permute-done((bf16[2,48,3072]{2,1,0:T(8,128)(2,1)S(1)}, bf16[2,48,3072]{2,1,0:T(8,128)(2,1)S(1)}, u32[]{:S(2)}, u32[]{:S(2)}) %collective-permute-start.44) | collective-permute-done | bytes 589856 | tf_op jit(solution)/shard_map/ppermute | solution.py:771
  202.5 3.5 collective-permute-start.48
  207.6 1.7 collective-permute-start.47
  209.4 2.8 collective-permute-start.46
  212.2 10.9 %collective-permute-done.40 = bf16[512,768]{1,0:T(8,128)(2,1)S(1)} collective-permute-done((bf16[512,768]{1,0:T(8,128)(2,1)S(1)}, bf16[512,768]{1,0:T(8,128)(2,1)S(1)}, u32[]{:S(2)}, u32[]{:S(2)}) %collective-permute-start.40) | collective-permute-done | bytes 786464 | tf_op jit(solution)/shard_map/ppermute | solution.py:907
  224.2 3.3 collective-permute-start.53
  231.9 7.4 %collective-permute-done.45 = bf16[256,768]{1,0:T(8,128)(2,1)S(1)} collective-permute-done((bf16[256,768]{1,0:T(8,128)(2,1)S(1)}, bf16[256,768]{1,0:T(8,128)(2,1)S(1)}, u32[]{:S(2)}, u32[]{:S(2)}) %collective-permute-start.45) | collective-permute-done | bytes 393248 | tf_op jit(solution)/shard_map/ppermute | solution.py:907
  240.2 5.9 %collective-permute-done.54 = bf16[1,192,768]{2,1,0:T(8,128)(2,1)S(1)} collective-permute-done((bf16[1,192,768]{2,1,0:T(8,128)(2,1)S(1)}, bf16[1,192,768]{2,1,0:T(8,128)(2,1)S(1)}, u32[]{:S(2)}, u32[]{:S(2)}) %collective-permute-start.54) | collective-permute-done | bytes 294944 | tf_op jit(solution)/shard_map/ppermute | solution.py:771
  247.3 1.9 collective-permute-start.57
  251.0 1.9 collective-permute-start.55
  252.8 4.4 %collective-permute-done.57 = bf16[1,48,3072]{2,1,0:T(8,128)(2,1)S(1)} collective-permute-done((bf16[1,48,3072]{2,1,0:T(8,128)(2,1)S(1)}, bf16[1,48,3072]{2,1,0:T(8,128)(2,1)S(1)}, u32[]{:S(2)}, u32[]{:S(2)}) %collective-permute-start.57) | collective-permute-done | bytes 294944 | tf_op jit(solution)/shard_map/ppermute | solution.py:771
  257.3 3.1 collective-permute-done.56
  260.4 3.1 collective-permute-done.55
  263.5 2.1 collective-permute-start.60
  266.4 3.2 collective-permute-done.60
  269.7 2.5 collective-permute-done.59
  272.2 2.0 collective-permute-start.61
  274.2 4.8 %collective-permute-done.61 = bf16[104,768]{1,0:T(8,128)(2,1)S(1)} collective-permute-done((bf16[104,768]{1,0:T(8,128)(2,1)S(1)}, bf16[104,768]{1,0:T(8,128)(2,1)S(1)}, u32[]{:S(2)}, u32[]{:S(2)}) %collective-permute-start.61) | collective-permute-done | bytes 159776 | tf_op jit(solution)/shard_map/ppermute | solution.py:771
  279.0 6.4 %collective-permute-start.62 = (bf16[104,768]{1,0:T(8,128)(2,1)S(1)}, bf16[104,768]{1,0:T(8,128)(2,1)S(1)}, u32[]{:S(2)}, u32[]{:S(2)}) collective-permute-start(bf16[104,768]{1,0:T(8,128)(2,1)S(1)} %add_convert_fusion.29), channel_id=1, source_target_pairs={{0,16},{2,18},{4,20},{6,22},{8,24},{10,26},{12,28},{14,30},{16,0},... | collective-permute-start | bytes 479240 | tf_op jit(solution)/shard_map/ppermute | solution.py:771
  285.7 1.7 collective-permute-start.65
  287.4 5.9 %collective-permute-done.62 = bf16[104,768]{1,0:T(8,128)(2,1)S(1)} collective-permute-done((bf16[104,768]{1,0:T(8,128)(2,1)S(1)}, bf16[104,768]{1,0:T(8,128)(2,1)S(1)}, u32[]{:S(2)}, u32[]{:S(2)}) %collective-permute-start.62) | collective-permute-done | bytes 159776 | tf_op jit(solution)/shard_map/ppermute | solution.py:771
  296.1 5.5 %collective-permute-done.65 = bf16[2,96,768]{2,1,0:T(8,128)(2,1)S(1)} collective-permute-done((bf16[2,96,768]{2,1,0:T(8,128)(2,1)S(1)}, bf16[2,96,768]{2,1,0:T(8,128)(2,1)S(1)}, u32[]{:S(2)}, u32[]{:S(2)}) %collective-permute-start.65) | collective-permute-done | bytes 294944 | tf_op jit(solution)/shard_map/ppermute | solution.py:771
  301.7 2.9 collective-permute-done.64
  304.9 12.5 %collective-permute-done.71.far_ref = bf16[4,96,768]{2,1,0:T(8,128)(2,1)} collective-permute-done((bf16[4,96,768]{2,1,0:T(8,128)(2,1)S(1)}, bf16[4,96,768]{2,1,0:T(8,128)(2,1)}, u32[]{:S(2)}, u32[]{:S(2)}) %collective-permute-start.71) | collective-permute-done | bytes 589856 | tf_op jit(solution)/shard_map/ppermute | solution.py:771
  317.3 5.2 %collective-permute-done.70.far_ref = bf16[4,192,768]{2,1,0:T(8,128)(2,1)} collective-permute-done((bf16[4,192,768]{2,1,0:T(8,128)(2,1)S(1)}, bf16[4,192,768]{2,1,0:T(8,128)(2,1)}, u32[]{:S(2)}, u32[]{:S(2)}) %collective-permute-start.70) | collective-permute-done | bytes 1179680 | tf_op jit(solution)/shard_map/ppermute | solution.py:771
  322.6 2.1 collective-permute-start.76
  325.2 3.1 collective-permute-done.69.far_ref
  328.3 3.2 collective-permute-done.68.far_ref
  336.7 3.9 %put_in_place.4 = f32[2,8,96,768]{3,2,1,0:T(8,128)} custom-call(s32[1]{0:T(128)} %bitcast.30.half_ref.core_ref, s32[8]{0:T(128)S(1)} %get-tuple-element.368.slot_ref, bf16[4,96,768]{2,1,0:T(8,128)(2,1)S(1)} %pad_maximum_fusion.5.near_ref, bf16[4,96,768]{2,1,0:T(8,128)(2,1)} %collective-permute-done.71.far_ref, bf16[4,96,768]{2,1,0:T(8,128)(2,1)S(1)} %copy-done.38, ...), custom_call_target="tpu_custom_call" | custom-call | flops 1 | bytes 1 | tf_op jit(solution)/shard_map/put_in_place/pallas_call | solution.py:741
  340.5 5.9 %put_in_place.5 = (f32[2,8,96,768]{3,2,1,0:T(8,128)}, f32[8,96,1536]{2,1,0:T(8,128)}) custom-call(s32[1]{0:T(128)} %bitcast.30.half_ref.core_ref, s32[8]{0:T(128)S(1)} %get-tuple-element.369.slot_ref, bf16[4,192,768]{2,1,0:T(8,128)(2,1)S(1)} %pad_maximum_fusion.1.near_ref, bf16[4,192,768]{2,1,0:T(8,128)(2,1)} %collective-permute-done.70.far_ref, ...), custom_call_target="tpu_custom_call" | custom-call | flops 1 | bytes 1 | tf_op jit(solution)/shard_map/put_in_place/pallas_call | solution.py:741
  346.5 3.7 %put_in_place.6 = f32[8,96,1536]{2,1,0:T(8,128)} custom-call(s32[1]{0:T(128)} %bitcast.30.half_ref.core_ref, s32[8]{0:T(128)S(1)} %get-tuple-element.370.slot_ref, bf16[4,96,768]{2,1,0:T(8,128)(2,1)S(1)} %pad_maximum_fusion.6.near_ref, bf16[4,96,768]{2,1,0:T(8,128)(2,1)} %collective-permute-done.69.far_ref, ...), custom_call_target="tpu_custom_call" | custom-call | flops 1 | bytes 1 | tf_op jit(solution)/shard_map/put_in_place/pallas_call | solution.py:741
  350.2 6.1 %put_in_place.7 = f32[2,8,48,3200]{3,2,1,0:T(8,128)} custom-call(s32[1]{0:T(128)} %bitcast.30.half_ref.core_ref, s32[8]{0:T(128)S(1)} %get-tuple-element.371.slot_ref, bf16[4,48,3072]{2,1,0:T(8,128)(2,1)S(1)} %pad_maximum_fusion.2.near_ref, bf16[4,48,3072]{2,1,0:T(8,128)(2,1)} %collective-permute-done.68.far_ref, ...), custom_call_target="tpu_custom_call" | custom-call | flops 1 | bytes 1 | tf_op jit(solution)/shard_map/put_in_place/pallas_call | solution.py:741
  (447 shorter events, 84.0 us)
Async XLA Ops:
  0.7 9.8 %collective-permute-start = (s32[2,8]{1,0:T(2,128)}, s32[2,8]{1,0:T(2,128)S(1)}, u32[]{:S(2)}, u32[]{:S(2)}) collective-permute-start(s32[2,8]{1,0:T(2,128)} %param.20), channel_id=1, source_target_pairs={{0,1},{1,0},{2,3},{3,2},{4,5},{5,4},{6,7},{7,6},{8,9},{9,8},{10,11... | collective-permute-start | bytes 200 | tf_op jit(solution)/shard_map/ppermute | solution.py:937
  2.2 9.4 %collective-permute-start.2 = (bf16[1,128,768]{2,1,0:T(8,128)(2,1)S(1)}, bf16[1,128,768]{2,1,0:T(8,128)(2,1)S(1)}, u32[]{:S(2)}, u32[]{:S(2)}) collective-permute-start(bf16[1,128,768]{2,1,0:T(8,128)(2,1)S(1)} %get-tuple-element.335), channel_id=1, source_target_pairs={{0,8},{1,24},{2,10},{3,26},{4,12},{5,28},{6,14},{7,30},{8,0},{9,16... | collective-permute-start | bytes 589832 | tf_op jit(solution)/shard_map/ppermute | solution.py:890
  14.4 7.7 %collective-permute-start.5 = (f32[2,16,768]{2,1,0:T(8,128)S(1)}, f32[2,16,768]{2,1,0:T(8,128)S(1)}, u32[]{:S(2)}, u32[]{:S(2)}) collective-permute-start(f32[2,16,768]{2,1,0:T(8,128)S(1)} %get-tuple-element.156), channel_id=1, source_target_pairs={{0,6},{2,4},{4,2},{6,0},{1,7},{3,5},{5,3},{7,1},{8,14},{10,12},{12... | collective-permute-start | bytes 294920 | tf_op jit(solution)/shard_map/ppermute | solution.py:907
  22.1 11.3 %collective-permute-start.6 = (f32[8,16,768]{2,1,0:T(8,128)S(1)}, f32[8,16,768]{2,1,0:T(8,128)S(1)}, u32[]{:S(2)}, u32[]{:S(2)}) collective-permute-start(f32[8,16,768]{2,1,0:T(8,128)S(1)} %get-tuple-element.349), channel_id=1, source_target_pairs={{0,1},{1,0},{2,3},{3,2},{4,5},{5,4},{6,7},{7,6},{8,9},{9,8},{10,11... | collective-permute-start | bytes 1179656 | tf_op jit(solution)/shard_map/ppermute | solution.py:766
  26.4 7.1 %collective-permute-start.16 = (bf16[1,128,768]{2,1,0:T(8,128)(2,1)S(1)}, bf16[1,128,768]{2,1,0:T(8,128)(2,1)S(1)}, u32[]{:S(2)}, u32[]{:S(2)}) collective-permute-start(bf16[1,128,768]{2,1,0:T(8,128)(2,1)S(1)} %get-tuple-element.334), channel_id=1, source_target_pairs={{0,8},{1,24},{2,10},{3,26},{4,12},{5,28},{6,14},{7,30},{8,0},{9,16... | collective-permute-start | bytes 589832 | tf_op jit(solution)/shard_map/ppermute | solution.py:890
  27.1 14.3 %collective-permute-start.13 = (bf16[2,128,768]{2,1,0:T(8,128)(2,1)S(1)}, bf16[2,128,768]{2,1,0:T(8,128)(2,1)S(1)}, u32[]{:S(2)}, u32[]{:S(2)}) collective-permute-start(bf16[2,128,768]{2,1,0:T(8,128)(2,1)S(1)} %constant_dynamic-update-slice_fusion.x_ref), channel_id=1, source_target_pairs={{0,6},{2,4},{4,2},{6,0},{1,7},{3,5},{5,3},{7,1},{8,14},{10,12},{12... | collective-permute-start | bytes 1179656 | tf_op jit(solution)/shard_map/ppermute | solution.py:907
  28.6 20.3 %collective-permute-start.12 = (bf16[2,128,768]{2,1,0:T(8,128)(2,1)S(1)}, bf16[2,128,768]{2,1,0:T(8,128)(2,1)S(1)}, u32[]{:S(2)}, u32[]{:S(2)}) collective-permute-start(bf16[2,128,768]{2,1,0:T(8,128)(2,1)S(1)} %constant_dynamic-update-slice_fusion.x_ref), channel_id=1, source_target_pairs={{0,4},{2,6},{4,0},{6,2},{1,5},{3,7},{5,1},{7,3},{8,12},{10,14},{12... | collective-permute-start | bytes 1179656 | tf_op jit(solution)/shard_map/ppermute | solution.py:907
  29.8 19.1 %collective-permute-start.11 = (bf16[2,128,768]{2,1,0:T(8,128)(2,1)S(1)}, bf16[2,128,768]{2,1,0:T(8,128)(2,1)S(1)}, u32[]{:S(2)}, u32[]{:S(2)}) collective-permute-start(bf16[2,128,768]{2,1,0:T(8,128)(2,1)S(1)} %constant_dynamic-update-slice_fusion.x_ref), channel_id=1, source_target_pairs={{0,2},{2,0},{4,6},{6,4},{1,3},{3,1},{5,7},{7,5},{8,10},{10,8},{12,... | collective-permute-start | bytes 1179656 | tf_op jit(solution)/shard_map/ppermute | solution.py:907
  39.1 13.1 %collective-permute-start.9 = (bf16[256,128]{1,0:T(8,128)(2,1)S(1)}, bf16[256,128]{1,0:T(8,128)(2,1)S(1)}, u32[]{:S(2)}, u32[]{:S(2)}) collective-permute-start(bf16[256,128]{1,0:T(8,128)(2,1)S(1)} %get-tuple-element.305), channel_id=1, source_target_pairs={{0,6},{2,4},{4,2},{6,0},{1,7},{3,5},{5,3},{7,1},{8,14},{10,12},{12... | collective-permute-start | bytes 196616 | tf_op jit(solution)/shard_map/ppermute | solution.py:907
  40.7 11.5 %collective-permute-start.8 = (bf16[256,128]{1,0:T(8,128)(2,1)S(1)}, bf16[256,128]{1,0:T(8,128)(2,1)S(1)}, u32[]{:S(2)}, u32[]{:S(2)}) collective-permute-start(bf16[256,128]{1,0:T(8,128)(2,1)S(1)} %get-tuple-element.305), channel_id=1, source_target_pairs={{0,4},{2,6},{4,0},{6,2},{1,5},{3,7},{5,1},{7,3},{8,12},{10,14},{12... | collective-permute-start | bytes 196616 | tf_op jit(solution)/shard_map/ppermute | solution.py:907
  41.5 10.8 %collective-permute-start.7 = (bf16[256,128]{1,0:T(8,128)(2,1)S(1)}, bf16[256,128]{1,0:T(8,128)(2,1)S(1)}, u32[]{:S(2)}, u32[]{:S(2)}) collective-permute-start(bf16[256,128]{1,0:T(8,128)(2,1)S(1)} %get-tuple-element.305), channel_id=1, source_target_pairs={{0,2},{2,0},{4,6},{6,4},{1,3},{3,1},{5,7},{7,5},{8,10},{10,8},{12,... | collective-permute-start | bytes 196616 | tf_op jit(solution)/shard_map/ppermute | solution.py:907
  92.6 23.1 %collective-permute-start.18 = (bf16[4,192,768]{2,1,0:T(8,128)(2,1)}, bf16[4,192,768]{2,1,0:T(8,128)(2,1)}, u32[]{:S(2)}, u32[]{:S(2)}) collective-permute-start(bf16[4,192,768]{2,1,0:T(8,128)(2,1)} %get-tuple-element.172), channel_id=1, source_target_pairs={{0,1},{1,0},{2,3},{3,2},{4,5},{5,4},{6,7},{7,6},{8,9},{9,8},{10,11... | collective-permute-start | bytes 3538952 | tf_op jit(solution)/shard_map/ppermute | solution.py:766
  98.8 24.3 %collective-permute-start.20 = (bf16[4,48,3072]{2,1,0:T(8,128)(2,1)S(1)}, bf16[4,48,3072]{2,1,0:T(8,128)(2,1)S(1)}, u32[]{:S(2)}, u32[]{:S(2)}) collective-permute-start(bf16[4,48,3072]{2,1,0:T(8,128)(2,1)S(1)} %get-tuple-element.174), channel_id=1, source_target_pairs={{0,1},{1,0},{2,3},{3,2},{4,5},{5,4},{6,7},{7,6},{8,9},{9,8},{10,11... | collective-permute-start | bytes 3538952 | tf_op jit(solution)/shard_map/ppermute | solution.py:766
  100.1 26.6 %collective-permute-start.29 = (bf16[4,192,768]{2,1,0:T(8,128)(2,1)}, bf16[4,192,768]{2,1,0:T(8,128)(2,1)S(1)}, u32[]{:S(2)}, u32[]{:S(2)}) collective-permute-start(bf16[4,192,768]{2,1,0:T(8,128)(2,1)} %copy-done.71), channel_id=1, source_target_pairs={{0,1},{1,0},{2,3},{3,2},{4,5},{5,4},{6,7},{7,6},{8,9},{9,8},{10,11... | collective-permute-start | bytes 3538952 | tf_op jit(solution)/shard_map/ppermute | solution.py:766
  115.4 10.8 %collective-permute-start.38 = (bf16[4,48,3072]{2,1,0:T(8,128)(2,1)S(1)}, bf16[4,48,3072]{2,1,0:T(8,128)(2,1)S(1)}, u32[]{:S(2)}, u32[]{:S(2)}) collective-permute-start(bf16[4,48,3072]{2,1,0:T(8,128)(2,1)S(1)} %get-tuple-element.232), channel_id=1, source_target_pairs={{0,1},{1,0},{2,3},{3,2},{4,5},{5,4},{6,7},{7,6},{8,9},{9,8},{10,11... | collective-permute-start | bytes 3538952 | tf_op jit(solution)/shard_map/ppermute | solution.py:766
  117.3 47.2 %collective-permute-start.30 = (bf16[4,192,768]{2,1,0:T(8,128)(2,1)S(1)}, bf16[4,192,768]{2,1,0:T(8,128)(2,1)S(1)}, u32[]{:S(2)}, u32[]{:S(2)}) collective-permute-start(bf16[4,192,768]{2,1,0:T(8,128)(2,1)S(1)} %add_convert_fusion.4), channel_id=1, source_target_pairs={{0,8},{2,10},{4,12},{6,14},{8,0},{10,2},{12,4},{14,6},{16,24},{18,... | collective-permute-start | bytes 3538952 | tf_op jit(solution)/shard_map/ppermute | solution.py:771
  123.6 54.8 %collective-permute-start.39 = (bf16[4,48,3072]{2,1,0:T(8,128)(2,1)S(1)}, bf16[4,48,3072]{2,1,0:T(8,128)(2,1)S(1)}, u32[]{:S(2)}, u32[]{:S(2)}) collective-permute-start(bf16[4,48,3072]{2,1,0:T(8,128)(2,1)S(1)} %add_convert_fusion.3), channel_id=1, source_target_pairs={{0,8},{2,10},{4,12},{6,14},{8,0},{10,2},{12,4},{14,6},{16,24},{18,... | collective-permute-start | bytes 3538952 | tf_op jit(solution)/shard_map/ppermute | solution.py:771
  126.7 28.8 %collective-permute-start.24 = (bf16[4,96,768]{2,1,0:T(8,128)(2,1)S(1)}, bf16[4,96,768]{2,1,0:T(8,128)(2,1)S(1)}, u32[]{:S(2)}, u32[]{:S(2)}) collective-permute-start(bf16[4,96,768]{2,1,0:T(8,128)(2,1)S(1)} %get-tuple-element.204), channel_id=1, source_target_pairs={{0,1},{1,0},{2,3},{3,2},{4,5},{5,4},{6,7},{7,6},{8,9},{9,8},{10,11... | collective-permute-start | bytes 1769480 | tf_op jit(solution)/shard_map/ppermute | solution.py:766
  131.2 14.4 %collective-permute-start.21 = (bf16[256,128]{1,0:T(8,128)(2,1)S(1)}, bf16[256,128]{1,0:T(8,128)(2,1)S(1)}, u32[]{:S(2)}, u32[]{:S(2)}) collective-permute-start(bf16[256,128]{1,0:T(8,128)(2,1)S(1)} %get-tuple-element.341), channel_id=1, source_target_pairs={{0,2},{2,0},{4,6},{6,4},{1,3},{3,1},{5,7},{7,5},{8,10},{10,8},{12,... | collective-permute-start | bytes 196616 | tf_op jit(solution)/shard_map/ppermute | solution.py:907
  131.9 23.9 %collective-permute-start.25 = (bf16[4,96,768]{2,1,0:T(8,128)(2,1)S(1)}, bf16[4,96,768]{2,1,0:T(8,128)(2,1)S(1)}, u32[]{:S(2)}, u32[]{:S(2)}) collective-permute-start(bf16[4,96,768]{2,1,0:T(8,128)(2,1)S(1)} %add_convert_fusion.13), channel_id=1, source_target_pairs={{0,2},{2,0},{4,6},{6,4},{8,10},{10,8},{12,14},{14,12},{16,18},{18,... | collective-permute-start | bytes 1769480 | tf_op jit(solution)/shard_map/ppermute | solution.py:771
  155.5 9.4 %collective-permute-start.28 = (bf16[4,96,768]{2,1,0:T(8,128)(2,1)S(1)}, bf16[4,96,768]{2,1,0:T(8,128)(2,1)S(1)}, u32[]{:S(2)}, u32[]{:S(2)}) collective-permute-start(bf16[4,96,768]{2,1,0:T(8,128)(2,1)S(1)} %get-tuple-element.208), channel_id=1, source_target_pairs={{0,1},{1,0},{2,3},{3,2},{4,5},{5,4},{6,7},{7,6},{8,9},{9,8},{10,11... | collective-permute-start | bytes 1769480 | tf_op jit(solution)/shard_map/ppermute | solution.py:766
  156.0 7.4 %collective-permute-start.26 = (f32[4,16,768]{2,1,0:T(8,128)S(1)}, f32[4,16,768]{2,1,0:T(8,128)S(1)}, u32[]{:S(2)}, u32[]{:S(2)}) collective-permute-start(f32[4,16,768]{2,1,0:T(8,128)S(1)} %get-tuple-element.345), channel_id=1, source_target_pairs={{0,4},{2,6},{4,0},{6,2},{1,5},{3,7},{5,1},{7,3},{8,12},{10,14},{12... | collective-permute-start | bytes 589832 | tf_op jit(solution)/shard_map/ppermute | solution.py:907
  157.8 8.6 %collective-permute-start.35 = (bf16[4,96,768]{2,1,0:T(8,128)(2,1)S(1)}, bf16[4,96,768]{2,1,0:T(8,128)(2,1)S(1)}, u32[]{:S(2)}, u32[]{:S(2)}) collective-permute-start(bf16[4,96,768]{2,1,0:T(8,128)(2,1)S(1)} %get-tuple-element.229), channel_id=1, source_target_pairs={{0,1},{1,0},{2,3},{3,2},{4,5},{5,4},{6,7},{7,6},{8,9},{9,8},{10,11... | collective-permute-start | bytes 1769480 | tf_op jit(solution)/shard_map/ppermute | solution.py:766
  163.3 16.8 %collective-permute-start.37 = (bf16[2,96,768]{2,1,0:T(8,128)(2,1)S(1)}, bf16[2,96,768]{2,1,0:T(8,128)(2,1)S(1)}, u32[]{:S(2)}, u32[]{:S(2)}) collective-permute-start(bf16[2,96,768]{2,1,0:T(8,128)(2,1)S(1)} %get-tuple-element.317), channel_id=1, source_target_pairs={{0,4},{2,6},{4,0},{6,2},{8,12},{10,14},{12,8},{14,10},{16,20},{18,... | collective-permute-start | bytes 884744 | tf_op jit(solution)/shard_map/ppermute | solution.py:771
  164.9 21.9 %collective-permute-start.34 = (bf16[2,192,768]{2,1,0:T(8,128)(2,1)S(1)}, bf16[2,192,768]{2,1,0:T(8,128)(2,1)S(1)}, u32[]{:S(2)}, u32[]{:S(2)}) collective-permute-start(bf16[2,192,768]{2,1,0:T(8,128)(2,1)S(1)} %get-tuple-element.313), channel_id=1, source_target_pairs={{0,2},{2,0},{4,6},{6,4},{8,10},{10,8},{12,14},{14,12},{16,18},{18,... | collective-permute-start | bytes 1769480 | tf_op jit(solution)/shard_map/ppermute | solution.py:771
  166.4 19.4 %collective-permute-start.36 = (bf16[4,96,768]{2,1,0:T(8,128)(2,1)S(1)}, bf16[4,96,768]{2,1,0:T(8,128)(2,1)S(1)}, u32[]{:S(2)}, u32[]{:S(2)}) collective-permute-start(bf16[4,96,768]{2,1,0:T(8,128)(2,1)S(1)} %add_convert_fusion.10), channel_id=1, source_target_pairs={{0,4},{2,6},{4,0},{6,2},{8,12},{10,14},{12,8},{14,10},{16,20},{18,... | collective-permute-start | bytes 1769480 | tf_op jit(solution)/shard_map/ppermute | solution.py:771
  167.8 31.0 %collective-permute-start.33 = (bf16[1024,768]{1,0:T(8,128)(2,1)S(1)}, bf16[1024,768]{1,0:T(8,128)(2,1)S(1)}, u32[]{:S(2)}, u32[]{:S(2)}) collective-permute-start(bf16[1024,768]{1,0:T(8,128)(2,1)S(1)} %get-tuple-element.226), channel_id=1, source_target_pairs={{0,1},{1,0},{2,3},{3,2},{4,5},{5,4},{6,7},{7,6},{8,9},{9,8},{10,11... | collective-permute-start | bytes 4718600 | tf_op jit(solution)/shard_map/ppermute | solution.py:766
  179.4 18.2 %collective-permute-start.44 = (bf16[2,48,3072]{2,1,0:T(8,128)(2,1)S(1)}, bf16[2,48,3072]{2,1,0:T(8,128)(2,1)S(1)}, u32[]{:S(2)}, u32[]{:S(2)}) collective-permute-start(bf16[2,48,3072]{2,1,0:T(8,128)(2,1)S(1)} %get-tuple-element.311), channel_id=1, source_target_pairs={{0,4},{2,6},{4,0},{6,2},{8,12},{10,14},{12,8},{14,10},{16,20},{18,... | collective-permute-start | bytes 1769480 | tf_op jit(solution)/shard_map/ppermute | solution.py:771
  180.2 22.2 %collective-permute-start.43 = (bf16[1,96,768]{2,1,0:T(8,128)(2,1)S(1)}, bf16[1,96,768]{2,1,0:T(8,128)(2,1)S(1)}, u32[]{:S(2)}, u32[]{:S(2)}) collective-permute-start(bf16[1,96,768]{2,1,0:T(8,128)(2,1)S(1)} %add_convert_fusion.40), channel_id=1, source_target_pairs={{0,8},{2,10},{4,12},{6,14},{8,0},{10,2},{12,4},{14,6},{16,24},{18,... | collective-permute-start | bytes 442376 | tf_op jit(solution)/shard_map/ppermute | solution.py:771
  185.8 14.6 %collective-permute-start.31 = (bf16[1,128,768]{2,1,0:T(8,128)(2,1)S(1)}, bf16[1,128,768]{2,1,0:T(8,128)(2,1)S(1)}, u32[]{:S(2)}, u32[]{:S(2)}) collective-permute-start(bf16[1,128,768]{2,1,0:T(8,128)(2,1)S(1)} %get-tuple-element.331), channel_id=1, source_target_pairs={{0,0},{16,1},{2,2},{18,3},{4,4},{20,5},{6,6},{22,7},{8,8},{24,9},{... | collective-permute-start | bytes 589832 | tf_op jit(solution)/shard_map/ppermute | solution.py:897
  186.8 13.6 %collective-permute-start.32 = (bf16[1,128,768]{2,1,0:T(8,128)(2,1)S(1)}, bf16[1,128,768]{2,1,0:T(8,128)(2,1)S(1)}, u32[]{:S(2)}, u32[]{:S(2)}) collective-permute-start(bf16[1,128,768]{2,1,0:T(8,128)(2,1)S(1)} %get-tuple-element.332), channel_id=1, source_target_pairs={{8,0},{24,1},{10,2},{26,3},{12,4},{28,5},{14,6},{30,7},{0,8},{16,9... | collective-permute-start | bytes 589832 | tf_op jit(solution)/shard_map/ppermute | solution.py:897
  197.6 9.9 %collective-permute-start.42 = (bf16[2,96,768]{2,1,0:T(8,128)(2,1)S(1)}, bf16[2,96,768]{2,1,0:T(8,128)(2,1)S(1)}, u32[]{:S(2)}, u32[]{:S(2)}) collective-permute-start(bf16[2,96,768]{2,1,0:T(8,128)(2,1)S(1)} %get-tuple-element.315), channel_id=1, source_target_pairs={{0,2},{2,0},{4,6},{6,4},{8,10},{10,8},{12,14},{14,12},{16,18},{18,... | collective-permute-start | bytes 884744 | tf_op jit(solution)/shard_map/ppermute | solution.py:771
  198.8 10.5 %collective-permute-start.41 = (bf16[1,192,768]{2,1,0:T(8,128)(2,1)S(1)}, bf16[1,192,768]{2,1,0:T(8,128)(2,1)S(1)}, u32[]{:S(2)}, u32[]{:S(2)}) collective-permute-start(bf16[1,192,768]{2,1,0:T(8,128)(2,1)S(1)} %add_convert_fusion.23), channel_id=1, source_target_pairs={{0,4},{2,6},{4,0},{6,2},{8,12},{10,14},{12,8},{14,10},{16,20},{18,... | collective-permute-start | bytes 884744 | tf_op jit(solution)/shard_map/ppermute | solution.py:771
  200.5 22.6 %collective-permute-start.40 = (bf16[512,768]{1,0:T(8,128)(2,1)S(1)}, bf16[512,768]{1,0:T(8,128)(2,1)S(1)}, u32[]{:S(2)}, u32[]{:S(2)}) collective-permute-start(bf16[512,768]{1,0:T(8,128)(2,1)S(1)} %slice.243), channel_id=1, source_target_pairs={{0,4},{2,6},{4,0},{6,2},{1,5},{3,7},{5,1},{7,3},{8,12},{10,14},{12... | collective-permute-start | bytes 2359304 | tf_op jit(solution)/shard_map/ppermute | solution.py:907
  201.5 21.8 %collective-permute-start.49 = (bf16[1,48,3072]{2,1,0:T(8,128)(2,1)S(1)}, bf16[1,48,3072]{2,1,0:T(8,128)(2,1)S(1)}, u32[]{:S(2)}, u32[]{:S(2)}) collective-permute-start(bf16[1,48,3072]{2,1,0:T(8,128)(2,1)S(1)} %add_convert_fusion.20), channel_id=1, source_target_pairs={{0,2},{2,0},{4,6},{6,4},{8,10},{10,8},{12,14},{14,12},{16,18},{18,... | collective-permute-start | bytes 884744 | tf_op jit(solution)/shard_map/ppermute | solution.py:771
  202.5 25.0 %collective-permute-start.48 = (bf16[1,96,768]{2,1,0:T(8,128)(2,1)S(1)}, bf16[1,96,768]{2,1,0:T(8,128)(2,1)S(1)}, u32[]{:S(2)}, u32[]{:S(2)}) collective-permute-start(bf16[1,96,768]{2,1,0:T(8,128)(2,1)S(1)} %add_convert_fusion.38), channel_id=1, source_target_pairs={{0,16},{2,18},{4,20},{6,22},{8,24},{10,26},{12,28},{14,30},{16,0},... | collective-permute-start | bytes 442376 | tf_op jit(solution)/shard_map/ppermute | solution.py:771
  207.6 21.4 %collective-permute-start.47 = (bf16[1,96,768]{2,1,0:T(8,128)(2,1)S(1)}, bf16[1,96,768]{2,1,0:T(8,128)(2,1)S(1)}, u32[]{:S(2)}, u32[]{:S(2)}) collective-permute-start(bf16[1,96,768]{2,1,0:T(8,128)(2,1)S(1)} %add_convert_fusion.37), channel_id=1, source_target_pairs={{0,8},{2,10},{4,12},{6,14},{8,0},{10,2},{12,4},{14,6},{16,24},{18,... | collective-permute-start | bytes 442376 | tf_op jit(solution)/shard_map/ppermute | solution.py:771
  209.4 20.9 %collective-permute-start.46 = (bf16[1,192,768]{2,1,0:T(8,128)(2,1)S(1)}, bf16[1,192,768]{2,1,0:T(8,128)(2,1)S(1)}, u32[]{:S(2)}, u32[]{:S(2)}) collective-permute-start(bf16[1,192,768]{2,1,0:T(8,128)(2,1)S(1)} %add_convert_fusion.19), channel_id=1, source_target_pairs={{0,16},{2,18},{4,20},{6,22},{8,24},{10,26},{12,28},{14,30},{16,0},... | collective-permute-start | bytes 884744 | tf_op jit(solution)/shard_map/ppermute | solution.py:771
  224.2 22.0 %collective-permute-start.53 = (bf16[1,48,3072]{2,1,0:T(8,128)(2,1)}, bf16[1,48,3072]{2,1,0:T(8,128)(2,1)}, u32[]{:S(2)}, u32[]{:S(2)}) collective-permute-start(bf16[1,48,3072]{2,1,0:T(8,128)(2,1)} %add_convert_fusion.17), channel_id=1, source_target_pairs={{0,16},{2,18},{4,20},{6,22},{8,24},{10,26},{12,28},{14,30},{16,0},... | collective-permute-start | bytes 884744 | tf_op jit(solution)/shard_map/ppermute | solution.py:771
  227.5 21.7 %collective-permute-start.52 = (bf16[1,96,768]{2,1,0:T(8,128)(2,1)S(1)}, bf16[1,96,768]{2,1,0:T(8,128)(2,1)S(1)}, u32[]{:S(2)}, u32[]{:S(2)}) collective-permute-start(bf16[1,96,768]{2,1,0:T(8,128)(2,1)S(1)} %add_convert_fusion.35), channel_id=1, source_target_pairs={{0,2},{2,0},{4,6},{6,4},{8,10},{10,8},{12,14},{14,12},{16,18},{18,... | collective-permute-start | bytes 442376 | tf_op jit(solution)/shard_map/ppermute | solution.py:771
  229.0 10.3 %collective-permute-start.45 = (bf16[256,768]{1,0:T(8,128)(2,1)S(1)}, bf16[256,768]{1,0:T(8,128)(2,1)S(1)}, u32[]{:S(2)}, u32[]{:S(2)}) collective-permute-start(bf16[256,768]{1,0:T(8,128)(2,1)S(1)} %slice.301), channel_id=1, source_target_pairs={{0,2},{2,0},{4,6},{6,4},{1,3},{3,1},{5,7},{7,5},{8,10},{10,8},{12,... | collective-permute-start | bytes 1179656 | tf_op jit(solution)/shard_map/ppermute | solution.py:907
  230.4 18.9 %collective-permute-start.51 = (bf16[1,96,768]{2,1,0:T(8,128)(2,1)}, bf16[1,96,768]{2,1,0:T(8,128)(2,1)}, u32[]{:S(2)}, u32[]{:S(2)}) collective-permute-start(bf16[1,96,768]{2,1,0:T(8,128)(2,1)} %add_convert_fusion.34), channel_id=1, source_target_pairs={{0,16},{2,18},{4,20},{6,22},{8,24},{10,26},{12,28},{14,30},{16,0},... | collective-permute-start | bytes 442376 | tf_op jit(solution)/shard_map/ppermute | solution.py:771
  230.5 15.6 %collective-permute-start.54 = (bf16[1,192,768]{2,1,0:T(8,128)(2,1)S(1)}, bf16[1,192,768]{2,1,0:T(8,128)(2,1)S(1)}, u32[]{:S(2)}, u32[]{:S(2)}) collective-permute-start(bf16[1,192,768]{2,1,0:T(8,128)(2,1)S(1)} %add_convert_fusion.16), channel_id=1, source_target_pairs={{0,8},{2,10},{4,12},{6,14},{8,0},{10,2},{12,4},{14,6},{16,24},{18,... | collective-permute-start | bytes 884744 | tf_op jit(solution)/shard_map/ppermute | solution.py:771
  247.3 9.9 %collective-permute-start.57 = (bf16[1,48,3072]{2,1,0:T(8,128)(2,1)S(1)}, bf16[1,48,3072]{2,1,0:T(8,128)(2,1)S(1)}, u32[]{:S(2)}, u32[]{:S(2)}) collective-permute-start(bf16[1,48,3072]{2,1,0:T(8,128)(2,1)S(1)} %add_convert_fusion.15), channel_id=1, source_target_pairs={{0,2},{2,0},{4,6},{6,4},{8,10},{10,8},{12,14},{14,12},{16,18},{18,... | collective-permute-start | bytes 884744 | tf_op jit(solution)/shard_map/ppermute | solution.py:771
  250.3 10.1 %collective-permute-start.56 = (bf16[1,96,768]{2,1,0:T(8,128)(2,1)S(1)}, bf16[1,96,768]{2,1,0:T(8,128)(2,1)S(1)}, u32[]{:S(2)}, u32[]{:S(2)}) collective-permute-start(bf16[1,96,768]{2,1,0:T(8,128)(2,1)S(1)} %add_convert_fusion.33), channel_id=1, source_target_pairs={{0,2},{2,0},{4,6},{6,4},{8,10},{10,8},{12,14},{14,12},{16,18},{18,... | collective-permute-start | bytes 442376 | tf_op jit(solution)/shard_map/ppermute | solution.py:771
  251.0 12.5 %collective-permute-start.55 = (bf16[104,768]{1,0:T(8,128)(2,1)S(1)}, bf16[104,768]{1,0:T(8,128)(2,1)S(1)}, u32[]{:S(2)}, u32[]{:S(2)}) collective-permute-start(bf16[104,768]{1,0:T(8,128)(2,1)S(1)} %add_convert_fusion.32), channel_id=1, source_target_pairs={{0,2},{2,0},{4,6},{6,4},{8,10},{10,8},{12,14},{14,12},{16,18},{18,... | collective-permute-start | bytes 479240 | tf_op jit(solution)/shard_map/ppermute | solution.py:771
  272.2 6.8 %collective-permute-start.61 = (bf16[104,768]{1,0:T(8,128)(2,1)S(1)}, bf16[104,768]{1,0:T(8,128)(2,1)S(1)}, u32[]{:S(2)}, u32[]{:S(2)}) collective-permute-start(bf16[104,768]{1,0:T(8,128)(2,1)S(1)} %add_convert_fusion.30), channel_id=1, source_target_pairs={{0,8},{2,10},{4,12},{6,14},{8,0},{10,2},{12,4},{14,6},{16,24},{18,... | collective-permute-start | bytes 479240 | tf_op jit(solution)/shard_map/ppermute | solution.py:771
  274.2 21.2 %collective-permute-start.66 = (bf16[2,192,768]{2,1,0:T(8,128)(2,1)S(1)}, bf16[2,192,768]{2,1,0:T(8,128)(2,1)S(1)}, u32[]{:S(2)}, u32[]{:S(2)}) collective-permute-start(bf16[2,192,768]{2,1,0:T(8,128)(2,1)S(1)} %pad_maximum_fusion.3), channel_id=1, source_target_pairs={{0,4},{2,6},{4,0},{6,2},{8,12},{10,14},{12,8},{14,10},{16,20},{18,... | collective-permute-start | bytes 1769480 | tf_op jit(solution)/shard_map/ppermute | solution.py:771
  279.0 14.3 %collective-permute-start.62 = (bf16[104,768]{1,0:T(8,128)(2,1)S(1)}, bf16[104,768]{1,0:T(8,128)(2,1)S(1)}, u32[]{:S(2)}, u32[]{:S(2)}) collective-permute-start(bf16[104,768]{1,0:T(8,128)(2,1)S(1)} %add_convert_fusion.29), channel_id=1, source_target_pairs={{0,16},{2,18},{4,20},{6,22},{8,24},{10,26},{12,28},{14,30},{16,0},... | collective-permute-start | bytes 479240 | tf_op jit(solution)/shard_map/ppermute | solution.py:771
  285.4 9.9 %collective-permute-start.67 = (bf16[2,96,768]{2,1,0:T(8,128)(2,1)S(1)}, bf16[2,96,768]{2,1,0:T(8,128)(2,1)S(1)}, u32[]{:S(2)}, u32[]{:S(2)}) collective-permute-start(bf16[2,96,768]{2,1,0:T(8,128)(2,1)S(1)} %pad_maximum_fusion.9), channel_id=1, source_target_pairs={{0,4},{2,6},{4,0},{6,2},{8,12},{10,14},{12,8},{14,10},{16,20},{18,... | collective-permute-start | bytes 884744 | tf_op jit(solution)/shard_map/ppermute | solution.py:771
  285.7 15.9 %collective-permute-start.65 = (bf16[2,96,768]{2,1,0:T(8,128)(2,1)S(1)}, bf16[2,96,768]{2,1,0:T(8,128)(2,1)S(1)}, u32[]{:S(2)}, u32[]{:S(2)}) collective-permute-start(bf16[2,96,768]{2,1,0:T(8,128)(2,1)S(1)} %pad_maximum_fusion.10), channel_id=1, source_target_pairs={{0,4},{2,6},{4,0},{6,2},{8,12},{10,14},{12,8},{14,10},{16,20},{18,... | collective-permute-start | bytes 884744 | tf_op jit(solution)/shard_map/ppermute | solution.py:771
  287.4 17.2 %collective-permute-start.64 = (bf16[2,48,3072]{2,1,0:T(8,128)(2,1)S(1)}, bf16[2,48,3072]{2,1,0:T(8,128)(2,1)S(1)}, u32[]{:S(2)}, u32[]{:S(2)}) collective-permute-start(bf16[2,48,3072]{2,1,0:T(8,128)(2,1)S(1)} %pad_maximum_fusion.4), channel_id=1, source_target_pairs={{0,8},{2,10},{4,12},{6,14},{8,0},{10,2},{12,4},{14,6},{16,24},{18,... | collective-permute-start | bytes 1769480 | tf_op jit(solution)/shard_map/ppermute | solution.py:771
  295.5 27.0 %collective-permute-start.70 = (bf16[4,192,768]{2,1,0:T(8,128)(2,1)S(1)}, bf16[4,192,768]{2,1,0:T(8,128)(2,1)}, u32[]{:S(2)}, u32[]{:S(2)}) collective-permute-start(bf16[4,192,768]{2,1,0:T(8,128)(2,1)S(1)} %pad_maximum_fusion.1.near_ref), channel_id=1, source_target_pairs={{0,2},{2,0},{4,6},{6,4},{8,10},{10,8},{12,14},{14,12},{16,18},{18,... | collective-permute-start | bytes 3538952 | tf_op jit(solution)/shard_map/ppermute | solution.py:771
  296.1 21.2 %collective-permute-start.71 = (bf16[4,96,768]{2,1,0:T(8,128)(2,1)S(1)}, bf16[4,96,768]{2,1,0:T(8,128)(2,1)}, u32[]{:S(2)}, u32[]{:S(2)}) collective-permute-start(bf16[4,96,768]{2,1,0:T(8,128)(2,1)S(1)} %pad_maximum_fusion.5.near_ref), channel_id=1, source_target_pairs={{0,8},{2,10},{4,12},{6,14},{8,0},{10,2},{12,4},{14,6},{16,24},{18,... | collective-permute-start | bytes 1769480 | tf_op jit(solution)/shard_map/ppermute | solution.py:771
  304.7 26.8 %collective-permute-start.68 = (bf16[4,48,3072]{2,1,0:T(8,128)(2,1)S(1)}, bf16[4,48,3072]{2,1,0:T(8,128)(2,1)}, u32[]{:S(2)}, u32[]{:S(2)}) collective-permute-start(bf16[4,48,3072]{2,1,0:T(8,128)(2,1)S(1)} %pad_maximum_fusion.2.near_ref), channel_id=1, source_target_pairs={{0,4},{2,6},{4,0},{6,2},{8,12},{10,14},{12,8},{14,10},{16,20},{18,... | collective-permute-start | bytes 3538952 | tf_op jit(solution)/shard_map/ppermute | solution.py:771
  304.8 23.5 %collective-permute-start.69 = (bf16[4,96,768]{2,1,0:T(8,128)(2,1)S(1)}, bf16[4,96,768]{2,1,0:T(8,128)(2,1)}, u32[]{:S(2)}, u32[]{:S(2)}) collective-permute-start(bf16[4,96,768]{2,1,0:T(8,128)(2,1)S(1)} %pad_maximum_fusion.6.near_ref), channel_id=1, source_target_pairs={{0,8},{2,10},{4,12},{6,14},{8,0},{10,2},{12,4},{14,6},{16,24},{18,... | collective-permute-start | bytes 1769480 | tf_op jit(solution)/shard_map/ppermute | solution.py:771
  322.6 10.4 %collective-permute-start.76 = (bf16[4,192,768]{2,1,0:T(8,128)(2,1)S(1)}, bf16[4,192,768]{2,1,0:T(8,128)(2,1)}, u32[]{:S(2)}, u32[]{:S(2)}) collective-permute-start(bf16[4,192,768]{2,1,0:T(8,128)(2,1)S(1)} %pad_maximum_fusion.1.near_ref), channel_id=1, source_target_pairs={{0,1},{1,0},{2,3},{3,2},{4,5},{5,4},{6,7},{7,6},{8,9},{9,8},{10,11... | collective-permute-start | bytes 3538952 | tf_op jit(solution)/shard_map/ppermute | solution.py:766
  324.7 6.8 %collective-permute-start.78 = (bf16[4,96,768]{2,1,0:T(8,128)(2,1)S(1)}, bf16[4,96,768]{2,1,0:T(8,128)(2,1)S(1)}, u32[]{:S(2)}, u32[]{:S(2)}) collective-permute-start(bf16[4,96,768]{2,1,0:T(8,128)(2,1)S(1)} %pad_maximum_fusion.5.near_ref), channel_id=1, source_target_pairs={{0,1},{1,0},{2,3},{3,2},{4,5},{5,4},{6,7},{7,6},{8,9},{9,8},{10,11... | collective-permute-start | bytes 1769480 | tf_op jit(solution)/shard_map/ppermute | solution.py:766
  324.7 10.1 %collective-permute-start.77 = (bf16[4,192,768]{2,1,0:T(8,128)(2,1)}, bf16[4,192,768]{2,1,0:T(8,128)(2,1)}, u32[]{:S(2)}, u32[]{:S(2)}) collective-permute-start(bf16[4,192,768]{2,1,0:T(8,128)(2,1)} %collective-permute-done.70.far_ref), channel_id=1, source_target_pairs={{0,1},{1,0},{2,3},{3,2},{4,5},{5,4},{6,7},{7,6},{8,9},{9,8},{10,11... | collective-permute-start | bytes 3538952 | tf_op jit(solution)/shard_map/ppermute | solution.py:766
  331.5 18.7 %collective-permute-start.72 = (bf16[4,48,3072]{2,1,0:T(8,128)(2,1)S(1)}, bf16[4,48,3072]{2,1,0:T(8,128)(2,1)}, u32[]{:S(2)}, u32[]{:S(2)}) collective-permute-start(bf16[4,48,3072]{2,1,0:T(8,128)(2,1)S(1)} %pad_maximum_fusion.2.near_ref), channel_id=1, source_target_pairs={{0,1},{1,0},{2,3},{3,2},{4,5},{5,4},{6,7},{7,6},{8,9},{9,8},{10,11... | collective-permute-start | bytes 3538952 | tf_op jit(solution)/shard_map/ppermute | solution.py:766
  332.3 17.9 %collective-permute-start.73 = (bf16[4,48,3072]{2,1,0:T(8,128)(2,1)}, bf16[4,48,3072]{2,1,0:T(8,128)(2,1)}, u32[]{:S(2)}, u32[]{:S(2)}) collective-permute-start(bf16[4,48,3072]{2,1,0:T(8,128)(2,1)} %collective-permute-done.68.far_ref), channel_id=1, source_target_pairs={{0,1},{1,0},{2,3},{3,2},{4,5},{5,4},{6,7},{7,6},{8,9},{9,8},{10,11... | collective-permute-start | bytes 3538952 | tf_op jit(solution)/shard_map/ppermute | solution.py:766
  332.8 13.6 %collective-permute-start.75 = (bf16[4,96,768]{2,1,0:T(8,128)(2,1)}, bf16[4,96,768]{2,1,0:T(8,128)(2,1)S(1)}, u32[]{:S(2)}, u32[]{:S(2)}) collective-permute-start(bf16[4,96,768]{2,1,0:T(8,128)(2,1)} %collective-permute-done.69.far_ref), channel_id=1, source_target_pairs={{0,1},{1,0},{2,3},{3,2},{4,5},{5,4},{6,7},{7,6},{8,9},{9,8},{10,11... | collective-permute-start | bytes 1769480 | tf_op jit(solution)/shard_map/ppermute | solution.py:766
  332.9 13.5 %collective-permute-start.74 = (bf16[4,96,768]{2,1,0:T(8,128)(2,1)S(1)}, bf16[4,96,768]{2,1,0:T(8,128)(2,1)S(1)}, u32[]{:S(2)}, u32[]{:S(2)}) collective-permute-start(bf16[4,96,768]{2,1,0:T(8,128)(2,1)S(1)} %pad_maximum_fusion.6.near_ref), channel_id=1, source_target_pairs={{0,1},{1,0},{2,3},{3,2},{4,5},{5,4},{6,7},{7,6},{8,9},{9,8},{10,11... | collective-permute-start | bytes 1769480 | tf_op jit(solution)/shard_map/ppermute | solution.py:766
  334.8 21.5 %collective-permute-start.63 = (bf16[104,768]{1,0:T(8,128)(2,1)S(1)}, bf16[104,768]{1,0:T(8,128)(2,1)S(1)}, u32[]{:S(2)}, u32[]{:S(2)}) collective-permute-start(bf16[104,768]{1,0:T(8,128)(2,1)S(1)} %copy-done.76), channel_id=1, source_target_pairs={{0,1},{1,0},{2,3},{3,2},{4,5},{5,4},{6,7},{7,6},{8,9},{9,8},{10,11... | collective-permute-start | bytes 479240 | tf_op jit(solution)/shard_map/ppermute | solution.py:766
  (112 other events, 1148.4 us)
where the time goes:
time: 362 us; the launch traced here: 359 us
  waiting for transfers between devices  116 us (32%)
  Pallas kernels  109 us (30%)
  starting transfers between devices  79.1 us (22%)
  local copies, waits for them, and re-layouts  28.7 us (8%)
  other arithmetic  21.8 us (6%)
    ppermute x32, waiting for transfers between devices, across(): lax.ppermute(part, ('g', 's'), [(i, i ^ 1 << bit) for i in range(chips)])  78.4 us
    ppermute x32, starting transfers between devices, across(): lax.ppermute(part, ('g', 's'), [(i, i ^ 1 << bit) for i in range(chips)])  44.6 us
    ppermute x15, waiting for transfers between devices, nearby(): return lax.ppermute(part, 's', [(i, i ^ k) for i in range(around)])  30.8 us
    pallas_call x8, Pallas kernels, grad_half(): pl.pallas_call(functools.partial(half_kernel, halved), out_shape=(jax.Sha...  26.5 us
    unnamed x206, local copies, waits for them, and re-layouts  21 us
    pallas_call x4, Pallas kernels, put_in_place(): pl.pallas_call(functools.partial(place_kernel, halved, lead, step), grid=...  19.6 us
    ppermute x15, starting transfers between devices, nearby(): return lax.ppermute(part, 's', [(i, i ^ k) for i in range(around)])  15.4 us
    ppermute x24, starting transfers between devices, swapped(): return lax.ppermute(part, 'core', CORES)  11 us
  transfers between devices with their start and end apart: 80, of which 26 were waited for; matrix products, arithmetic and copies ran while one was open for 8% of the time, Pallas kernels for 22%

commit v1 on v0

--- a/solution.py
+++ b/solution.py
@@ -47,6 +47,10 @@
 
 
 SMEM = functools.partial(pl.BlockSpec, memory_space=pltpu.SMEM)
+
+
+def in_hbm(value):
+    return pltpu.with_memory_space_constraint(value, pltpu.HBM)
 
 
 def whole(*shape):
@@ -275,9 +279,9 @@
         values_kernel,
         grid=(segs // 2,),
         out_shape=(
-            jax.ShapeDtypeStruct((count, width), BF16),
+            pltpu.HBM((count, width), BF16),
             jax.ShapeDtypeStruct((count, wide), BF16),
-            jax.ShapeDtypeStruct((count, wide), BF16),
+            pltpu.HBM((count, wide), BF16),
         ),
         in_specs=[pl.BlockSpec((2, length, width), lambda b: (b, 0, 0)), whole(1, width), whole(width, wide)],
         out_specs=(
@@ -339,7 +343,7 @@
         compiler_params=pltpu.CompilerParams(vmem_limit_bytes=16 * MIB),
         cost_estimate=BRIEF,
         name="values_back",
-    )(probs, d_attended, slope, w_value)
+    )(in_hbm(probs), d_attended, in_hbm(slope), w_value)
 
 
 def attend_kernel(
@@ -394,8 +398,8 @@
         functools.partial(attend_kernel, scale),
         grid=(wide // chunk,),
         out_shape=(
-            jax.ShapeDtypeStruct((count, every), F32),
-            jax.ShapeDtypeStruct((count, every), BF16),
+            pltpu.HBM((count, every), F32),
+            pltpu.HBM((count, every), BF16),
             jax.ShapeDtypeStruct((count, 1), F32),
             jax.ShapeDtypeStruct((count, wide), F32),
             jax.ShapeDtypeStruct((count, wide), BF16),
@@ -556,7 +560,7 @@
         compiler_params=pltpu.CompilerParams(vmem_limit_bytes=10 * MIB),
         cost_estimate=BRIEF,
         name="scores_back",
-    )(weight, inverse, delta, d_attended, values, queries, keys)
+    )(in_hbm(weight), inverse, delta, d_attended, in_hbm(values), queries, keys)
 
 
 def third_kernel(
@@ -692,63 +696,55 @@
     )(half, slots, *pairs)
 
 
-def place_kernel(halved, lead, step, core_ref, slot_ref, near_ref, far_ref, near_other_ref, far_other_ref, *out_refs):
-    half, _, wide = near_ref.shape
+def place_kernel(halved, lead, core_ref, place_ref, own_ref, other_ref, *refs):
+    wide = own_ref.shape[2]
     core = core_ref[0]
-    for b in range(step):
-        slot = slot_ref[pl.program_id(0) * step + b]
-
-        def put(own, other):
-            at = 0
-            for kind, out_ref in zip(halved, out_refs, strict=True):
-                if kind == "right":
-                    rows = out_ref.shape[1]
-                    mine = pl.ds(pl.multiple_of(core * wide, 128), wide)
-                    others = pl.ds(pl.multiple_of((1 - core) * wide, 128), wide)
-                    out_ref[b, :, mine] = own[at : at + rows].astype(F32)
-                    out_ref[b, :, others] = other[at : at + rows].astype(F32)
-                else:
-                    rows = out_ref.shape[2]
-                    if lead:
-                        out_ref[:, b, :, :lead] = jnp.zeros((2, rows, lead), F32)
-                    out_ref[core, b, :, lead:] = own[at : at + rows].astype(F32)
-                    out_ref[1 - core, b, :, lead:] = other[at : at + rows].astype(F32)
-                at += rows
-
-        @pl.when(slot < half)
-        def _():
-            put(near_ref[slot], near_other_ref[slot])
-
-        @pl.when(slot >= half)
-        def _():
-            put(far_ref[slot - half], far_other_ref[slot - half])
-
-
-def put_in_place(core, slots, halved, talls, lead, near, far, near_other, far_other):
-    half, rows, wide = near.shape
+    own, other = own_ref[0].astype(F32), other_ref[0].astype(F32)
+    at = 0
+    for kind, out_ref in zip(halved, refs[-len(halved) :], strict=True):
+        if kind == "right":
+            rows = out_ref.shape[1]
+            mine = pl.ds(pl.multiple_of(core * wide, 128), wide)
+            others = pl.ds(pl.multiple_of((1 - core) * wide, 128), wide)
+            out_ref[0, :, mine] = own[at : at + rows]
+            out_ref[0, :, others] = other[at : at + rows]
+        else:
+            rows = out_ref.shape[2]
+            if lead:
+                out_ref[:, 0, :, :lead] = jnp.zeros((2, rows, lead), F32)
+            out_ref[core, 0, :, lead:] = own[at : at + rows]
+            out_ref[1 - core, 0, :, lead:] = other[at : at + rows]
+        at += rows
+
+
+def put_in_place(core, places, halved, talls, lead, own, other, before=()):
+    half, rows, wide = own.shape
     blocks = 2 * half
-    step = 2
     shapes, specs = [], []
     for kind, tall in zip(halved, talls, strict=True):
-        if kind != "left":
+        if kind == "right":
             each = tall // blocks
             shapes.append(jax.ShapeDtypeStruct((blocks, each, 2 * wide), F32))
-            specs.append(pl.BlockSpec((step, each, 2 * wide), lambda b: (b, 0, 0)))
+            specs.append(pl.BlockSpec((1, each, 2 * wide), lambda i, core, places: (places[i], 0, 0)))
         else:
             each = tall // 2 // blocks
             shapes.append(jax.ShapeDtypeStruct((2, blocks, each, lead + wide), F32))
-            specs.append(pl.BlockSpec((2, step, each, lead + wide), lambda b: (0, b, 0, 0)))
-    outs = pl.pallas_call(
-        functools.partial(place_kernel, halved, lead, step),
-        grid=(blocks // step,),
+            specs.append(pl.BlockSpec((2, 1, each, lead + wide), lambda i, core, places: (0, places[i], 0, 0)))
+    block = pl.BlockSpec((1, rows, wide), lambda i, core, places: (i, 0, 0))
+    return pl.pallas_call(
+        functools.partial(place_kernel, halved, lead),
         out_shape=shapes,
-        in_specs=[SMEM()] * 2 + [whole(half, rows, wide)] * 4,
-        out_specs=specs,
+        grid_spec=pltpu.PrefetchScalarGridSpec(
+            num_scalar_prefetch=2,
+            grid=(half,),
+            in_specs=[block, block] + [pl.BlockSpec(memory_space=pl.ANY)] * len(before),
+            out_specs=specs,
+        ),
+        input_output_aliases={4 + i: i for i in range(len(before))},
         compiler_params=pltpu.CompilerParams(vmem_limit_bytes=20 * MIB),
         cost_estimate=BRIEF,
         name="put_in_place",
-    )(core, slots, near, far, near_other, far_other)
-    return [out.reshape(tall, -1) for out, tall in zip(outs, talls, strict=True)]
+    )(core, places, own, other, *before)
 
 
 def after(value, *others):
@@ -830,16 +826,27 @@
         self.turn += 1
         return self.sent
 
+    def end_near(self, last, lead=0):
+        self.lead = lead
+        other = after(swapped(self.sent), last)
+        half = self.sent.shape[0]
+        slot = jnp.arange(2 * half, dtype=jnp.int32)
+        self.places = jnp.sum(jnp.where(self.back_slots[None] == slot[:, None], slot[None], 0), axis=1, dtype=jnp.int32)
+        self.outs = put_in_place(self.core, self.places[:half], self.halved, self.talls, lead, self.sent, other)
+        return self.outs[0]
+
     def arrive(self, *others):
         self.received = after(self.received, *others)
-        self.others = swapped(after(self.sent, self.received)), swapped(self.received)
+        self.other = swapped(self.received)
         return self.received
 
-    def end(self, last, lead=0):
-        return put_in_place(
-            self.core, self.back_slots, self.halved, self.talls, lead,
-            self.sent, self.received, *after(self.others, last),
+    def end(self, last):
+        half = self.sent.shape[0]
+        outs = put_in_place(
+            self.core, self.places[half:], self.halved, self.talls, self.lead,
+            self.received, after(self.other, last), self.outs,
         )
+        return [out.reshape(tall, -1) for out, tall in zip(outs, self.talls, strict=True)]
 
 
 def local(
@@ -1114,9 +1121,11 @@
     last = all_step(last, *order_of_end)
     ended = {}
     for lane in order_of_end:
+        last = lane.end_near(last, zdim if lane is three else 0)
+    for lane in order_of_end:
         last = lane.arrive(last)
     for lane in order_of_end:
-        ended[lane] = lane.end(last, zdim if lane is three else 0)
+        ended[lane] = lane.end(last)
         last = ended[lane][0]
     small_near = after(small_near, last)
     small = jnp.where(core == 0, jnp.concatenate([small, small_near]), jnp.concatenate([small_near, small]))

time: 362 us -> 352 us (0.972)
  waiting for transfers between devices: 116 us -> 95.5 us
  Pallas kernels: 109 us -> 123 us
  local copies, waits for them, and re-layouts: 28.7 us -> 15.6 us
  starting transfers between devices: 79.1 us -> 86.2 us
    ppermute x32, waiting for transfers between devices: 78.4 us -> 62.5 us  [across(): lax.ppermute(part, ('g', 's'), [(i, i ^ 1 << bit) for i in range(chips)])]
    unnamed x206 -> x182, local copies, waits for them, and re-layouts: 21 us -> 7.64 us
    pallas_call x5 -> x9, Pallas kernels: 29.8 us -> 38.7 us  [the longest x8 27.7 us: put_in_place(): pl.pallas_call(functools.partial(place_kernel, halved, lead), out_shape=s...]
  transfers between devices with their start and end apart: 80 -> 80, of which waited for: 26 -> 26; matrix products, arithmetic and copies ran while one was open for 8% -> 8% of each run, Pallas kernels for 22% -> 26%
where the time goes in v1:
time: 352 us; the launch traced here: 348 us
  Pallas kernels  123 us (35%)
  waiting for transfers between devices  95.5 us (27%)
  starting transfers between devices  86.2 us (24%)
  other arithmetic  23.2 us (7%)
  local copies, waits for them, and re-layouts  15.6 us (4%)
    ppermute x32, waiting for transfers between devices, across(): lax.ppermute(part, ('g', 's'), [(i, i ^ 1 << bit) for i in range(chips)])  62.5 us
    ppermute x32, starting transfers between devices, across(): lax.ppermute(part, ('g', 's'), [(i, i ^ 1 << bit) for i in range(chips)])  47.3 us
    ppermute x15, waiting for transfers between devices, nearby(): return lax.ppermute(part, 's', [(i, i ^ k) for i in range(around)])  29.9 us
    pallas_call x8, Pallas kernels, put_in_place(): pl.pallas_call(functools.partial(place_kernel, halved, lead), out_shape=s...  27.7 us
    pallas_call x8, Pallas kernels, grad_half(): pl.pallas_call(functools.partial(half_kernel, halved), out_shape=(jax.Sha...  26.6 us
    ppermute x15, starting transfers between devices, nearby(): return lax.ppermute(part, 's', [(i, i ^ k) for i in range(around)])  17.8 us
    pallas_call x1, Pallas kernels, values_back(): pl.pallas_call(values_back_kernel, grid=(every // rows,), out_shape=(jax....  11.5 us
    pallas_call x1, Pallas kernels, row_values(): pl.pallas_call(values_kernel, grid=(segs // 2,), out_shape=(pltpu.HBM((co...  11 us
  transfers between devices with their start and end apart: 80, of which 26 were waited for; matrix products, arithmetic and copies ran while one was open for 8% of the time, Pallas kernels for 26%

profile of v1, /device:TPU:0, one launch (start us, length us, event | category | flops | bytes accessed | tf_op | source)
XLA Modules:
  0.0 348.2 jit_solution(4199862860822949346)
XLA Ops:
  2.4 3.1 collective-permute-start.2
  5.5 3.4 collective-permute-start
  12.2 1.5 multiply_multiply_fusion
  15.0 2.7 ema_first.1
  17.7 1.6 collective-permute-start.3
  21.2 1.6 collective-permute-done.3
  22.9 2.4 collective-permute-done.4
  27.3 1.6 collective-permute-start.16
  33.3 5.1 %ema_second.1 = (f32[2,128,768]{2,1,0:T(8,128)S(1)}, bf16[2,128,768]{2,1,0:T(8,128)(2,1)S(1)}, f32[2,16,768]{2,1,0:T(8,128)S(1)}) custom-call(s32[2]{0:T(128)S(1)} %get-tuple-element.305.place_ref, s32[16]{0:T(128)S(1)} %fusion.18.slot_ref, f32[16]{0:T(128)S(1)} %get-tuple-element.296.pass_ref, f32[2,128]{1,0:T(2,128)S(1)} %subtract_bitcast_fusion.1.keep_ref, ...), custom_call_target="tpu_custom_call" | custom-call | flops 1 | bytes 1 | tf_op jit(solution)/shard_map/ema_second/pallas_call | solution.py:145
  42.4 5.5 %collective-permute-done.13 = bf16[2,128,768]{2,1,0:T(8,128)(2,1)S(1)} collective-permute-done((bf16[2,128,768]{2,1,0:T(8,128)(2,1)S(1)}, bf16[2,128,768]{2,1,0:T(8,128)(2,1)S(1)}, u32[]{:S(2)}, u32[]{:S(2)}) %collective-permute-start.13) | collective-permute-done | bytes 393248 | tf_op jit(solution)/shard_map/ppermute | solution.py:914
  48.1 4.6 %collective-permute-start.14 = (bf16[8,128,768]{2,1,0:T(8,128)(2,1)S(1)}, bf16[8,128,768]{2,1,0:T(8,128)(2,1)S(1)}, u32[]{:S(2)}, u32[]{:S(2)}) collective-permute-start(bf16[8,128,768]{2,1,0:T(8,128)(2,1)S(1)} %pad_maximum_fusion), channel_id=1, source_target_pairs={{0,1},{1,0},{2,3},{3,2},{4,5},{5,4},{6,7},{7,6},{8,9},{9,8},{10,11... | collective-permute-start | bytes 4718600 | tf_op jit(solution)/shard_map/ppermute | solution.py:762
  56.4 1.7 copy-done.3
  58.1 11.0 %row_values.1 = (bf16[2048,768]{1,0:T(8,128)(2,1)}, bf16[2048,1536]{1,0:T(8,128)(2,1)S(1)}, bf16[2048,1536]{1,0:T(8,128)(2,1)}) custom-call(bf16[16,128,768]{2,1,0:T(8,128)(2,1)S(1)} %constant_dynamic-update-slice_fusion.16.x_ref, f32[1,768]{1,0:T(1,128)S(1)} %broadcast_in_dim.48.gain_ref, bf16[768,1536]{1,0:T(8,128)(2,1)S(1)} %copy-done.3), custom_call_target="tpu_custom_call" | custom-call | flops 1 | bytes 1 | tf_op jit(solution)/shard_map/row_values/pallas_call | solution.py:278
  69.2 7.2 %attend.1 = (f32[256,2048]{1,0:T(8,128)}, bf16[256,2048]{1,0:T(8,128)(2,1)}, f32[256,1]{1,0:T(8,128)S(1)}, f32[256,1536]{1,0:T(8,128)S(1)}, bf16[256,1536]{1,0:T(8,128)(2,1)S(1)}) custom-call(s32[256,1]{1,0:T(8,128)S(1)} %copy.44.at_ref, s32[256,1]{1,0:T(8,128)S(1)} %copy.45.doc_ref, s32[1,2048]{1,0:T(1,128)S(1)} %bitcast.99, s32[1,2048]{1,0:T(1,128)S(1)} %bitcast.100, ...), custom_call_target="tpu_custom_call" | custom-call | flops 1 | bytes 1 | tf_op jit(solution)/shard_map/attend/pallas_call | solution.py:397
  76.4 5.9 %middle.1 = (bf16[256,768]{1,0:T(8,128)(2,1)S(1)}, bf16[256,768]{1,0:T(8,128)(2,1)S(1)}, bf16[256,1536]{1,0:T(8,128)(2,1)S(1)}, bf16[256,1536]{1,0:T(8,128)(2,1)...) custom-call(bf16[256,1536]{1,0:T(8,128)(2,1)S(1)} %get-tuple-element, ...), custom_call_target="tpu_custom_call" | custom-call | flops 1 | bytes 1 | tf_op jit(solution)/shard_map/middle/pallas_call | solution.py:497
  84.7 3.7 %grad_half.8 = (bf16[4,192,768]{2,1,0:T(8,128)(2,1)S(1)}, bf16[4,192,768]{2,1,0:T(8,128)(2,1)}) custom-call(s32[1]{0:T(128)S(6)} %sub.95.half_ref, s32[8]{0:T(128)S(1)} %copy-done.58, bf16[256,1536]{1,0:T(8,128)(2,1)S(1)} %get-tuple-element.160.gated_ref.refs_0_, bf16[256,768]{1,0:T(8,128)(2,1)S(1)} %slice.241.refs_1_, ...), custom_call_target="tpu_custom_call" | custom-call | flops 1 | bytes 1 | tf_op jit(solution)/shard_map/grad_half/pallas_call | solution.py:688
  91.7 4.0 %grad_half.9 = (bf16[4,48,3072]{2,1,0:T(8,128)(2,1)S(1)}, bf16[4,48,3072]{2,1,0:T(8,128)(2,1)S(1)}) custom-call(s32[1]{0:T(128)S(6)} %sub.95.half_ref, s32[8]{0:T(128)S(1)} %copy-done.55, bf16[256,768]{1,0:T(8,128)(2,1)S(1)} %bitcast.93, bf16[256,3072]{1,0:T(8,128)(2,1)S(1)} %get-tuple-element.167.refs_1_.d_tail_ref), custom_call_target="tpu_custom_call" | custom-call | flops 1 | bytes 1 | tf_op jit(solution)/shard_map/grad_half/pallas_call | solution.py:688
  96.5 9.8 %scores_back.1 = (bf16[1024,128]{1,0:T(8,128)(2,1)S(1)}, bf16[1024,128]{1,0:T(8,128)(2,1)S(1)}, f32[256,128]{1,0:T(8,128)S(1)}) custom-call(f32[256,2048]{1,0:T(8,128)} %get-tuple-element.164.weight_ref, f32[256,1]{1,0:T(8,128)S(1)} %copy-done.44, f32[256,1]{1,0:T(8,128)S(1)} %copy-done.46, bf16[256,1536]{1,0:T(8,128)(2,1)S(1)} %copy-done.10, ...), custom_call_target="tpu_custom_call" | custom-call | flops 1 | bytes 1 | tf_op jit(solution)/shard_map/scores_back/pallas_call | solution.py:543
  106.4 2.7 grad_half.10
  110.5 1.6 add_convert_fusion.4
  113.0 3.7 %grad_half.11 = (bf16[4,48,3072]{2,1,0:T(8,128)(2,1)S(1)}, bf16[4,48,3072]{2,1,0:T(8,128)(2,1)S(1)}) custom-call(s32[1]{0:T(128)} %bitcast.30.half_ref.core_ref, s32[8]{0:T(128)S(1)} %copy-done.56, bf16[256,768]{1,0:T(8,128)(2,1)S(1)} %bitcast.94, bf16[256,3072]{1,0:T(8,128)(2,1)S(1)} %get-tuple-element.167.refs_1_.d_tail_ref), custom_call_target="tpu_custom_call" | custom-call | flops 1 | bytes 1 | tf_op jit(solution)/shard_map/grad_half/pallas_call | solution.py:688
  119.4 1.6 grad_half.12
  122.1 1.6 collective-permute-done.19
  123.7 2.0 grad_half.13
  129.7 11.5 %values_back.1 = (bf16[2048,1536]{1,0:T(8,128)(2,1)S(1)}, bf16[1024,768]{1,0:T(8,128)(2,1)S(1)}, bf16[1024,768]{1,0:T(8,128)(2,1)S(1)}) custom-call(bf16[256,2048]{1,0:T(8,128)(2,1)} %get-tuple-element.194.probs_ref, bf16[256,1536]{1,0:T(8,128)(2,1)S(1)} %copy-done.10, bf16[2048,1536]{1,0:T(8,128)(2,1)} %get-tuple-element.195.slope_ref, ...), custom_call_target="tpu_custom_call" | custom-call | flops 1 | bytes 1 | tf_op jit(solution)/shard_map/values_back/pallas_call | solution.py:324
  141.4 4.9 %ema_third.1 = (bf16[256,128]{1,0:T(8,128)(2,1)}, bf16[128,768]{1,0:T(8,128)(2,1)S(1)}, f32[2,128,768]{2,1,0:T(8,128)S(1)}, f32[2,16,768]{2,1,0:T(8,128)S(1)}, f...) custom-call(f32[2,128]{1,0:T(2,128)S(1)} %subtract_bitcast_fusion.next_ref, f32[256,128]{1,0:T(8,128)S(1)} %get-tuple-element.175.dq_ref, ...), custom_call_target="tpu_custom_call" | custom-call | flops 1 | bytes 1 | tf_op jit(solution)/shard_map/ema_third/pallas_call | solution.py:622
  147.5 4.4 %grad_half.14 = (bf16[4,96,768]{2,1,0:T(8,128)(2,1)S(1)}, bf16[4,96,768]{2,1,0:T(8,128)(2,1)S(1)}) custom-call(s32[1]{0:T(128)S(6)} %sub.95.half_ref, s32[8]{0:T(128)S(1)} %iota_xor_fusion.slot_ref, bf16[2048,768]{1,0:T(8,128)(2,1)S(1)} %copy-done.1, bf16[2048,1536]{1,0:T(8,128)(2,1)S(1)} %get-tuple-element.209.refs_1_), custom_call_target="tpu_custom_call" | custom-call | flops 1 | bytes 1 | tf_op jit(solution)/shard_map/grad_half/pallas_call | solution.py:688
  153.0 1.8 collective-permute-start.26
  156.0 4.4 %grad_half.15 = (bf16[4,96,768]{2,1,0:T(8,128)(2,1)S(1)}, bf16[4,96,768]{2,1,0:T(8,128)(2,1)S(1)}) custom-call(s32[1]{0:T(128)} %bitcast.30.half_ref.core_ref, s32[8]{0:T(128)S(1)} %iota_xor_fusion.slot_ref, bf16[2048,768]{1,0:T(8,128)(2,1)S(1)} %copy-done.1, bf16[2048,1536]{1,0:T(8,128)(2,1)S(1)} %get-tuple-element.209.refs_1_), custom_call_target="tpu_custom_call" | custom-call | flops 1 | bytes 1 | tf_op jit(solution)/shard_map/grad_half/pallas_call | solution.py:688
  164.0 10.3 %ema_fourth.1 = (f32[2,128,768]{2,1,0:T(8,128)S(1)}, bf16[64,768]{1,0:T(8,128)(2,1)S(1)}) custom-call(s32[2]{0:T(128)S(1)} %get-tuple-element.305.place_ref, s32[16]{0:T(128)S(1)} %copy-done.50, f32[16]{0:T(128)S(1)} %copy-done.57, f32[2,128]{1,0:T(2,128)S(1)} %subtract_bitcast_fusion.1.keep_ref, f32[2,128]{1,0:T(2,128)S(1)} %subtract_bitcast_fusion.next_ref, ...), custom_call_target="tpu_custom_call" | custom-call | flops 1 | bytes 1 | tf_op jit(solution)/shard_map/ema_fourth/pallas_call | solution.py:240
  176.4 6.7 %collective-permute-done.36 = bf16[4,96,768]{2,1,0:T(8,128)(2,1)S(1)} collective-permute-done((bf16[4,96,768]{2,1,0:T(8,128)(2,1)S(1)}, bf16[4,96,768]{2,1,0:T(8,128)(2,1)S(1)}, u32[]{:S(2)}, u32[]{:S(2)}) %collective-permute-start.36) | collective-permute-done | bytes 589856 | tf_op jit(solution)/shard_map/ppermute | solution.py:767
  184.6 9.9 %collective-permute-done.44 = bf16[2,48,3072]{2,1,0:T(8,128)(2,1)S(1)} collective-permute-done((bf16[2,48,3072]{2,1,0:T(8,128)(2,1)S(1)}, bf16[2,48,3072]{2,1,0:T(8,128)(2,1)S(1)}, u32[]{:S(2)}, u32[]{:S(2)}) %collective-permute-start.44) | collective-permute-done | bytes 589856 | tf_op jit(solution)/shard_map/ppermute | solution.py:767
  197.2 2.1 collective-permute-start.49
  199.3 2.4 collective-permute-start.48
  201.7 2.7 collective-permute-done.42
  204.7 4.1 %collective-permute-start.46 = (bf16[1,192,768]{2,1,0:T(8,128)(2,1)S(1)}, bf16[1,192,768]{2,1,0:T(8,128)(2,1)S(1)}, u32[]{:S(2)}, u32[]{:S(2)}) collective-permute-start(bf16[1,192,768]{2,1,0:T(8,128)(2,1)S(1)} %add_convert_fusion.19), channel_id=1, source_target_pairs={{0,16},{2,18},{4,20},{6,22},{8,24},{10,26},{12,28},{14,30},{16,0},... | collective-permute-start | bytes 884744 | tf_op jit(solution)/shard_map/ppermute | solution.py:767
  208.7 10.4 %collective-permute-done.40 = bf16[512,768]{1,0:T(8,128)(2,1)S(1)} collective-permute-done((bf16[512,768]{1,0:T(8,128)(2,1)S(1)}, bf16[512,768]{1,0:T(8,128)(2,1)S(1)}, u32[]{:S(2)}, u32[]{:S(2)}) %collective-permute-start.40) | collective-permute-done | bytes 786464 | tf_op jit(solution)/shard_map/ppermute | solution.py:914
  220.2 2.6 collective-permute-start.53
  226.9 7.4 %collective-permute-done.45 = bf16[256,768]{1,0:T(8,128)(2,1)S(1)} collective-permute-done((bf16[256,768]{1,0:T(8,128)(2,1)S(1)}, bf16[256,768]{1,0:T(8,128)(2,1)S(1)}, u32[]{:S(2)}, u32[]{:S(2)}) %collective-permute-start.45) | collective-permute-done | bytes 393248 | tf_op jit(solution)/shard_map/ppermute | solution.py:914
  235.3 5.7 %collective-permute-done.54 = bf16[1,192,768]{2,1,0:T(8,128)(2,1)} collective-permute-done((bf16[1,192,768]{2,1,0:T(8,128)(2,1)S(1)}, bf16[1,192,768]{2,1,0:T(8,128)(2,1)}, u32[]{:S(2)}, u32[]{:S(2)}) %collective-permute-start.54) | collective-permute-done | bytes 294944 | tf_op jit(solution)/shard_map/ppermute | solution.py:767
  243.2 2.1 collective-permute-start.57
  248.9 2.9 collective-permute-done.57
  251.9 2.5 collective-permute-done.56
  254.4 2.1 collective-permute-done.55
  257.5 4.9 %collective-permute-done.60 = bf16[104,768]{1,0:T(8,128)(2,1)S(1)} collective-permute-done((bf16[104,768]{1,0:T(8,128)(2,1)S(1)}, bf16[104,768]{1,0:T(8,128)(2,1)S(1)}, u32[]{:S(2)}, u32[]{:S(2)}) %collective-permute-start.60) | collective-permute-done | bytes 159776 | tf_op jit(solution)/shard_map/ppermute | solution.py:767
  263.2 3.8 %collective-permute-start.66 = (bf16[2,192,768]{2,1,0:T(8,128)(2,1)S(1)}, bf16[2,192,768]{2,1,0:T(8,128)(2,1)S(1)}, u32[]{:S(2)}, u32[]{:S(2)}) collective-permute-start(bf16[2,192,768]{2,1,0:T(8,128)(2,1)S(1)} %pad_maximum_fusion.3), channel_id=1, source_target_pairs={{0,4},{2,6},{4,0},{6,2},{8,12},{10,14},{12,8},{14,10},{16,20},{18,... | collective-permute-start | bytes 1769480 | tf_op jit(solution)/shard_map/ppermute | solution.py:767
  266.9 1.9 collective-permute-done.61
  268.9 10.7 %collective-permute-start.62 = (bf16[104,768]{1,0:T(8,128)(2,1)S(1)}, bf16[104,768]{1,0:T(8,128)(2,1)S(1)}, u32[]{:S(2)}, u32[]{:S(2)}) collective-permute-start(bf16[104,768]{1,0:T(8,128)(2,1)S(1)} %add_convert_fusion.29), channel_id=1, source_target_pairs={{0,16},{2,18},{4,20},{6,22},{8,24},{10,26},{12,28},{14,30},{16,0},... | collective-permute-start | bytes 479240 | tf_op jit(solution)/shard_map/ppermute | solution.py:767
  280.0 1.7 collective-permute-start.65
  281.7 4.2 %collective-permute-done.62 = bf16[104,768]{1,0:T(8,128)(2,1)S(1)} collective-permute-done((bf16[104,768]{1,0:T(8,128)(2,1)S(1)}, bf16[104,768]{1,0:T(8,128)(2,1)S(1)}, u32[]{:S(2)}, u32[]{:S(2)}) %collective-permute-start.62) | collective-permute-done | bytes 159776 | tf_op jit(solution)/shard_map/ppermute | solution.py:767
  286.6 2.9 collective-permute-done.67
  291.4 1.5 collective-permute-start.70
  296.8 1.6 collective-permute-start.71
  299.1 2.5 put_in_place.8.refs_0_
  301.6 3.1 put_in_place.9
  304.7 2.5 put_in_place.10.refs_0_
  307.2 3.2 put_in_place.11.refs_0_
  310.4 2.7 collective-permute-done.71.own_ref
  313.1 6.4 %collective-permute-done.70.own_ref = bf16[4,192,768]{2,1,0:T(8,128)(2,1)S(1)} collective-permute-done((bf16[4,192,768]{2,1,0:T(8,128)(2,1)S(1)}, bf16[4,192,768]{2,1,0:T(8,128)(2,1)S(1)}, u32[]{:S(2)}, u32[]{:S(2)}) %collective-permute-start.70) | collective-permute-done | bytes 1179680 | tf_op jit(solution)/shard_map/ppermute | solution.py:767
  319.4 5.1 %collective-permute-done.69.own_ref = bf16[4,96,768]{2,1,0:T(8,128)(2,1)} collective-permute-done((bf16[4,96,768]{2,1,0:T(8,128)(2,1)S(1)}, bf16[4,96,768]{2,1,0:T(8,128)(2,1)}, u32[]{:S(2)}, u32[]{:S(2)}) %collective-permute-start.69) | collective-permute-done | bytes 589856 | tf_op jit(solution)/shard_map/ppermute | solution.py:767
  328.7 4.3 %put_in_place.12 = f32[2,8,96,768]{3,2,1,0:T(8,128)} custom-call(s32[1]{0:T(128)} %bitcast.30.half_ref.core_ref, s32[4]{0:T(128)S(1)} %get-tuple-element.358.place_ref, bf16[4,96,768]{2,1,0:T(8,128)(2,1)} %collective-permute-done.71.own_ref, bf16[4,96,768]{2,1,0:T(8,128)(2,1)} %collective-permute-done.79.other_ref, ...), custom_call_target="tpu_custom_call", output_to_operand_aliasing={{}: (4, {})} | custom-call | flops 1 | bytes 1 | tf_op jit(solution)/shard_map/put_in_place/pallas_call | solution.py:734
  333.0 4.7 %put_in_place.13 = (f32[2,8,96,768]{3,2,1,0:T(8,128)}, f32[8,96,1536]{2,1,0:T(8,128)}) custom-call(s32[1]{0:T(128)} %bitcast.30.half_ref.core_ref, s32[4]{0:T(128)S(1)} %get-tuple-element.360.place_ref, bf16[4,192,768]{2,1,0:T(8,128)(2,1)S(1)} %collective-permute-done.70.own_ref, ...), custom_call_target="tpu_custom_call", output_to_operand_aliasing={{0}: (4, {}), {1}: (5, {})} | custom-call | flops 1 | bytes 1 | tf_op jit(solution)/shard_map/put_in_place/pallas_call | solution.py:734
  337.6 4.3 %put_in_place.14 = f32[8,96,1536]{2,1,0:T(8,128)} custom-call(s32[1]{0:T(128)} %bitcast.30.half_ref.core_ref, s32[4]{0:T(128)S(1)} %get-tuple-element.362.place_ref, bf16[4,96,768]{2,1,0:T(8,128)(2,1)} %collective-permute-done.69.own_ref, bf16[4,96,768]{2,1,0:T(8,128)(2,1)} %collective-permute-done.77.other_ref, ...), custom_call_target="tpu_custom_call", output_to_operand_aliasing={{}: (4, {})} | custom-call | flops 1 | bytes 1 | tf_op jit(solution)/shard_map/put_in_place/pallas_call | solution.py:734
  341.9 3.2 put_in_place.15
  (434 shorter events, 79.7 us)
Async XLA Ops:
  1.7 13.2 %collective-permute-start.1 = (bf16[1,128,768]{2,1,0:T(8,128)(2,1)S(1)}, bf16[1,128,768]{2,1,0:T(8,128)(2,1)S(1)}, u32[]{:S(2)}, u32[]{:S(2)}) collective-permute-start(bf16[1,128,768]{2,1,0:T(8,128)(2,1)S(1)} %get-tuple-element.332), channel_id=1, source_target_pairs={{0,0},{1,16},{2,2},{3,18},{4,4},{5,20},{6,6},{7,22},{8,8},{9,24},{... | collective-permute-start | bytes 589832 | tf_op jit(solution)/shard_map/ppermute | solution.py:897
  2.4 12.5 %collective-permute-start.2 = (bf16[1,128,768]{2,1,0:T(8,128)(2,1)S(1)}, bf16[1,128,768]{2,1,0:T(8,128)(2,1)S(1)}, u32[]{:S(2)}, u32[]{:S(2)}) collective-permute-start(bf16[1,128,768]{2,1,0:T(8,128)(2,1)S(1)} %get-tuple-element.331), channel_id=1, source_target_pairs={{0,8},{1,24},{2,10},{3,26},{4,12},{5,28},{6,14},{7,30},{8,0},{9,16... | collective-permute-start | bytes 589832 | tf_op jit(solution)/shard_map/ppermute | solution.py:897
  5.5 8.2 %collective-permute-start = (s32[2,8]{1,0:T(2,128)}, s32[2,8]{1,0:T(2,128)S(1)}, u32[]{:S(2)}, u32[]{:S(2)}) collective-permute-start(s32[2,8]{1,0:T(2,128)} %param.20), channel_id=1, source_target_pairs={{0,1},{1,0},{2,3},{3,2},{4,5},{5,4},{6,7},{7,6},{8,9},{9,8},{10,11... | collective-permute-start | bytes 200 | tf_op jit(solution)/shard_map/ppermute | solution.py:944
  19.2 6.1 %collective-permute-start.4 = (f32[2,16,768]{2,1,0:T(8,128)S(1)}, f32[2,16,768]{2,1,0:T(8,128)S(1)}, u32[]{:S(2)}, u32[]{:S(2)}) collective-permute-start(f32[2,16,768]{2,1,0:T(8,128)S(1)} %get-tuple-element.154), channel_id=1, source_target_pairs={{0,4},{2,6},{4,0},{6,2},{1,5},{3,7},{5,1},{7,3},{8,12},{10,14},{12... | collective-permute-start | bytes 294920 | tf_op jit(solution)/shard_map/ppermute | solution.py:914
  26.3 6.9 %collective-permute-start.6 = (f32[8,16,768]{2,1,0:T(8,128)S(1)}, f32[8,16,768]{2,1,0:T(8,128)S(1)}, u32[]{:S(2)}, u32[]{:S(2)}) collective-permute-start(f32[8,16,768]{2,1,0:T(8,128)S(1)} %get-tuple-element.345), channel_id=1, source_target_pairs={{0,1},{1,0},{2,3},{3,2},{4,5},{5,4},{6,7},{7,6},{8,9},{9,8},{10,11... | collective-permute-start | bytes 1179656 | tf_op jit(solution)/shard_map/ppermute | solution.py:762
  29.6 11.5 %collective-permute-start.11 = (bf16[2,128,768]{2,1,0:T(8,128)(2,1)S(1)}, bf16[2,128,768]{2,1,0:T(8,128)(2,1)S(1)}, u32[]{:S(2)}, u32[]{:S(2)}) collective-permute-start(bf16[2,128,768]{2,1,0:T(8,128)(2,1)S(1)} %constant_dynamic-update-slice_fusion.x_ref), channel_id=1, source_target_pairs={{0,2},{2,0},{4,6},{6,4},{1,3},{3,1},{5,7},{7,5},{8,10},{10,8},{12,... | collective-permute-start | bytes 1179656 | tf_op jit(solution)/shard_map/ppermute | solution.py:914
  30.8 11.6 %collective-permute-start.12 = (bf16[2,128,768]{2,1,0:T(8,128)(2,1)S(1)}, bf16[2,128,768]{2,1,0:T(8,128)(2,1)S(1)}, u32[]{:S(2)}, u32[]{:S(2)}) collective-permute-start(bf16[2,128,768]{2,1,0:T(8,128)(2,1)S(1)} %constant_dynamic-update-slice_fusion.x_ref), channel_id=1, source_target_pairs={{0,4},{2,6},{4,0},{6,2},{1,5},{3,7},{5,1},{7,3},{8,12},{10,14},{12... | collective-permute-start | bytes 1179656 | tf_op jit(solution)/shard_map/ppermute | solution.py:914
  31.7 16.2 %collective-permute-start.13 = (bf16[2,128,768]{2,1,0:T(8,128)(2,1)S(1)}, bf16[2,128,768]{2,1,0:T(8,128)(2,1)S(1)}, u32[]{:S(2)}, u32[]{:S(2)}) collective-permute-start(bf16[2,128,768]{2,1,0:T(8,128)(2,1)S(1)} %constant_dynamic-update-slice_fusion.x_ref), channel_id=1, source_target_pairs={{0,6},{2,4},{4,2},{6,0},{1,7},{3,5},{5,3},{7,1},{8,14},{10,12},{12... | collective-permute-start | bytes 1179656 | tf_op jit(solution)/shard_map/ppermute | solution.py:914
  38.9 15.7 %collective-permute-start.7 = (bf16[256,128]{1,0:T(8,128)(2,1)S(1)}, bf16[256,128]{1,0:T(8,128)(2,1)S(1)}, u32[]{:S(2)}, u32[]{:S(2)}) collective-permute-start(bf16[256,128]{1,0:T(8,128)(2,1)S(1)} %get-tuple-element.301), channel_id=1, source_target_pairs={{0,2},{2,0},{4,6},{6,4},{1,3},{3,1},{5,7},{7,5},{8,10},{10,8},{12,... | collective-permute-start | bytes 196616 | tf_op jit(solution)/shard_map/ppermute | solution.py:914
  40.1 14.5 %collective-permute-start.8 = (bf16[256,128]{1,0:T(8,128)(2,1)S(1)}, bf16[256,128]{1,0:T(8,128)(2,1)S(1)}, u32[]{:S(2)}, u32[]{:S(2)}) collective-permute-start(bf16[256,128]{1,0:T(8,128)(2,1)S(1)} %get-tuple-element.301), channel_id=1, source_target_pairs={{0,4},{2,6},{4,0},{6,2},{1,5},{3,7},{5,1},{7,3},{8,12},{10,14},{12... | collective-permute-start | bytes 196616 | tf_op jit(solution)/shard_map/ppermute | solution.py:914
  41.0 13.6 %collective-permute-start.9 = (bf16[256,128]{1,0:T(8,128)(2,1)S(1)}, bf16[256,128]{1,0:T(8,128)(2,1)S(1)}, u32[]{:S(2)}, u32[]{:S(2)}) collective-permute-start(bf16[256,128]{1,0:T(8,128)(2,1)S(1)} %get-tuple-element.301), channel_id=1, source_target_pairs={{0,6},{2,4},{4,2},{6,0},{1,7},{3,5},{5,3},{7,1},{8,14},{10,12},{12... | collective-permute-start | bytes 196616 | tf_op jit(solution)/shard_map/ppermute | solution.py:914
  48.1 8.2 %collective-permute-start.14 = (bf16[8,128,768]{2,1,0:T(8,128)(2,1)S(1)}, bf16[8,128,768]{2,1,0:T(8,128)(2,1)S(1)}, u32[]{:S(2)}, u32[]{:S(2)}) collective-permute-start(bf16[8,128,768]{2,1,0:T(8,128)(2,1)S(1)} %pad_maximum_fusion), channel_id=1, source_target_pairs={{0,1},{1,0},{2,3},{3,2},{4,5},{5,4},{6,7},{7,6},{8,9},{9,8},{10,11... | collective-permute-start | bytes 4718600 | tf_op jit(solution)/shard_map/ppermute | solution.py:762
  89.5 21.1 %collective-permute-start.18 = (bf16[4,192,768]{2,1,0:T(8,128)(2,1)}, bf16[4,192,768]{2,1,0:T(8,128)(2,1)}, u32[]{:S(2)}, u32[]{:S(2)}) collective-permute-start(bf16[4,192,768]{2,1,0:T(8,128)(2,1)} %get-tuple-element.170), channel_id=1, source_target_pairs={{0,1},{1,0},{2,3},{3,2},{4,5},{5,4},{6,7},{7,6},{8,9},{9,8},{10,11... | collective-permute-start | bytes 3538952 | tf_op jit(solution)/shard_map/ppermute | solution.py:762
  95.7 21.1 %collective-permute-start.20 = (bf16[4,48,3072]{2,1,0:T(8,128)(2,1)S(1)}, bf16[4,48,3072]{2,1,0:T(8,128)(2,1)S(1)}, u32[]{:S(2)}, u32[]{:S(2)}) collective-permute-start(bf16[4,48,3072]{2,1,0:T(8,128)(2,1)S(1)} %get-tuple-element.172), channel_id=1, source_target_pairs={{0,1},{1,0},{2,3},{3,2},{4,5},{5,4},{6,7},{7,6},{8,9},{9,8},{10,11... | collective-permute-start | bytes 3538952 | tf_op jit(solution)/shard_map/ppermute | solution.py:762
  109.4 12.1 %collective-permute-start.29 = (bf16[4,192,768]{2,1,0:T(8,128)(2,1)S(1)}, bf16[4,192,768]{2,1,0:T(8,128)(2,1)S(1)}, u32[]{:S(2)}, u32[]{:S(2)}) collective-permute-start(bf16[4,192,768]{2,1,0:T(8,128)(2,1)S(1)} %copy-done.63), channel_id=1, source_target_pairs={{0,1},{1,0},{2,3},{3,2},{4,5},{5,4},{6,7},{7,6},{8,9},{9,8},{10,11... | collective-permute-start | bytes 3538952 | tf_op jit(solution)/shard_map/ppermute | solution.py:762
  109.7 11.3 %collective-permute-start.38 = (bf16[4,48,3072]{2,1,0:T(8,128)(2,1)S(1)}, bf16[4,48,3072]{2,1,0:T(8,128)(2,1)S(1)}, u32[]{:S(2)}, u32[]{:S(2)}) collective-permute-start(bf16[4,48,3072]{2,1,0:T(8,128)(2,1)S(1)} %get-tuple-element.230), channel_id=1, source_target_pairs={{0,1},{1,0},{2,3},{3,2},{4,5},{5,4},{6,7},{7,6},{8,9},{9,8},{10,11... | collective-permute-start | bytes 3538952 | tf_op jit(solution)/shard_map/ppermute | solution.py:762
  112.2 49.4 %collective-permute-start.30 = (bf16[4,192,768]{2,1,0:T(8,128)(2,1)S(1)}, bf16[4,192,768]{2,1,0:T(8,128)(2,1)S(1)}, u32[]{:S(2)}, u32[]{:S(2)}) collective-permute-start(bf16[4,192,768]{2,1,0:T(8,128)(2,1)S(1)} %add_convert_fusion.4), channel_id=1, source_target_pairs={{0,8},{2,10},{4,12},{6,14},{8,0},{10,2},{12,4},{14,6},{16,24},{18,... | collective-permute-start | bytes 3538952 | tf_op jit(solution)/shard_map/ppermute | solution.py:767
  117.2 57.1 %collective-permute-start.39 = (bf16[4,48,3072]{2,1,0:T(8,128)(2,1)S(1)}, bf16[4,48,3072]{2,1,0:T(8,128)(2,1)S(1)}, u32[]{:S(2)}, u32[]{:S(2)}) collective-permute-start(bf16[4,48,3072]{2,1,0:T(8,128)(2,1)S(1)} %add_convert_fusion.3), channel_id=1, source_target_pairs={{0,8},{2,10},{4,12},{6,14},{8,0},{10,2},{12,4},{14,6},{16,24},{18,... | collective-permute-start | bytes 3538952 | tf_op jit(solution)/shard_map/ppermute | solution.py:767
  121.0 6.1 %collective-permute-start.22 = (bf16[4,96,768]{2,1,0:T(8,128)(2,1)S(1)}, bf16[4,96,768]{2,1,0:T(8,128)(2,1)S(1)}, u32[]{:S(2)}, u32[]{:S(2)}) collective-permute-start(bf16[4,96,768]{2,1,0:T(8,128)(2,1)S(1)} %get-tuple-element.188), channel_id=1, source_target_pairs={{0,1},{1,0},{2,3},{3,2},{4,5},{5,4},{6,7},{7,6},{8,9},{9,8},{10,11... | collective-permute-start | bytes 1769480 | tf_op jit(solution)/shard_map/ppermute | solution.py:762
  121.5 30.5 %collective-permute-start.24 = (bf16[4,96,768]{2,1,0:T(8,128)(2,1)S(1)}, bf16[4,96,768]{2,1,0:T(8,128)(2,1)S(1)}, u32[]{:S(2)}, u32[]{:S(2)}) collective-permute-start(bf16[4,96,768]{2,1,0:T(8,128)(2,1)S(1)} %get-tuple-element.202), channel_id=1, source_target_pairs={{0,1},{1,0},{2,3},{3,2},{4,5},{5,4},{6,7},{7,6},{8,9},{9,8},{10,11... | collective-permute-start | bytes 1769480 | tf_op jit(solution)/shard_map/ppermute | solution.py:762
  125.7 15.6 %collective-permute-start.21 = (bf16[256,128]{1,0:T(8,128)(2,1)S(1)}, bf16[256,128]{1,0:T(8,128)(2,1)S(1)}, u32[]{:S(2)}, u32[]{:S(2)}) collective-permute-start(bf16[256,128]{1,0:T(8,128)(2,1)S(1)} %get-tuple-element.337), channel_id=1, source_target_pairs={{0,2},{2,0},{4,6},{6,4},{1,3},{3,1},{5,7},{7,5},{8,10},{10,8},{12,... | collective-permute-start | bytes 196616 | tf_op jit(solution)/shard_map/ppermute | solution.py:914
  127.2 25.0 %collective-permute-start.25 = (bf16[4,96,768]{2,1,0:T(8,128)(2,1)S(1)}, bf16[4,96,768]{2,1,0:T(8,128)(2,1)S(1)}, u32[]{:S(2)}, u32[]{:S(2)}) collective-permute-start(bf16[4,96,768]{2,1,0:T(8,128)(2,1)S(1)} %add_convert_fusion.13), channel_id=1, source_target_pairs={{0,2},{2,0},{4,6},{6,4},{8,10},{10,8},{12,14},{14,12},{16,18},{18,... | collective-permute-start | bytes 1769480 | tf_op jit(solution)/shard_map/ppermute | solution.py:767
  146.2 6.7 %collective-permute-start.23 = (f32[2,16,768]{2,1,0:T(8,128)S(1)}, f32[2,16,768]{2,1,0:T(8,128)S(1)}, u32[]{:S(2)}, u32[]{:S(2)}) collective-permute-start(f32[2,16,768]{2,1,0:T(8,128)S(1)} %get-tuple-element.200), channel_id=1, source_target_pairs={{0,2},{2,0},{4,6},{6,4},{1,3},{3,1},{5,7},{7,5},{8,10},{10,8},{12,... | collective-permute-start | bytes 294920 | tf_op jit(solution)/shard_map/ppermute | solution.py:914
  152.0 10.1 %collective-permute-start.28 = (bf16[4,96,768]{2,1,0:T(8,128)(2,1)S(1)}, bf16[4,96,768]{2,1,0:T(8,128)(2,1)S(1)}, u32[]{:S(2)}, u32[]{:S(2)}) collective-permute-start(bf16[4,96,768]{2,1,0:T(8,128)(2,1)S(1)} %get-tuple-element.206), channel_id=1, source_target_pairs={{0,1},{1,0},{2,3},{3,2},{4,5},{5,4},{6,7},{7,6},{8,9},{9,8},{10,11... | collective-permute-start | bytes 1769480 | tf_op jit(solution)/shard_map/ppermute | solution.py:762
  152.3 10.2 %collective-permute-start.35 = (bf16[4,96,768]{2,1,0:T(8,128)(2,1)S(1)}, bf16[4,96,768]{2,1,0:T(8,128)(2,1)S(1)}, u32[]{:S(2)}, u32[]{:S(2)}) collective-permute-start(bf16[4,96,768]{2,1,0:T(8,128)(2,1)S(1)} %get-tuple-element.227), channel_id=1, source_target_pairs={{0,1},{1,0},{2,3},{3,2},{4,5},{5,4},{6,7},{7,6},{8,9},{9,8},{10,11... | collective-permute-start | bytes 1769480 | tf_op jit(solution)/shard_map/ppermute | solution.py:762
  153.0 7.4 %collective-permute-start.26 = (f32[4,16,768]{2,1,0:T(8,128)S(1)}, f32[4,16,768]{2,1,0:T(8,128)S(1)}, u32[]{:S(2)}, u32[]{:S(2)}) collective-permute-start(f32[4,16,768]{2,1,0:T(8,128)S(1)} %get-tuple-element.341), channel_id=1, source_target_pairs={{0,4},{2,6},{4,0},{6,2},{1,5},{3,7},{5,1},{7,3},{8,12},{10,14},{12... | collective-permute-start | bytes 589832 | tf_op jit(solution)/shard_map/ppermute | solution.py:914
  160.5 15.3 %collective-permute-start.37 = (bf16[2,96,768]{2,1,0:T(8,128)(2,1)S(1)}, bf16[2,96,768]{2,1,0:T(8,128)(2,1)S(1)}, u32[]{:S(2)}, u32[]{:S(2)}) collective-permute-start(bf16[2,96,768]{2,1,0:T(8,128)(2,1)S(1)} %get-tuple-element.313), channel_id=1, source_target_pairs={{0,4},{2,6},{4,0},{6,2},{8,12},{10,14},{12,8},{14,10},{16,20},{18,... | collective-permute-start | bytes 884744 | tf_op jit(solution)/shard_map/ppermute | solution.py:767
  162.1 22.0 %collective-permute-start.34 = (bf16[2,192,768]{2,1,0:T(8,128)(2,1)S(1)}, bf16[2,192,768]{2,1,0:T(8,128)(2,1)S(1)}, u32[]{:S(2)}, u32[]{:S(2)}) collective-permute-start(bf16[2,192,768]{2,1,0:T(8,128)(2,1)S(1)} %get-tuple-element.309), channel_id=1, source_target_pairs={{0,2},{2,0},{4,6},{6,4},{8,10},{10,8},{12,14},{14,12},{16,18},{18,... | collective-permute-start | bytes 1769480 | tf_op jit(solution)/shard_map/ppermute | solution.py:767
  162.4 20.6 %collective-permute-start.36 = (bf16[4,96,768]{2,1,0:T(8,128)(2,1)S(1)}, bf16[4,96,768]{2,1,0:T(8,128)(2,1)S(1)}, u32[]{:S(2)}, u32[]{:S(2)}) collective-permute-start(bf16[4,96,768]{2,1,0:T(8,128)(2,1)S(1)} %add_convert_fusion.10), channel_id=1, source_target_pairs={{0,4},{2,6},{4,0},{6,2},{8,12},{10,14},{12,8},{14,10},{16,20},{18,... | collective-permute-start | bytes 1769480 | tf_op jit(solution)/shard_map/ppermute | solution.py:767
  163.7 30.8 %collective-permute-start.33 = (bf16[1024,768]{1,0:T(8,128)(2,1)S(1)}, bf16[1024,768]{1,0:T(8,128)(2,1)S(1)}, u32[]{:S(2)}, u32[]{:S(2)}) collective-permute-start(bf16[1024,768]{1,0:T(8,128)(2,1)S(1)} %get-tuple-element.224), channel_id=1, source_target_pairs={{0,1},{1,0},{2,3},{3,2},{4,5},{5,4},{6,7},{7,6},{8,9},{9,8},{10,11... | collective-permute-start | bytes 4718600 | tf_op jit(solution)/shard_map/ppermute | solution.py:762
  174.7 19.8 %collective-permute-start.44 = (bf16[2,48,3072]{2,1,0:T(8,128)(2,1)S(1)}, bf16[2,48,3072]{2,1,0:T(8,128)(2,1)S(1)}, u32[]{:S(2)}, u32[]{:S(2)}) collective-permute-start(bf16[2,48,3072]{2,1,0:T(8,128)(2,1)S(1)} %get-tuple-element.307), channel_id=1, source_target_pairs={{0,4},{2,6},{4,0},{6,2},{8,12},{10,14},{12,8},{14,10},{16,20},{18,... | collective-permute-start | bytes 1769480 | tf_op jit(solution)/shard_map/ppermute | solution.py:767
  175.8 23.4 %collective-permute-start.43 = (bf16[1,96,768]{2,1,0:T(8,128)(2,1)S(1)}, bf16[1,96,768]{2,1,0:T(8,128)(2,1)S(1)}, u32[]{:S(2)}, u32[]{:S(2)}) collective-permute-start(bf16[1,96,768]{2,1,0:T(8,128)(2,1)S(1)} %add_convert_fusion.40), channel_id=1, source_target_pairs={{0,8},{2,10},{4,12},{6,14},{8,0},{10,2},{12,4},{14,6},{16,24},{18,... | collective-permute-start | bytes 442376 | tf_op jit(solution)/shard_map/ppermute | solution.py:767
  183.1 12.8 %collective-permute-start.31 = (bf16[1,128,768]{2,1,0:T(8,128)(2,1)S(1)}, bf16[1,128,768]{2,1,0:T(8,128)(2,1)S(1)}, u32[]{:S(2)}, u32[]{:S(2)}) collective-permute-start(bf16[1,128,768]{2,1,0:T(8,128)(2,1)S(1)} %get-tuple-element.327), channel_id=1, source_target_pairs={{0,0},{16,1},{2,2},{18,3},{4,4},{20,5},{6,6},{22,7},{8,8},{24,9},{... | collective-permute-start | bytes 589832 | tf_op jit(solution)/shard_map/ppermute | solution.py:904
  184.1 11.9 %collective-permute-start.32 = (bf16[1,128,768]{2,1,0:T(8,128)(2,1)S(1)}, bf16[1,128,768]{2,1,0:T(8,128)(2,1)S(1)}, u32[]{:S(2)}, u32[]{:S(2)}) collective-permute-start(bf16[1,128,768]{2,1,0:T(8,128)(2,1)S(1)} %get-tuple-element.328), channel_id=1, source_target_pairs={{8,0},{24,1},{10,2},{26,3},{12,4},{28,5},{14,6},{30,7},{0,8},{16,9... | collective-permute-start | bytes 589832 | tf_op jit(solution)/shard_map/ppermute | solution.py:904
  194.5 9.9 %collective-permute-start.42 = (bf16[2,96,768]{2,1,0:T(8,128)(2,1)S(1)}, bf16[2,96,768]{2,1,0:T(8,128)(2,1)S(1)}, u32[]{:S(2)}, u32[]{:S(2)}) collective-permute-start(bf16[2,96,768]{2,1,0:T(8,128)(2,1)S(1)} %get-tuple-element.311), channel_id=1, source_target_pairs={{0,2},{2,0},{4,6},{6,4},{8,10},{10,8},{12,14},{14,12},{16,18},{18,... | collective-permute-start | bytes 884744 | tf_op jit(solution)/shard_map/ppermute | solution.py:767
  194.5 10.0 %collective-permute-start.41 = (bf16[1,192,768]{2,1,0:T(8,128)(2,1)S(1)}, bf16[1,192,768]{2,1,0:T(8,128)(2,1)S(1)}, u32[]{:S(2)}, u32[]{:S(2)}) collective-permute-start(bf16[1,192,768]{2,1,0:T(8,128)(2,1)S(1)} %add_convert_fusion.23), channel_id=1, source_target_pairs={{0,4},{2,6},{4,0},{6,2},{8,12},{10,14},{12,8},{14,10},{16,20},{18,... | collective-permute-start | bytes 884744 | tf_op jit(solution)/shard_map/ppermute | solution.py:767
  196.0 23.1 %collective-permute-start.40 = (bf16[512,768]{1,0:T(8,128)(2,1)S(1)}, bf16[512,768]{1,0:T(8,128)(2,1)S(1)}, u32[]{:S(2)}, u32[]{:S(2)}) collective-permute-start(bf16[512,768]{1,0:T(8,128)(2,1)S(1)} %slice.267), channel_id=1, source_target_pairs={{0,4},{2,6},{4,0},{6,2},{1,5},{3,7},{5,1},{7,3},{8,12},{10,14},{12... | collective-permute-start | bytes 2359304 | tf_op jit(solution)/shard_map/ppermute | solution.py:914
  197.2 22.1 %collective-permute-start.49 = (bf16[1,48,3072]{2,1,0:T(8,128)(2,1)S(1)}, bf16[1,48,3072]{2,1,0:T(8,128)(2,1)S(1)}, u32[]{:S(2)}, u32[]{:S(2)}) collective-permute-start(bf16[1,48,3072]{2,1,0:T(8,128)(2,1)S(1)} %add_convert_fusion.20), channel_id=1, source_target_pairs={{0,2},{2,0},{4,6},{6,4},{8,10},{10,8},{12,14},{14,12},{16,18},{18,... | collective-permute-start | bytes 884744 | tf_op jit(solution)/shard_map/ppermute | solution.py:767
  199.3 23.4 %collective-permute-start.48 = (bf16[1,96,768]{2,1,0:T(8,128)(2,1)S(1)}, bf16[1,96,768]{2,1,0:T(8,128)(2,1)S(1)}, u32[]{:S(2)}, u32[]{:S(2)}) collective-permute-start(bf16[1,96,768]{2,1,0:T(8,128)(2,1)S(1)} %add_convert_fusion.38), channel_id=1, source_target_pairs={{0,16},{2,18},{4,20},{6,22},{8,24},{10,26},{12,28},{14,30},{16,0},... | collective-permute-start | bytes 442376 | tf_op jit(solution)/shard_map/ppermute | solution.py:767
  204.5 19.7 %collective-permute-start.47 = (bf16[1,96,768]{2,1,0:T(8,128)(2,1)S(1)}, bf16[1,96,768]{2,1,0:T(8,128)(2,1)S(1)}, u32[]{:S(2)}, u32[]{:S(2)}) collective-permute-start(bf16[1,96,768]{2,1,0:T(8,128)(2,1)S(1)} %add_convert_fusion.37), channel_id=1, source_target_pairs={{0,8},{2,10},{4,12},{6,14},{8,0},{10,2},{12,4},{14,6},{16,24},{18,... | collective-permute-start | bytes 442376 | tf_op jit(solution)/shard_map/ppermute | solution.py:767
  204.7 20.8 %collective-permute-start.46 = (bf16[1,192,768]{2,1,0:T(8,128)(2,1)S(1)}, bf16[1,192,768]{2,1,0:T(8,128)(2,1)S(1)}, u32[]{:S(2)}, u32[]{:S(2)}) collective-permute-start(bf16[1,192,768]{2,1,0:T(8,128)(2,1)S(1)} %add_convert_fusion.19), channel_id=1, source_target_pairs={{0,16},{2,18},{4,20},{6,22},{8,24},{10,26},{12,28},{14,30},{16,0},... | collective-permute-start | bytes 884744 | tf_op jit(solution)/shard_map/ppermute | solution.py:767
  220.2 21.9 %collective-permute-start.53 = (bf16[1,48,3072]{2,1,0:T(8,128)(2,1)}, bf16[1,48,3072]{2,1,0:T(8,128)(2,1)}, u32[]{:S(2)}, u32[]{:S(2)}) collective-permute-start(bf16[1,48,3072]{2,1,0:T(8,128)(2,1)} %add_convert_fusion.17), channel_id=1, source_target_pairs={{0,16},{2,18},{4,20},{6,22},{8,24},{10,26},{12,28},{14,30},{16,0},... | collective-permute-start | bytes 884744 | tf_op jit(solution)/shard_map/ppermute | solution.py:767
  222.8 22.5 %collective-permute-start.52 = (bf16[1,96,768]{2,1,0:T(8,128)(2,1)S(1)}, bf16[1,96,768]{2,1,0:T(8,128)(2,1)S(1)}, u32[]{:S(2)}, u32[]{:S(2)}) collective-permute-start(bf16[1,96,768]{2,1,0:T(8,128)(2,1)S(1)} %add_convert_fusion.35), channel_id=1, source_target_pairs={{0,2},{2,0},{4,6},{6,4},{8,10},{10,8},{12,14},{14,12},{16,18},{18,... | collective-permute-start | bytes 442376 | tf_op jit(solution)/shard_map/ppermute | solution.py:767
  224.2 10.2 %collective-permute-start.45 = (bf16[256,768]{1,0:T(8,128)(2,1)S(1)}, bf16[256,768]{1,0:T(8,128)(2,1)S(1)}, u32[]{:S(2)}, u32[]{:S(2)}) collective-permute-start(bf16[256,768]{1,0:T(8,128)(2,1)S(1)} %slice.333), channel_id=1, source_target_pairs={{0,2},{2,0},{4,6},{6,4},{1,3},{3,1},{5,7},{7,5},{8,10},{10,8},{12,... | collective-permute-start | bytes 1179656 | tf_op jit(solution)/shard_map/ppermute | solution.py:914
  225.0 20.3 %collective-permute-start.51 = (bf16[1,96,768]{2,1,0:T(8,128)(2,1)S(1)}, bf16[1,96,768]{2,1,0:T(8,128)(2,1)}, u32[]{:S(2)}, u32[]{:S(2)}) collective-permute-start(bf16[1,96,768]{2,1,0:T(8,128)(2,1)S(1)} %add_convert_fusion.34), channel_id=1, source_target_pairs={{0,16},{2,18},{4,20},{6,22},{8,24},{10,26},{12,28},{14,30},{16,0},... | collective-permute-start | bytes 442376 | tf_op jit(solution)/shard_map/ppermute | solution.py:767
  225.6 15.5 %collective-permute-start.54 = (bf16[1,192,768]{2,1,0:T(8,128)(2,1)S(1)}, bf16[1,192,768]{2,1,0:T(8,128)(2,1)}, u32[]{:S(2)}, u32[]{:S(2)}) collective-permute-start(bf16[1,192,768]{2,1,0:T(8,128)(2,1)S(1)} %add_convert_fusion.16), channel_id=1, source_target_pairs={{0,8},{2,10},{4,12},{6,14},{8,0},{10,2},{12,4},{14,6},{16,24},{18,... | collective-permute-start | bytes 884744 | tf_op jit(solution)/shard_map/ppermute | solution.py:767
  243.2 8.6 %collective-permute-start.57 = (bf16[1,48,3072]{2,1,0:T(8,128)(2,1)S(1)}, bf16[1,48,3072]{2,1,0:T(8,128)(2,1)S(1)}, u32[]{:S(2)}, u32[]{:S(2)}) collective-permute-start(bf16[1,48,3072]{2,1,0:T(8,128)(2,1)S(1)} %add_convert_fusion.15), channel_id=1, source_target_pairs={{0,2},{2,0},{4,6},{6,4},{8,10},{10,8},{12,14},{14,12},{16,18},{18,... | collective-permute-start | bytes 884744 | tf_op jit(solution)/shard_map/ppermute | solution.py:767
  246.4 8.0 %collective-permute-start.56 = (bf16[1,96,768]{2,1,0:T(8,128)(2,1)S(1)}, bf16[1,96,768]{2,1,0:T(8,128)(2,1)S(1)}, u32[]{:S(2)}, u32[]{:S(2)}) collective-permute-start(bf16[1,96,768]{2,1,0:T(8,128)(2,1)S(1)} %add_convert_fusion.33), channel_id=1, source_target_pairs={{0,2},{2,0},{4,6},{6,4},{8,10},{10,8},{12,14},{14,12},{16,18},{18,... | collective-permute-start | bytes 442376 | tf_op jit(solution)/shard_map/ppermute | solution.py:767
  247.8 8.8 %collective-permute-start.55 = (bf16[104,768]{1,0:T(8,128)(2,1)S(1)}, bf16[104,768]{1,0:T(8,128)(2,1)S(1)}, u32[]{:S(2)}, u32[]{:S(2)}) collective-permute-start(bf16[104,768]{1,0:T(8,128)(2,1)S(1)} %add_convert_fusion.32), channel_id=1, source_target_pairs={{0,2},{2,0},{4,6},{6,4},{8,10},{10,8},{12,14},{14,12},{16,18},{18,... | collective-permute-start | bytes 479240 | tf_op jit(solution)/shard_map/ppermute | solution.py:767
  263.2 26.4 %collective-permute-start.66 = (bf16[2,192,768]{2,1,0:T(8,128)(2,1)S(1)}, bf16[2,192,768]{2,1,0:T(8,128)(2,1)S(1)}, u32[]{:S(2)}, u32[]{:S(2)}) collective-permute-start(bf16[2,192,768]{2,1,0:T(8,128)(2,1)S(1)} %pad_maximum_fusion.3), channel_id=1, source_target_pairs={{0,4},{2,6},{4,0},{6,2},{8,12},{10,14},{12,8},{14,10},{16,20},{18,... | collective-permute-start | bytes 1769480 | tf_op jit(solution)/shard_map/ppermute | solution.py:767
  268.9 17.1 %collective-permute-start.62 = (bf16[104,768]{1,0:T(8,128)(2,1)S(1)}, bf16[104,768]{1,0:T(8,128)(2,1)S(1)}, u32[]{:S(2)}, u32[]{:S(2)}) collective-permute-start(bf16[104,768]{1,0:T(8,128)(2,1)S(1)} %add_convert_fusion.29), channel_id=1, source_target_pairs={{0,16},{2,18},{4,20},{6,22},{8,24},{10,26},{12,28},{14,30},{16,0},... | collective-permute-start | bytes 479240 | tf_op jit(solution)/shard_map/ppermute | solution.py:767
  279.6 9.9 %collective-permute-start.67 = (bf16[2,96,768]{2,1,0:T(8,128)(2,1)S(1)}, bf16[2,96,768]{2,1,0:T(8,128)(2,1)S(1)}, u32[]{:S(2)}, u32[]{:S(2)}) collective-permute-start(bf16[2,96,768]{2,1,0:T(8,128)(2,1)S(1)} %pad_maximum_fusion.9), channel_id=1, source_target_pairs={{0,4},{2,6},{4,0},{6,2},{8,12},{10,14},{12,8},{14,10},{16,20},{18,... | collective-permute-start | bytes 884744 | tf_op jit(solution)/shard_map/ppermute | solution.py:767
  280.0 13.8 %collective-permute-start.65 = (bf16[2,96,768]{2,1,0:T(8,128)(2,1)S(1)}, bf16[2,96,768]{2,1,0:T(8,128)(2,1)S(1)}, u32[]{:S(2)}, u32[]{:S(2)}) collective-permute-start(bf16[2,96,768]{2,1,0:T(8,128)(2,1)S(1)} %pad_maximum_fusion.10), channel_id=1, source_target_pairs={{0,4},{2,6},{4,0},{6,2},{8,12},{10,14},{12,8},{14,10},{16,20},{18,... | collective-permute-start | bytes 884744 | tf_op jit(solution)/shard_map/ppermute | solution.py:767
  281.7 13.3 %collective-permute-start.64 = (bf16[2,48,3072]{2,1,0:T(8,128)(2,1)S(1)}, bf16[2,48,3072]{2,1,0:T(8,128)(2,1)S(1)}, u32[]{:S(2)}, u32[]{:S(2)}) collective-permute-start(bf16[2,48,3072]{2,1,0:T(8,128)(2,1)S(1)} %pad_maximum_fusion.4), channel_id=1, source_target_pairs={{0,8},{2,10},{4,12},{6,14},{8,0},{10,2},{12,4},{14,6},{16,24},{18,... | collective-permute-start | bytes 1769480 | tf_op jit(solution)/shard_map/ppermute | solution.py:767
  290.7 7.6 %collective-permute-start.74 = (bf16[4,192,768]{2,1,0:T(8,128)(2,1)S(1)}, bf16[4,192,768]{2,1,0:T(8,128)(2,1)S(1)}, u32[]{:S(2)}, u32[]{:S(2)}) collective-permute-start(bf16[4,192,768]{2,1,0:T(8,128)(2,1)S(1)} %pad_maximum_fusion.1.own_ref), channel_id=1, source_target_pairs={{0,1},{1,0},{2,3},{3,2},{4,5},{5,4},{6,7},{7,6},{8,9},{9,8},{10,11... | collective-permute-start | bytes 3538952 | tf_op jit(solution)/shard_map/ppermute | solution.py:762
  291.4 28.0 %collective-permute-start.70 = (bf16[4,192,768]{2,1,0:T(8,128)(2,1)S(1)}, bf16[4,192,768]{2,1,0:T(8,128)(2,1)S(1)}, u32[]{:S(2)}, u32[]{:S(2)}) collective-permute-start(bf16[4,192,768]{2,1,0:T(8,128)(2,1)S(1)} %pad_maximum_fusion.1.own_ref), channel_id=1, source_target_pairs={{0,2},{2,0},{4,6},{6,4},{8,10},{10,8},{12,14},{14,12},{16,18},{18,... | collective-permute-start | bytes 3538952 | tf_op jit(solution)/shard_map/ppermute | solution.py:767
  295.1 12.0 %collective-permute-start.72 = (bf16[4,48,3072]{2,1,0:T(8,128)(2,1)S(1)}, bf16[4,48,3072]{2,1,0:T(8,128)(2,1)S(1)}, u32[]{:S(2)}, u32[]{:S(2)}) collective-permute-start(bf16[4,48,3072]{2,1,0:T(8,128)(2,1)S(1)} %pad_maximum_fusion.2.own_ref), channel_id=1, source_target_pairs={{0,1},{1,0},{2,3},{3,2},{4,5},{5,4},{6,7},{7,6},{8,9},{9,8},{10,11... | collective-permute-start | bytes 3538952 | tf_op jit(solution)/shard_map/ppermute | solution.py:762
  295.2 29.3 %collective-permute-start.68 = (bf16[4,48,3072]{2,1,0:T(8,128)(2,1)S(1)}, bf16[4,48,3072]{2,1,0:T(8,128)(2,1)S(1)}, u32[]{:S(2)}, u32[]{:S(2)}) collective-permute-start(bf16[4,48,3072]{2,1,0:T(8,128)(2,1)S(1)} %pad_maximum_fusion.2.own_ref), channel_id=1, source_target_pairs={{0,4},{2,6},{4,0},{6,2},{8,12},{10,14},{12,8},{14,10},{16,20},{18,... | collective-permute-start | bytes 3538952 | tf_op jit(solution)/shard_map/ppermute | solution.py:767
  296.8 16.3 %collective-permute-start.71 = (bf16[4,96,768]{2,1,0:T(8,128)(2,1)S(1)}, bf16[4,96,768]{2,1,0:T(8,128)(2,1)}, u32[]{:S(2)}, u32[]{:S(2)}) collective-permute-start(bf16[4,96,768]{2,1,0:T(8,128)(2,1)S(1)} %pad_maximum_fusion.5.own_ref), channel_id=1, source_target_pairs={{0,8},{2,10},{4,12},{6,14},{8,0},{10,2},{12,4},{14,6},{16,24},{18,... | collective-permute-start | bytes 1769480 | tf_op jit(solution)/shard_map/ppermute | solution.py:767
  298.3 26.2 %collective-permute-start.69 = (bf16[4,96,768]{2,1,0:T(8,128)(2,1)S(1)}, bf16[4,96,768]{2,1,0:T(8,128)(2,1)}, u32[]{:S(2)}, u32[]{:S(2)}) collective-permute-start(bf16[4,96,768]{2,1,0:T(8,128)(2,1)S(1)} %pad_maximum_fusion.6.own_ref), channel_id=1, source_target_pairs={{0,8},{2,10},{4,12},{6,14},{8,0},{10,2},{12,4},{14,6},{16,24},{18,... | collective-permute-start | bytes 1769480 | tf_op jit(solution)/shard_map/ppermute | solution.py:767
  319.4 13.5 %collective-permute-start.78 = (bf16[4,192,768]{2,1,0:T(8,128)(2,1)S(1)}, bf16[4,192,768]{2,1,0:T(8,128)(2,1)}, u32[]{:S(2)}, u32[]{:S(2)}) collective-permute-start(bf16[4,192,768]{2,1,0:T(8,128)(2,1)S(1)} %collective-permute-done.70.own_ref), channel_id=1, source_target_pairs={{0,1},{1,0},{2,3},{3,2},{4,5},{5,4},{6,7},{7,6},{8,9},{9,8},{10,11... | collective-permute-start | bytes 3538952 | tf_op jit(solution)/shard_map/ppermute | solution.py:762
  324.6 17.3 %collective-permute-start.76 = (bf16[4,48,3072]{2,1,0:T(8,128)(2,1)S(1)}, bf16[4,48,3072]{2,1,0:T(8,128)(2,1)S(1)}, u32[]{:S(2)}, u32[]{:S(2)}) collective-permute-start(bf16[4,48,3072]{2,1,0:T(8,128)(2,1)S(1)} %collective-permute-done.68.own_ref), channel_id=1, source_target_pairs={{0,1},{1,0},{2,3},{3,2},{4,5},{5,4},{6,7},{7,6},{8,9},{9,8},{10,11... | collective-permute-start | bytes 3538952 | tf_op jit(solution)/shard_map/ppermute | solution.py:762
  325.1 12.6 %collective-permute-start.77 = (bf16[4,96,768]{2,1,0:T(8,128)(2,1)}, bf16[4,96,768]{2,1,0:T(8,128)(2,1)}, u32[]{:S(2)}, u32[]{:S(2)}) collective-permute-start(bf16[4,96,768]{2,1,0:T(8,128)(2,1)} %collective-permute-done.69.own_ref), channel_id=1, source_target_pairs={{0,1},{1,0},{2,3},{3,2},{4,5},{5,4},{6,7},{7,6},{8,9},{9,8},{10,11... | collective-permute-start | bytes 1769480 | tf_op jit(solution)/shard_map/ppermute | solution.py:762
  326.4 18.7 %collective-permute-start.63 = (bf16[104,768]{1,0:T(8,128)(2,1)S(1)}, bf16[104,768]{1,0:T(8,128)(2,1)S(1)}, u32[]{:S(2)}, u32[]{:S(2)}) collective-permute-start(bf16[104,768]{1,0:T(8,128)(2,1)S(1)} %copy-done.64), channel_id=1, source_target_pairs={{0,1},{1,0},{2,3},{3,2},{4,5},{5,4},{6,7},{7,6},{8,9},{9,8},{10,11... | collective-permute-start | bytes 479240 | tf_op jit(solution)/shard_map/ppermute | solution.py:762
  (100 other events, 1036.2 us)

commit v2 on v1

--- a/solution.py
+++ b/solution.py
@@ -292,7 +292,7 @@
         compiler_params=pltpu.CompilerParams(vmem_limit_bytes=16 * MIB),
         cost_estimate=BRIEF,
         name="row_values",
-    )(x, gain, w_value)
+    )(x, gain, in_hbm(w_value))
 
 
 def values_back_kernel(probs_ref, d_ref, slope_ref, w_ref, pre_ref, near_ref, far_ref):
@@ -343,7 +343,7 @@
         compiler_params=pltpu.CompilerParams(vmem_limit_bytes=16 * MIB),
         cost_estimate=BRIEF,
         name="values_back",
-    )(in_hbm(probs), d_attended, in_hbm(slope), w_value)
+    )(in_hbm(probs), d_attended, in_hbm(slope), in_hbm(w_value))
 
 
 def attend_kernel(

time: 352 us -> 351 us (level)
    unnamed x182 -> x178, local copies, waits for them, and re-layouts: 7.64 us -> 4.59 us
  transfers between devices with their start and end apart: 80 -> 80, of which waited for: 26 -> 26; matrix products, arithmetic and copies ran while one was open for 8% -> 8% of each run, Pallas kernels for 26% -> 27%
where the time goes in v2:
time: 351 us; the launch traced here: 347 us
  Pallas kernels  125 us (36%)
  waiting for transfers between devices  95.7 us (27%)
  starting transfers between devices  86 us (25%)
  other arithmetic  23.2 us (7%)
  local copies, waits for them, and re-layouts  12.6 us (4%)
    ppermute x32, waiting for transfers between devices, across(): lax.ppermute(part, ('g', 's'), [(i, i ^ 1 << bit) for i in range(chips)])  62.6 us
    ppermute x32, starting transfers between devices, across(): lax.ppermute(part, ('g', 's'), [(i, i ^ 1 << bit) for i in range(chips)])  47.1 us
    ppermute x15, waiting for transfers between devices, nearby(): return lax.ppermute(part, 's', [(i, i ^ k) for i in range(around)])  29.9 us
    pallas_call x8, Pallas kernels, put_in_place(): pl.pallas_call(functools.partial(place_kernel, halved, lead), out_shape=s...  27.7 us
    pallas_call x8, Pallas kernels, grad_half(): pl.pallas_call(functools.partial(half_kernel, halved), out_shape=(jax.Sha...  26.6 us
    ppermute x15, starting transfers between devices, nearby(): return lax.ppermute(part, 's', [(i, i ^ k) for i in range(around)])  17.8 us
    pallas_call x1, Pallas kernels, row_values(): pl.pallas_call(values_kernel, grid=(segs // 2,), out_shape=(pltpu.HBM((co...  12.4 us
    pallas_call x1, Pallas kernels, values_back(): pl.pallas_call(values_back_kernel, grid=(every // rows,), out_shape=(jax....  12.1 us
  transfers between devices with their start and end apart: 80, of which 26 were waited for; matrix products, arithmetic and copies ran while one was open for 8% of the time, Pallas kernels for 27%

profile of v2, /device:TPU:0, one launch (start us, length us, event | category | flops | bytes accessed | tf_op | source)
XLA Modules:
  0.0 347.2 jit_solution(673000480640869459)
XLA Ops:
  2.4 3.1 collective-permute-start.2
  5.5 3.4 collective-permute-start
  12.2 1.5 multiply_multiply_fusion
  15.0 2.7 ema_first.1
  17.7 1.6 collective-permute-start.3
  19.2 1.5 collective-permute-start.4
  21.2 1.6 collective-permute-done.3
  22.9 2.4 collective-permute-done.4
  27.3 1.6 collective-permute-start.16
  33.3 5.1 %ema_second.1 = (f32[2,128,768]{2,1,0:T(8,128)S(1)}, bf16[2,128,768]{2,1,0:T(8,128)(2,1)S(1)}, f32[2,16,768]{2,1,0:T(8,128)S(1)}) custom-call(s32[2]{0:T(128)S(1)} %get-tuple-element.305.place_ref, s32[16]{0:T(128)S(1)} %fusion.18.slot_ref, f32[16]{0:T(128)S(1)} %get-tuple-element.296.pass_ref, f32[2,128]{1,0:T(2,128)S(1)} %subtract_bitcast_fusion.1.keep_ref, ...), custom_call_target="tpu_custom_call" | custom-call | flops 1 | bytes 1 | tf_op jit(solution)/shard_map/ema_second/pallas_call | solution.py:145
  42.4 5.5 %collective-permute-done.13 = bf16[2,128,768]{2,1,0:T(8,128)(2,1)S(1)} collective-permute-done((bf16[2,128,768]{2,1,0:T(8,128)(2,1)S(1)}, bf16[2,128,768]{2,1,0:T(8,128)(2,1)S(1)}, u32[]{:S(2)}, u32[]{:S(2)}) %collective-permute-start.13) | collective-permute-done | bytes 393248 | tf_op jit(solution)/shard_map/ppermute | solution.py:914
  48.1 4.6 %collective-permute-start.14 = (bf16[8,128,768]{2,1,0:T(8,128)(2,1)S(1)}, bf16[8,128,768]{2,1,0:T(8,128)(2,1)S(1)}, u32[]{:S(2)}, u32[]{:S(2)}) collective-permute-start(bf16[8,128,768]{2,1,0:T(8,128)(2,1)S(1)} %pad_maximum_fusion), channel_id=1, source_target_pairs={{0,1},{1,0},{2,3},{3,2},{4,5},{5,4},{6,7},{7,6},{8,9},{9,8},{10,11... | collective-permute-start | bytes 4718600 | tf_op jit(solution)/shard_map/ppermute | solution.py:762
  56.4 12.4 %row_values.1 = (bf16[2048,768]{1,0:T(8,128)(2,1)}, bf16[2048,1536]{1,0:T(8,128)(2,1)S(1)}, bf16[2048,1536]{1,0:T(8,128)(2,1)}) custom-call(bf16[16,128,768]{2,1,0:T(8,128)(2,1)S(1)} %constant_dynamic-update-slice_fusion.16.x_ref, f32[1,768]{1,0:T(1,128)S(1)} %broadcast_in_dim.48.gain_ref, bf16[768,1536]{1,0:T(8,128)(2,1)} %w_ref.4), custom_call_target="tpu_custom_call" | custom-call | flops 1 | bytes 1 | tf_op jit(solution)/shard_map/row_values/pallas_call | solution.py:278
  68.9 7.2 %attend.1 = (f32[256,2048]{1,0:T(8,128)}, bf16[256,2048]{1,0:T(8,128)(2,1)}, f32[256,1]{1,0:T(8,128)S(1)}, f32[256,1536]{1,0:T(8,128)S(1)}, bf16[256,1536]{1,0:T(8,128)(2,1)S(1)}) custom-call(s32[256,1]{1,0:T(8,128)S(1)} %copy.44.at_ref, s32[256,1]{1,0:T(8,128)S(1)} %copy.45.doc_ref, s32[1,2048]{1,0:T(1,128)S(1)} %bitcast.99, s32[1,2048]{1,0:T(1,128)S(1)} %bitcast.100, ...), custom_call_target="tpu_custom_call" | custom-call | flops 1 | bytes 1 | tf_op jit(solution)/shard_map/attend/pallas_call | solution.py:397
  76.1 5.9 %middle.1 = (bf16[256,768]{1,0:T(8,128)(2,1)S(1)}, bf16[256,768]{1,0:T(8,128)(2,1)S(1)}, bf16[256,1536]{1,0:T(8,128)(2,1)S(1)}, bf16[256,1536]{1,0:T(8,128)(2,1)...) custom-call(bf16[256,1536]{1,0:T(8,128)(2,1)S(1)} %get-tuple-element, ...), custom_call_target="tpu_custom_call" | custom-call | flops 1 | bytes 1 | tf_op jit(solution)/shard_map/middle/pallas_call | solution.py:497
  84.4 3.7 %grad_half.8 = (bf16[4,192,768]{2,1,0:T(8,128)(2,1)S(1)}, bf16[4,192,768]{2,1,0:T(8,128)(2,1)}) custom-call(s32[1]{0:T(128)S(6)} %sub.95.half_ref, s32[8]{0:T(128)S(1)} %copy-done.56, bf16[256,1536]{1,0:T(8,128)(2,1)S(1)} %get-tuple-element.160.gated_ref.refs_0_, bf16[256,768]{1,0:T(8,128)(2,1)S(1)} %slice.241.refs_1_, ...), custom_call_target="tpu_custom_call" | custom-call | flops 1 | bytes 1 | tf_op jit(solution)/shard_map/grad_half/pallas_call | solution.py:688
  91.4 4.0 %grad_half.9 = (bf16[4,48,3072]{2,1,0:T(8,128)(2,1)S(1)}, bf16[4,48,3072]{2,1,0:T(8,128)(2,1)S(1)}) custom-call(s32[1]{0:T(128)S(6)} %sub.95.half_ref, s32[8]{0:T(128)S(1)} %copy-done.53, bf16[256,768]{1,0:T(8,128)(2,1)S(1)} %bitcast.93, bf16[256,3072]{1,0:T(8,128)(2,1)S(1)} %get-tuple-element.167.refs_1_.d_tail_ref), custom_call_target="tpu_custom_call" | custom-call | flops 1 | bytes 1 | tf_op jit(solution)/shard_map/grad_half/pallas_call | solution.py:688
  96.2 9.8 %scores_back.1 = (bf16[1024,128]{1,0:T(8,128)(2,1)S(1)}, bf16[1024,128]{1,0:T(8,128)(2,1)S(1)}, f32[256,128]{1,0:T(8,128)S(1)}) custom-call(f32[256,2048]{1,0:T(8,128)} %get-tuple-element.164.weight_ref, f32[256,1]{1,0:T(8,128)S(1)} %copy-done.42, f32[256,1]{1,0:T(8,128)S(1)} %copy-done.44, bf16[256,1536]{1,0:T(8,128)(2,1)S(1)} %copy-done.8, ...), custom_call_target="tpu_custom_call" | custom-call | flops 1 | bytes 1 | tf_op jit(solution)/shard_map/scores_back/pallas_call | solution.py:543
  106.1 2.7 grad_half.10
  110.3 1.6 add_convert_fusion.4
  112.8 3.7 %grad_half.11 = (bf16[4,48,3072]{2,1,0:T(8,128)(2,1)S(1)}, bf16[4,48,3072]{2,1,0:T(8,128)(2,1)S(1)}) custom-call(s32[1]{0:T(128)} %bitcast.30.half_ref.core_ref, s32[8]{0:T(128)S(1)} %copy-done.54, bf16[256,768]{1,0:T(8,128)(2,1)S(1)} %bitcast.94, bf16[256,3072]{1,0:T(8,128)(2,1)S(1)} %get-tuple-element.167.refs_1_.d_tail_ref), custom_call_target="tpu_custom_call" | custom-call | flops 1 | bytes 1 | tf_op jit(solution)/shard_map/grad_half/pallas_call | solution.py:688
  119.1 1.6 grad_half.12
  121.8 1.6 collective-permute-done.19
  123.4 2.0 grad_half.13
  128.2 12.1 %values_back.1 = (bf16[2048,1536]{1,0:T(8,128)(2,1)S(1)}, bf16[1024,768]{1,0:T(8,128)(2,1)S(1)}, bf16[1024,768]{1,0:T(8,128)(2,1)S(1)}) custom-call(bf16[256,2048]{1,0:T(8,128)(2,1)} %get-tuple-element.194.probs_ref, bf16[256,1536]{1,0:T(8,128)(2,1)S(1)} %copy-done.8, bf16[2048,1536]{1,0:T(8,128)(2,1)} %get-tuple-element.195.slope_ref, bf16[768,1536]{1,0:T(8,128)(2,1)} %w_ref.4), custom_call_target="tpu_custom_call" | custom-call | flops 1 | bytes 1 | tf_op jit(solution)/shard_map/values_back/pallas_call | solution.py:324
  140.4 4.9 %ema_third.1 = (bf16[256,128]{1,0:T(8,128)(2,1)}, bf16[128,768]{1,0:T(8,128)(2,1)S(1)}, f32[2,128,768]{2,1,0:T(8,128)S(1)}, f32[2,16,768]{2,1,0:T(8,128)S(1)}, f...) custom-call(f32[2,128]{1,0:T(2,128)S(1)} %subtract_bitcast_fusion.next_ref, f32[256,128]{1,0:T(8,128)S(1)} %get-tuple-element.175.dq_ref, ...), custom_call_target="tpu_custom_call" | custom-call | flops 1 | bytes 1 | tf_op jit(solution)/shard_map/ema_third/pallas_call | solution.py:622
  146.5 4.5 %grad_half.14 = (bf16[4,96,768]{2,1,0:T(8,128)(2,1)S(1)}, bf16[4,96,768]{2,1,0:T(8,128)(2,1)S(1)}) custom-call(s32[1]{0:T(128)S(6)} %sub.95.half_ref, s32[8]{0:T(128)S(1)} %iota_xor_fusion.slot_ref, bf16[2048,768]{1,0:T(8,128)(2,1)S(1)} %copy-done.1, bf16[2048,1536]{1,0:T(8,128)(2,1)S(1)} %get-tuple-element.209.refs_1_), custom_call_target="tpu_custom_call" | custom-call | flops 1 | bytes 1 | tf_op jit(solution)/shard_map/grad_half/pallas_call | solution.py:688
  152.0 1.8 collective-permute-start.26
  155.0 4.5 %grad_half.15 = (bf16[4,96,768]{2,1,0:T(8,128)(2,1)S(1)}, bf16[4,96,768]{2,1,0:T(8,128)(2,1)S(1)}) custom-call(s32[1]{0:T(128)} %bitcast.30.half_ref.core_ref, s32[8]{0:T(128)S(1)} %iota_xor_fusion.slot_ref, bf16[2048,768]{1,0:T(8,128)(2,1)S(1)} %copy-done.1, bf16[2048,1536]{1,0:T(8,128)(2,1)S(1)} %get-tuple-element.209.refs_1_), custom_call_target="tpu_custom_call" | custom-call | flops 1 | bytes 1 | tf_op jit(solution)/shard_map/grad_half/pallas_call | solution.py:688
  163.0 10.3 %ema_fourth.1 = (f32[2,128,768]{2,1,0:T(8,128)S(1)}, bf16[64,768]{1,0:T(8,128)(2,1)S(1)}) custom-call(s32[2]{0:T(128)S(1)} %get-tuple-element.305.place_ref, s32[16]{0:T(128)S(1)} %copy-done.48, f32[16]{0:T(128)S(1)} %copy-done.55, f32[2,128]{1,0:T(2,128)S(1)} %subtract_bitcast_fusion.1.keep_ref, f32[2,128]{1,0:T(2,128)S(1)} %subtract_bitcast_fusion.next_ref, ...), custom_call_target="tpu_custom_call" | custom-call | flops 1 | bytes 1 | tf_op jit(solution)/shard_map/ema_fourth/pallas_call | solution.py:240
  175.4 6.7 %collective-permute-done.36 = bf16[4,96,768]{2,1,0:T(8,128)(2,1)S(1)} collective-permute-done((bf16[4,96,768]{2,1,0:T(8,128)(2,1)S(1)}, bf16[4,96,768]{2,1,0:T(8,128)(2,1)S(1)}, u32[]{:S(2)}, u32[]{:S(2)}) %collective-permute-start.36) | collective-permute-done | bytes 589856 | tf_op jit(solution)/shard_map/ppermute | solution.py:767
  183.6 9.9 %collective-permute-done.44 = bf16[2,48,3072]{2,1,0:T(8,128)(2,1)S(1)} collective-permute-done((bf16[2,48,3072]{2,1,0:T(8,128)(2,1)S(1)}, bf16[2,48,3072]{2,1,0:T(8,128)(2,1)S(1)}, u32[]{:S(2)}, u32[]{:S(2)}) %collective-permute-start.44) | collective-permute-done | bytes 589856 | tf_op jit(solution)/shard_map/ppermute | solution.py:767
  196.2 2.1 collective-permute-start.49
  198.3 2.4 collective-permute-start.48
  200.8 2.6 collective-permute-done.42
  203.7 4.0 %collective-permute-start.46 = (bf16[1,192,768]{2,1,0:T(8,128)(2,1)S(1)}, bf16[1,192,768]{2,1,0:T(8,128)(2,1)S(1)}, u32[]{:S(2)}, u32[]{:S(2)}) collective-permute-start(bf16[1,192,768]{2,1,0:T(8,128)(2,1)S(1)} %add_convert_fusion.19), channel_id=1, source_target_pairs={{0,16},{2,18},{4,20},{6,22},{8,24},{10,26},{12,28},{14,30},{16,0},... | collective-permute-start | bytes 884744 | tf_op jit(solution)/shard_map/ppermute | solution.py:767
  207.7 10.4 %collective-permute-done.40 = bf16[512,768]{1,0:T(8,128)(2,1)S(1)} collective-permute-done((bf16[512,768]{1,0:T(8,128)(2,1)S(1)}, bf16[512,768]{1,0:T(8,128)(2,1)S(1)}, u32[]{:S(2)}, u32[]{:S(2)}) %collective-permute-start.40) | collective-permute-done | bytes 786464 | tf_op jit(solution)/shard_map/ppermute | solution.py:914
  219.2 2.6 collective-permute-start.53
  225.9 7.4 %collective-permute-done.45 = bf16[256,768]{1,0:T(8,128)(2,1)S(1)} collective-permute-done((bf16[256,768]{1,0:T(8,128)(2,1)S(1)}, bf16[256,768]{1,0:T(8,128)(2,1)S(1)}, u32[]{:S(2)}, u32[]{:S(2)}) %collective-permute-start.45) | collective-permute-done | bytes 393248 | tf_op jit(solution)/shard_map/ppermute | solution.py:914
  234.3 5.8 %collective-permute-done.54 = bf16[1,192,768]{2,1,0:T(8,128)(2,1)} collective-permute-done((bf16[1,192,768]{2,1,0:T(8,128)(2,1)S(1)}, bf16[1,192,768]{2,1,0:T(8,128)(2,1)}, u32[]{:S(2)}, u32[]{:S(2)}) %collective-permute-start.54) | collective-permute-done | bytes 294944 | tf_op jit(solution)/shard_map/ppermute | solution.py:767
  242.2 2.1 collective-permute-start.57
  247.9 2.9 collective-permute-done.57
  250.9 2.5 collective-permute-done.56
  253.5 2.1 collective-permute-done.55
  256.5 4.9 %collective-permute-done.60 = bf16[104,768]{1,0:T(8,128)(2,1)S(1)} collective-permute-done((bf16[104,768]{1,0:T(8,128)(2,1)S(1)}, bf16[104,768]{1,0:T(8,128)(2,1)S(1)}, u32[]{:S(2)}, u32[]{:S(2)}) %collective-permute-start.60) | collective-permute-done | bytes 159776 | tf_op jit(solution)/shard_map/ppermute | solution.py:767
  262.2 3.8 %collective-permute-start.66 = (bf16[2,192,768]{2,1,0:T(8,128)(2,1)S(1)}, bf16[2,192,768]{2,1,0:T(8,128)(2,1)S(1)}, u32[]{:S(2)}, u32[]{:S(2)}) collective-permute-start(bf16[2,192,768]{2,1,0:T(8,128)(2,1)S(1)} %pad_maximum_fusion.3), channel_id=1, source_target_pairs={{0,4},{2,6},{4,0},{6,2},{8,12},{10,14},{12,8},{14,10},{16,20},{18,... | collective-permute-start | bytes 1769480 | tf_op jit(solution)/shard_map/ppermute | solution.py:767
  265.9 1.9 collective-permute-done.61
  267.9 10.7 %collective-permute-start.62 = (bf16[104,768]{1,0:T(8,128)(2,1)S(1)}, bf16[104,768]{1,0:T(8,128)(2,1)S(1)}, u32[]{:S(2)}, u32[]{:S(2)}) collective-permute-start(bf16[104,768]{1,0:T(8,128)(2,1)S(1)} %add_convert_fusion.29), channel_id=1, source_target_pairs={{0,16},{2,18},{4,20},{6,22},{8,24},{10,26},{12,28},{14,30},{16,0},... | collective-permute-start | bytes 479240 | tf_op jit(solution)/shard_map/ppermute | solution.py:767
  279.0 1.7 collective-permute-start.65
  280.7 4.2 %collective-permute-done.62 = bf16[104,768]{1,0:T(8,128)(2,1)S(1)} collective-permute-done((bf16[104,768]{1,0:T(8,128)(2,1)S(1)}, bf16[104,768]{1,0:T(8,128)(2,1)S(1)}, u32[]{:S(2)}, u32[]{:S(2)}) %collective-permute-start.62) | collective-permute-done | bytes 159776 | tf_op jit(solution)/shard_map/ppermute | solution.py:767
  285.6 2.9 collective-permute-done.67
  290.4 1.5 collective-permute-start.70
  295.8 1.6 collective-permute-start.71
  298.1 2.5 put_in_place.8.refs_0_
  300.6 3.1 put_in_place.9
  303.7 2.5 put_in_place.10.refs_0_
  306.2 3.2 put_in_place.11.refs_0_
  309.4 2.7 collective-permute-done.71.own_ref
  312.1 6.3 %collective-permute-done.70.own_ref = bf16[4,192,768]{2,1,0:T(8,128)(2,1)S(1)} collective-permute-done((bf16[4,192,768]{2,1,0:T(8,128)(2,1)S(1)}, bf16[4,192,768]{2,1,0:T(8,128)(2,1)S(1)}, u32[]{:S(2)}, u32[]{:S(2)}) %collective-permute-start.70) | collective-permute-done | bytes 1179680 | tf_op jit(solution)/shard_map/ppermute | solution.py:767
  318.4 5.1 %collective-permute-done.69.own_ref = bf16[4,96,768]{2,1,0:T(8,128)(2,1)} collective-permute-done((bf16[4,96,768]{2,1,0:T(8,128)(2,1)S(1)}, bf16[4,96,768]{2,1,0:T(8,128)(2,1)}, u32[]{:S(2)}, u32[]{:S(2)}) %collective-permute-start.69) | collective-permute-done | bytes 589856 | tf_op jit(solution)/shard_map/ppermute | solution.py:767
  327.7 4.3 %put_in_place.12 = f32[2,8,96,768]{3,2,1,0:T(8,128)} custom-call(s32[1]{0:T(128)} %bitcast.30.half_ref.core_ref, s32[4]{0:T(128)S(1)} %get-tuple-element.358.place_ref, bf16[4,96,768]{2,1,0:T(8,128)(2,1)} %collective-permute-done.71.own_ref, bf16[4,96,768]{2,1,0:T(8,128)(2,1)} %collective-permute-done.79.other_ref, ...), custom_call_target="tpu_custom_call", output_to_operand_aliasing={{}: (4, {})} | custom-call | flops 1 | bytes 1 | tf_op jit(solution)/shard_map/put_in_place/pallas_call | solution.py:734
  332.0 4.7 %put_in_place.13 = (f32[2,8,96,768]{3,2,1,0:T(8,128)}, f32[8,96,1536]{2,1,0:T(8,128)}) custom-call(s32[1]{0:T(128)} %bitcast.30.half_ref.core_ref, s32[4]{0:T(128)S(1)} %get-tuple-element.360.place_ref, bf16[4,192,768]{2,1,0:T(8,128)(2,1)S(1)} %collective-permute-done.70.own_ref, ...), custom_call_target="tpu_custom_call", output_to_operand_aliasing={{0}: (4, {}), {1}: (5, {})} | custom-call | flops 1 | bytes 1 | tf_op jit(solution)/shard_map/put_in_place/pallas_call | solution.py:734
  336.7 4.3 %put_in_place.14 = f32[8,96,1536]{2,1,0:T(8,128)} custom-call(s32[1]{0:T(128)} %bitcast.30.half_ref.core_ref, s32[4]{0:T(128)S(1)} %get-tuple-element.362.place_ref, bf16[4,96,768]{2,1,0:T(8,128)(2,1)} %collective-permute-done.69.own_ref, bf16[4,96,768]{2,1,0:T(8,128)(2,1)} %collective-permute-done.77.other_ref, ...), custom_call_target="tpu_custom_call", output_to_operand_aliasing={{}: (4, {})} | custom-call | flops 1 | bytes 1 | tf_op jit(solution)/shard_map/put_in_place/pallas_call | solution.py:734
  340.9 3.2 put_in_place.15
  (430 shorter events, 76.8 us)
Async XLA Ops:
  1.7 13.2 %collective-permute-start.1 = (bf16[1,128,768]{2,1,0:T(8,128)(2,1)S(1)}, bf16[1,128,768]{2,1,0:T(8,128)(2,1)S(1)}, u32[]{:S(2)}, u32[]{:S(2)}) collective-permute-start(bf16[1,128,768]{2,1,0:T(8,128)(2,1)S(1)} %get-tuple-element.332), channel_id=1, source_target_pairs={{0,0},{1,16},{2,2},{3,18},{4,4},{5,20},{6,6},{7,22},{8,8},{9,24},{... | collective-permute-start | bytes 589832 | tf_op jit(solution)/shard_map/ppermute | solution.py:897
  2.4 12.5 %collective-permute-start.2 = (bf16[1,128,768]{2,1,0:T(8,128)(2,1)S(1)}, bf16[1,128,768]{2,1,0:T(8,128)(2,1)S(1)}, u32[]{:S(2)}, u32[]{:S(2)}) collective-permute-start(bf16[1,128,768]{2,1,0:T(8,128)(2,1)S(1)} %get-tuple-element.331), channel_id=1, source_target_pairs={{0,8},{1,24},{2,10},{3,26},{4,12},{5,28},{6,14},{7,30},{8,0},{9,16... | collective-permute-start | bytes 589832 | tf_op jit(solution)/shard_map/ppermute | solution.py:897
  5.5 8.2 %collective-permute-start = (s32[2,8]{1,0:T(2,128)}, s32[2,8]{1,0:T(2,128)S(1)}, u32[]{:S(2)}, u32[]{:S(2)}) collective-permute-start(s32[2,8]{1,0:T(2,128)} %param.20), channel_id=1, source_target_pairs={{0,1},{1,0},{2,3},{3,2},{4,5},{5,4},{6,7},{7,6},{8,9},{9,8},{10,11... | collective-permute-start | bytes 200 | tf_op jit(solution)/shard_map/ppermute | solution.py:944
  19.2 6.1 %collective-permute-start.4 = (f32[2,16,768]{2,1,0:T(8,128)S(1)}, f32[2,16,768]{2,1,0:T(8,128)S(1)}, u32[]{:S(2)}, u32[]{:S(2)}) collective-permute-start(f32[2,16,768]{2,1,0:T(8,128)S(1)} %get-tuple-element.154), channel_id=1, source_target_pairs={{0,4},{2,6},{4,0},{6,2},{1,5},{3,7},{5,1},{7,3},{8,12},{10,14},{12... | collective-permute-start | bytes 294920 | tf_op jit(solution)/shard_map/ppermute | solution.py:914
  26.3 6.9 %collective-permute-start.6 = (f32[8,16,768]{2,1,0:T(8,128)S(1)}, f32[8,16,768]{2,1,0:T(8,128)S(1)}, u32[]{:S(2)}, u32[]{:S(2)}) collective-permute-start(f32[8,16,768]{2,1,0:T(8,128)S(1)} %get-tuple-element.345), channel_id=1, source_target_pairs={{0,1},{1,0},{2,3},{3,2},{4,5},{5,4},{6,7},{7,6},{8,9},{9,8},{10,11... | collective-permute-start | bytes 1179656 | tf_op jit(solution)/shard_map/ppermute | solution.py:762
  29.6 11.5 %collective-permute-start.11 = (bf16[2,128,768]{2,1,0:T(8,128)(2,1)S(1)}, bf16[2,128,768]{2,1,0:T(8,128)(2,1)S(1)}, u32[]{:S(2)}, u32[]{:S(2)}) collective-permute-start(bf16[2,128,768]{2,1,0:T(8,128)(2,1)S(1)} %constant_dynamic-update-slice_fusion.x_ref), channel_id=1, source_target_pairs={{0,2},{2,0},{4,6},{6,4},{1,3},{3,1},{5,7},{7,5},{8,10},{10,8},{12,... | collective-permute-start | bytes 1179656 | tf_op jit(solution)/shard_map/ppermute | solution.py:914
  30.8 11.6 %collective-permute-start.12 = (bf16[2,128,768]{2,1,0:T(8,128)(2,1)S(1)}, bf16[2,128,768]{2,1,0:T(8,128)(2,1)S(1)}, u32[]{:S(2)}, u32[]{:S(2)}) collective-permute-start(bf16[2,128,768]{2,1,0:T(8,128)(2,1)S(1)} %constant_dynamic-update-slice_fusion.x_ref), channel_id=1, source_target_pairs={{0,4},{2,6},{4,0},{6,2},{1,5},{3,7},{5,1},{7,3},{8,12},{10,14},{12... | collective-permute-start | bytes 1179656 | tf_op jit(solution)/shard_map/ppermute | solution.py:914
  31.7 16.2 %collective-permute-start.13 = (bf16[2,128,768]{2,1,0:T(8,128)(2,1)S(1)}, bf16[2,128,768]{2,1,0:T(8,128)(2,1)S(1)}, u32[]{:S(2)}, u32[]{:S(2)}) collective-permute-start(bf16[2,128,768]{2,1,0:T(8,128)(2,1)S(1)} %constant_dynamic-update-slice_fusion.x_ref), channel_id=1, source_target_pairs={{0,6},{2,4},{4,2},{6,0},{1,7},{3,5},{5,3},{7,1},{8,14},{10,12},{12... | collective-permute-start | bytes 1179656 | tf_op jit(solution)/shard_map/ppermute | solution.py:914
  38.9 15.7 %collective-permute-start.7 = (bf16[256,128]{1,0:T(8,128)(2,1)S(1)}, bf16[256,128]{1,0:T(8,128)(2,1)S(1)}, u32[]{:S(2)}, u32[]{:S(2)}) collective-permute-start(bf16[256,128]{1,0:T(8,128)(2,1)S(1)} %get-tuple-element.301), channel_id=1, source_target_pairs={{0,2},{2,0},{4,6},{6,4},{1,3},{3,1},{5,7},{7,5},{8,10},{10,8},{12,... | collective-permute-start | bytes 196616 | tf_op jit(solution)/shard_map/ppermute | solution.py:914
  40.1 14.5 %collective-permute-start.8 = (bf16[256,128]{1,0:T(8,128)(2,1)S(1)}, bf16[256,128]{1,0:T(8,128)(2,1)S(1)}, u32[]{:S(2)}, u32[]{:S(2)}) collective-permute-start(bf16[256,128]{1,0:T(8,128)(2,1)S(1)} %get-tuple-element.301), channel_id=1, source_target_pairs={{0,4},{2,6},{4,0},{6,2},{1,5},{3,7},{5,1},{7,3},{8,12},{10,14},{12... | collective-permute-start | bytes 196616 | tf_op jit(solution)/shard_map/ppermute | solution.py:914
  41.0 13.6 %collective-permute-start.9 = (bf16[256,128]{1,0:T(8,128)(2,1)S(1)}, bf16[256,128]{1,0:T(8,128)(2,1)S(1)}, u32[]{:S(2)}, u32[]{:S(2)}) collective-permute-start(bf16[256,128]{1,0:T(8,128)(2,1)S(1)} %get-tuple-element.301), channel_id=1, source_target_pairs={{0,6},{2,4},{4,2},{6,0},{1,7},{3,5},{5,3},{7,1},{8,14},{10,12},{12... | collective-permute-start | bytes 196616 | tf_op jit(solution)/shard_map/ppermute | solution.py:914
  48.1 8.2 %collective-permute-start.14 = (bf16[8,128,768]{2,1,0:T(8,128)(2,1)S(1)}, bf16[8,128,768]{2,1,0:T(8,128)(2,1)S(1)}, u32[]{:S(2)}, u32[]{:S(2)}) collective-permute-start(bf16[8,128,768]{2,1,0:T(8,128)(2,1)S(1)} %pad_maximum_fusion), channel_id=1, source_target_pairs={{0,1},{1,0},{2,3},{3,2},{4,5},{5,4},{6,7},{7,6},{8,9},{9,8},{10,11... | collective-permute-start | bytes 4718600 | tf_op jit(solution)/shard_map/ppermute | solution.py:762
  89.2 21.1 %collective-permute-start.18 = (bf16[4,192,768]{2,1,0:T(8,128)(2,1)}, bf16[4,192,768]{2,1,0:T(8,128)(2,1)}, u32[]{:S(2)}, u32[]{:S(2)}) collective-permute-start(bf16[4,192,768]{2,1,0:T(8,128)(2,1)} %get-tuple-element.170), channel_id=1, source_target_pairs={{0,1},{1,0},{2,3},{3,2},{4,5},{5,4},{6,7},{7,6},{8,9},{9,8},{10,11... | collective-permute-start | bytes 3538952 | tf_op jit(solution)/shard_map/ppermute | solution.py:762
  95.4 21.1 %collective-permute-start.20 = (bf16[4,48,3072]{2,1,0:T(8,128)(2,1)S(1)}, bf16[4,48,3072]{2,1,0:T(8,128)(2,1)S(1)}, u32[]{:S(2)}, u32[]{:S(2)}) collective-permute-start(bf16[4,48,3072]{2,1,0:T(8,128)(2,1)S(1)} %get-tuple-element.172), channel_id=1, source_target_pairs={{0,1},{1,0},{2,3},{3,2},{4,5},{5,4},{6,7},{7,6},{8,9},{9,8},{10,11... | collective-permute-start | bytes 3538952 | tf_op jit(solution)/shard_map/ppermute | solution.py:762
  109.2 12.1 %collective-permute-start.29 = (bf16[4,192,768]{2,1,0:T(8,128)(2,1)S(1)}, bf16[4,192,768]{2,1,0:T(8,128)(2,1)S(1)}, u32[]{:S(2)}, u32[]{:S(2)}) collective-permute-start(bf16[4,192,768]{2,1,0:T(8,128)(2,1)S(1)} %copy-done.61), channel_id=1, source_target_pairs={{0,1},{1,0},{2,3},{3,2},{4,5},{5,4},{6,7},{7,6},{8,9},{9,8},{10,11... | collective-permute-start | bytes 3538952 | tf_op jit(solution)/shard_map/ppermute | solution.py:762
  109.4 11.3 %collective-permute-start.38 = (bf16[4,48,3072]{2,1,0:T(8,128)(2,1)S(1)}, bf16[4,48,3072]{2,1,0:T(8,128)(2,1)S(1)}, u32[]{:S(2)}, u32[]{:S(2)}) collective-permute-start(bf16[4,48,3072]{2,1,0:T(8,128)(2,1)S(1)} %get-tuple-element.230), channel_id=1, source_target_pairs={{0,1},{1,0},{2,3},{3,2},{4,5},{5,4},{6,7},{7,6},{8,9},{9,8},{10,11... | collective-permute-start | bytes 3538952 | tf_op jit(solution)/shard_map/ppermute | solution.py:762
  112.0 48.7 %collective-permute-start.30 = (bf16[4,192,768]{2,1,0:T(8,128)(2,1)S(1)}, bf16[4,192,768]{2,1,0:T(8,128)(2,1)S(1)}, u32[]{:S(2)}, u32[]{:S(2)}) collective-permute-start(bf16[4,192,768]{2,1,0:T(8,128)(2,1)S(1)} %add_convert_fusion.4), channel_id=1, source_target_pairs={{0,8},{2,10},{4,12},{6,14},{8,0},{10,2},{12,4},{14,6},{16,24},{18,... | collective-permute-start | bytes 3538952 | tf_op jit(solution)/shard_map/ppermute | solution.py:767
  116.9 56.4 %collective-permute-start.39 = (bf16[4,48,3072]{2,1,0:T(8,128)(2,1)S(1)}, bf16[4,48,3072]{2,1,0:T(8,128)(2,1)S(1)}, u32[]{:S(2)}, u32[]{:S(2)}) collective-permute-start(bf16[4,48,3072]{2,1,0:T(8,128)(2,1)S(1)} %add_convert_fusion.3), channel_id=1, source_target_pairs={{0,8},{2,10},{4,12},{6,14},{8,0},{10,2},{12,4},{14,6},{16,24},{18,... | collective-permute-start | bytes 3538952 | tf_op jit(solution)/shard_map/ppermute | solution.py:767
  120.7 6.1 %collective-permute-start.22 = (bf16[4,96,768]{2,1,0:T(8,128)(2,1)S(1)}, bf16[4,96,768]{2,1,0:T(8,128)(2,1)S(1)}, u32[]{:S(2)}, u32[]{:S(2)}) collective-permute-start(bf16[4,96,768]{2,1,0:T(8,128)(2,1)S(1)} %get-tuple-element.188), channel_id=1, source_target_pairs={{0,1},{1,0},{2,3},{3,2},{4,5},{5,4},{6,7},{7,6},{8,9},{9,8},{10,11... | collective-permute-start | bytes 1769480 | tf_op jit(solution)/shard_map/ppermute | solution.py:762
  121.2 29.8 %collective-permute-start.24 = (bf16[4,96,768]{2,1,0:T(8,128)(2,1)S(1)}, bf16[4,96,768]{2,1,0:T(8,128)(2,1)S(1)}, u32[]{:S(2)}, u32[]{:S(2)}) collective-permute-start(bf16[4,96,768]{2,1,0:T(8,128)(2,1)S(1)} %get-tuple-element.202), channel_id=1, source_target_pairs={{0,1},{1,0},{2,3},{3,2},{4,5},{5,4},{6,7},{7,6},{8,9},{9,8},{10,11... | collective-permute-start | bytes 1769480 | tf_op jit(solution)/shard_map/ppermute | solution.py:762
  125.4 14.9 %collective-permute-start.21 = (bf16[256,128]{1,0:T(8,128)(2,1)S(1)}, bf16[256,128]{1,0:T(8,128)(2,1)S(1)}, u32[]{:S(2)}, u32[]{:S(2)}) collective-permute-start(bf16[256,128]{1,0:T(8,128)(2,1)S(1)} %get-tuple-element.337), channel_id=1, source_target_pairs={{0,2},{2,0},{4,6},{6,4},{1,3},{3,1},{5,7},{7,5},{8,10},{10,8},{12,... | collective-permute-start | bytes 196616 | tf_op jit(solution)/shard_map/ppermute | solution.py:914
  126.9 24.3 %collective-permute-start.25 = (bf16[4,96,768]{2,1,0:T(8,128)(2,1)S(1)}, bf16[4,96,768]{2,1,0:T(8,128)(2,1)S(1)}, u32[]{:S(2)}, u32[]{:S(2)}) collective-permute-start(bf16[4,96,768]{2,1,0:T(8,128)(2,1)S(1)} %add_convert_fusion.13), channel_id=1, source_target_pairs={{0,2},{2,0},{4,6},{6,4},{8,10},{10,8},{12,14},{14,12},{16,18},{18,... | collective-permute-start | bytes 1769480 | tf_op jit(solution)/shard_map/ppermute | solution.py:767
  145.3 6.7 %collective-permute-start.23 = (f32[2,16,768]{2,1,0:T(8,128)S(1)}, f32[2,16,768]{2,1,0:T(8,128)S(1)}, u32[]{:S(2)}, u32[]{:S(2)}) collective-permute-start(f32[2,16,768]{2,1,0:T(8,128)S(1)} %get-tuple-element.200), channel_id=1, source_target_pairs={{0,2},{2,0},{4,6},{6,4},{1,3},{3,1},{5,7},{7,5},{8,10},{10,8},{12,... | collective-permute-start | bytes 294920 | tf_op jit(solution)/shard_map/ppermute | solution.py:914
  151.0 10.1 %collective-permute-start.28 = (bf16[4,96,768]{2,1,0:T(8,128)(2,1)S(1)}, bf16[4,96,768]{2,1,0:T(8,128)(2,1)S(1)}, u32[]{:S(2)}, u32[]{:S(2)}) collective-permute-start(bf16[4,96,768]{2,1,0:T(8,128)(2,1)S(1)} %get-tuple-element.206), channel_id=1, source_target_pairs={{0,1},{1,0},{2,3},{3,2},{4,5},{5,4},{6,7},{7,6},{8,9},{9,8},{10,11... | collective-permute-start | bytes 1769480 | tf_op jit(solution)/shard_map/ppermute | solution.py:762
  151.3 10.2 %collective-permute-start.35 = (bf16[4,96,768]{2,1,0:T(8,128)(2,1)S(1)}, bf16[4,96,768]{2,1,0:T(8,128)(2,1)S(1)}, u32[]{:S(2)}, u32[]{:S(2)}) collective-permute-start(bf16[4,96,768]{2,1,0:T(8,128)(2,1)S(1)} %get-tuple-element.227), channel_id=1, source_target_pairs={{0,1},{1,0},{2,3},{3,2},{4,5},{5,4},{6,7},{7,6},{8,9},{9,8},{10,11... | collective-permute-start | bytes 1769480 | tf_op jit(solution)/shard_map/ppermute | solution.py:762
  152.0 7.5 %collective-permute-start.26 = (f32[4,16,768]{2,1,0:T(8,128)S(1)}, f32[4,16,768]{2,1,0:T(8,128)S(1)}, u32[]{:S(2)}, u32[]{:S(2)}) collective-permute-start(f32[4,16,768]{2,1,0:T(8,128)S(1)} %get-tuple-element.341), channel_id=1, source_target_pairs={{0,4},{2,6},{4,0},{6,2},{1,5},{3,7},{5,1},{7,3},{8,12},{10,14},{12... | collective-permute-start | bytes 589832 | tf_op jit(solution)/shard_map/ppermute | solution.py:914
  159.5 15.3 %collective-permute-start.37 = (bf16[2,96,768]{2,1,0:T(8,128)(2,1)S(1)}, bf16[2,96,768]{2,1,0:T(8,128)(2,1)S(1)}, u32[]{:S(2)}, u32[]{:S(2)}) collective-permute-start(bf16[2,96,768]{2,1,0:T(8,128)(2,1)S(1)} %get-tuple-element.313), channel_id=1, source_target_pairs={{0,4},{2,6},{4,0},{6,2},{8,12},{10,14},{12,8},{14,10},{16,20},{18,... | collective-permute-start | bytes 884744 | tf_op jit(solution)/shard_map/ppermute | solution.py:767
  161.1 22.0 %collective-permute-start.34 = (bf16[2,192,768]{2,1,0:T(8,128)(2,1)S(1)}, bf16[2,192,768]{2,1,0:T(8,128)(2,1)S(1)}, u32[]{:S(2)}, u32[]{:S(2)}) collective-permute-start(bf16[2,192,768]{2,1,0:T(8,128)(2,1)S(1)} %get-tuple-element.309), channel_id=1, source_target_pairs={{0,2},{2,0},{4,6},{6,4},{8,10},{10,8},{12,14},{14,12},{16,18},{18,... | collective-permute-start | bytes 1769480 | tf_op jit(solution)/shard_map/ppermute | solution.py:767
  161.4 20.7 %collective-permute-start.36 = (bf16[4,96,768]{2,1,0:T(8,128)(2,1)S(1)}, bf16[4,96,768]{2,1,0:T(8,128)(2,1)S(1)}, u32[]{:S(2)}, u32[]{:S(2)}) collective-permute-start(bf16[4,96,768]{2,1,0:T(8,128)(2,1)S(1)} %add_convert_fusion.10), channel_id=1, source_target_pairs={{0,4},{2,6},{4,0},{6,2},{8,12},{10,14},{12,8},{14,10},{16,20},{18,... | collective-permute-start | bytes 1769480 | tf_op jit(solution)/shard_map/ppermute | solution.py:767
  162.7 30.8 %collective-permute-start.33 = (bf16[1024,768]{1,0:T(8,128)(2,1)S(1)}, bf16[1024,768]{1,0:T(8,128)(2,1)S(1)}, u32[]{:S(2)}, u32[]{:S(2)}) collective-permute-start(bf16[1024,768]{1,0:T(8,128)(2,1)S(1)} %get-tuple-element.224), channel_id=1, source_target_pairs={{0,1},{1,0},{2,3},{3,2},{4,5},{5,4},{6,7},{7,6},{8,9},{9,8},{10,11... | collective-permute-start | bytes 4718600 | tf_op jit(solution)/shard_map/ppermute | solution.py:762
  173.8 19.7 %collective-permute-start.44 = (bf16[2,48,3072]{2,1,0:T(8,128)(2,1)S(1)}, bf16[2,48,3072]{2,1,0:T(8,128)(2,1)S(1)}, u32[]{:S(2)}, u32[]{:S(2)}) collective-permute-start(bf16[2,48,3072]{2,1,0:T(8,128)(2,1)S(1)} %get-tuple-element.307), channel_id=1, source_target_pairs={{0,4},{2,6},{4,0},{6,2},{8,12},{10,14},{12,8},{14,10},{16,20},{18,... | collective-permute-start | bytes 1769480 | tf_op jit(solution)/shard_map/ppermute | solution.py:767
  174.9 23.4 %collective-permute-start.43 = (bf16[1,96,768]{2,1,0:T(8,128)(2,1)S(1)}, bf16[1,96,768]{2,1,0:T(8,128)(2,1)S(1)}, u32[]{:S(2)}, u32[]{:S(2)}) collective-permute-start(bf16[1,96,768]{2,1,0:T(8,128)(2,1)S(1)} %add_convert_fusion.40), channel_id=1, source_target_pairs={{0,8},{2,10},{4,12},{6,14},{8,0},{10,2},{12,4},{14,6},{16,24},{18,... | collective-permute-start | bytes 442376 | tf_op jit(solution)/shard_map/ppermute | solution.py:767
  182.1 12.8 %collective-permute-start.31 = (bf16[1,128,768]{2,1,0:T(8,128)(2,1)S(1)}, bf16[1,128,768]{2,1,0:T(8,128)(2,1)S(1)}, u32[]{:S(2)}, u32[]{:S(2)}) collective-permute-start(bf16[1,128,768]{2,1,0:T(8,128)(2,1)S(1)} %get-tuple-element.327), channel_id=1, source_target_pairs={{0,0},{16,1},{2,2},{18,3},{4,4},{20,5},{6,6},{22,7},{8,8},{24,9},{... | collective-permute-start | bytes 589832 | tf_op jit(solution)/shard_map/ppermute | solution.py:904
  183.1 11.9 %collective-permute-start.32 = (bf16[1,128,768]{2,1,0:T(8,128)(2,1)S(1)}, bf16[1,128,768]{2,1,0:T(8,128)(2,1)S(1)}, u32[]{:S(2)}, u32[]{:S(2)}) collective-permute-start(bf16[1,128,768]{2,1,0:T(8,128)(2,1)S(1)} %get-tuple-element.328), channel_id=1, source_target_pairs={{8,0},{24,1},{10,2},{26,3},{12,4},{28,5},{14,6},{30,7},{0,8},{16,9... | collective-permute-start | bytes 589832 | tf_op jit(solution)/shard_map/ppermute | solution.py:904
  193.5 9.9 %collective-permute-start.42 = (bf16[2,96,768]{2,1,0:T(8,128)(2,1)S(1)}, bf16[2,96,768]{2,1,0:T(8,128)(2,1)S(1)}, u32[]{:S(2)}, u32[]{:S(2)}) collective-permute-start(bf16[2,96,768]{2,1,0:T(8,128)(2,1)S(1)} %get-tuple-element.311), channel_id=1, source_target_pairs={{0,2},{2,0},{4,6},{6,4},{8,10},{10,8},{12,14},{14,12},{16,18},{18,... | collective-permute-start | bytes 884744 | tf_op jit(solution)/shard_map/ppermute | solution.py:767
  193.5 10.0 %collective-permute-start.41 = (bf16[1,192,768]{2,1,0:T(8,128)(2,1)S(1)}, bf16[1,192,768]{2,1,0:T(8,128)(2,1)S(1)}, u32[]{:S(2)}, u32[]{:S(2)}) collective-permute-start(bf16[1,192,768]{2,1,0:T(8,128)(2,1)S(1)} %add_convert_fusion.23), channel_id=1, source_target_pairs={{0,4},{2,6},{4,0},{6,2},{8,12},{10,14},{12,8},{14,10},{16,20},{18,... | collective-permute-start | bytes 884744 | tf_op jit(solution)/shard_map/ppermute | solution.py:767
  195.0 23.1 %collective-permute-start.40 = (bf16[512,768]{1,0:T(8,128)(2,1)S(1)}, bf16[512,768]{1,0:T(8,128)(2,1)S(1)}, u32[]{:S(2)}, u32[]{:S(2)}) collective-permute-start(bf16[512,768]{1,0:T(8,128)(2,1)S(1)} %slice.267), channel_id=1, source_target_pairs={{0,4},{2,6},{4,0},{6,2},{1,5},{3,7},{5,1},{7,3},{8,12},{10,14},{12... | collective-permute-start | bytes 2359304 | tf_op jit(solution)/shard_map/ppermute | solution.py:914
  196.2 22.1 %collective-permute-start.49 = (bf16[1,48,3072]{2,1,0:T(8,128)(2,1)S(1)}, bf16[1,48,3072]{2,1,0:T(8,128)(2,1)S(1)}, u32[]{:S(2)}, u32[]{:S(2)}) collective-permute-start(bf16[1,48,3072]{2,1,0:T(8,128)(2,1)S(1)} %add_convert_fusion.20), channel_id=1, source_target_pairs={{0,2},{2,0},{4,6},{6,4},{8,10},{10,8},{12,14},{14,12},{16,18},{18,... | collective-permute-start | bytes 884744 | tf_op jit(solution)/shard_map/ppermute | solution.py:767
  198.3 23.4 %collective-permute-start.48 = (bf16[1,96,768]{2,1,0:T(8,128)(2,1)S(1)}, bf16[1,96,768]{2,1,0:T(8,128)(2,1)S(1)}, u32[]{:S(2)}, u32[]{:S(2)}) collective-permute-start(bf16[1,96,768]{2,1,0:T(8,128)(2,1)S(1)} %add_convert_fusion.38), channel_id=1, source_target_pairs={{0,16},{2,18},{4,20},{6,22},{8,24},{10,26},{12,28},{14,30},{16,0},... | collective-permute-start | bytes 442376 | tf_op jit(solution)/shard_map/ppermute | solution.py:767
  203.5 19.7 %collective-permute-start.47 = (bf16[1,96,768]{2,1,0:T(8,128)(2,1)S(1)}, bf16[1,96,768]{2,1,0:T(8,128)(2,1)S(1)}, u32[]{:S(2)}, u32[]{:S(2)}) collective-permute-start(bf16[1,96,768]{2,1,0:T(8,128)(2,1)S(1)} %add_convert_fusion.37), channel_id=1, source_target_pairs={{0,8},{2,10},{4,12},{6,14},{8,0},{10,2},{12,4},{14,6},{16,24},{18,... | collective-permute-start | bytes 442376 | tf_op jit(solution)/shard_map/ppermute | solution.py:767
  203.7 20.8 %collective-permute-start.46 = (bf16[1,192,768]{2,1,0:T(8,128)(2,1)S(1)}, bf16[1,192,768]{2,1,0:T(8,128)(2,1)S(1)}, u32[]{:S(2)}, u32[]{:S(2)}) collective-permute-start(bf16[1,192,768]{2,1,0:T(8,128)(2,1)S(1)} %add_convert_fusion.19), channel_id=1, source_target_pairs={{0,16},{2,18},{4,20},{6,22},{8,24},{10,26},{12,28},{14,30},{16,0},... | collective-permute-start | bytes 884744 | tf_op jit(solution)/shard_map/ppermute | solution.py:767
  219.2 21.9 %collective-permute-start.53 = (bf16[1,48,3072]{2,1,0:T(8,128)(2,1)}, bf16[1,48,3072]{2,1,0:T(8,128)(2,1)}, u32[]{:S(2)}, u32[]{:S(2)}) collective-permute-start(bf16[1,48,3072]{2,1,0:T(8,128)(2,1)} %add_convert_fusion.17), channel_id=1, source_target_pairs={{0,16},{2,18},{4,20},{6,22},{8,24},{10,26},{12,28},{14,30},{16,0},... | collective-permute-start | bytes 884744 | tf_op jit(solution)/shard_map/ppermute | solution.py:767
  221.8 22.5 %collective-permute-start.52 = (bf16[1,96,768]{2,1,0:T(8,128)(2,1)S(1)}, bf16[1,96,768]{2,1,0:T(8,128)(2,1)S(1)}, u32[]{:S(2)}, u32[]{:S(2)}) collective-permute-start(bf16[1,96,768]{2,1,0:T(8,128)(2,1)S(1)} %add_convert_fusion.35), channel_id=1, source_target_pairs={{0,2},{2,0},{4,6},{6,4},{8,10},{10,8},{12,14},{14,12},{16,18},{18,... | collective-permute-start | bytes 442376 | tf_op jit(solution)/shard_map/ppermute | solution.py:767
  223.2 10.2 %collective-permute-start.45 = (bf16[256,768]{1,0:T(8,128)(2,1)S(1)}, bf16[256,768]{1,0:T(8,128)(2,1)S(1)}, u32[]{:S(2)}, u32[]{:S(2)}) collective-permute-start(bf16[256,768]{1,0:T(8,128)(2,1)S(1)} %slice.333), channel_id=1, source_target_pairs={{0,2},{2,0},{4,6},{6,4},{1,3},{3,1},{5,7},{7,5},{8,10},{10,8},{12,... | collective-permute-start | bytes 1179656 | tf_op jit(solution)/shard_map/ppermute | solution.py:914
  224.0 20.4 %collective-permute-start.51 = (bf16[1,96,768]{2,1,0:T(8,128)(2,1)S(1)}, bf16[1,96,768]{2,1,0:T(8,128)(2,1)}, u32[]{:S(2)}, u32[]{:S(2)}) collective-permute-start(bf16[1,96,768]{2,1,0:T(8,128)(2,1)S(1)} %add_convert_fusion.34), channel_id=1, source_target_pairs={{0,16},{2,18},{4,20},{6,22},{8,24},{10,26},{12,28},{14,30},{16,0},... | collective-permute-start | bytes 442376 | tf_op jit(solution)/shard_map/ppermute | solution.py:767
  224.6 15.5 %collective-permute-start.54 = (bf16[1,192,768]{2,1,0:T(8,128)(2,1)S(1)}, bf16[1,192,768]{2,1,0:T(8,128)(2,1)}, u32[]{:S(2)}, u32[]{:S(2)}) collective-permute-start(bf16[1,192,768]{2,1,0:T(8,128)(2,1)S(1)} %add_convert_fusion.16), channel_id=1, source_target_pairs={{0,8},{2,10},{4,12},{6,14},{8,0},{10,2},{12,4},{14,6},{16,24},{18,... | collective-permute-start | bytes 884744 | tf_op jit(solution)/shard_map/ppermute | solution.py:767
  242.2 8.6 %collective-permute-start.57 = (bf16[1,48,3072]{2,1,0:T(8,128)(2,1)S(1)}, bf16[1,48,3072]{2,1,0:T(8,128)(2,1)S(1)}, u32[]{:S(2)}, u32[]{:S(2)}) collective-permute-start(bf16[1,48,3072]{2,1,0:T(8,128)(2,1)S(1)} %add_convert_fusion.15), channel_id=1, source_target_pairs={{0,2},{2,0},{4,6},{6,4},{8,10},{10,8},{12,14},{14,12},{16,18},{18,... | collective-permute-start | bytes 884744 | tf_op jit(solution)/shard_map/ppermute | solution.py:767
  245.4 8.0 %collective-permute-start.56 = (bf16[1,96,768]{2,1,0:T(8,128)(2,1)S(1)}, bf16[1,96,768]{2,1,0:T(8,128)(2,1)S(1)}, u32[]{:S(2)}, u32[]{:S(2)}) collective-permute-start(bf16[1,96,768]{2,1,0:T(8,128)(2,1)S(1)} %add_convert_fusion.33), channel_id=1, source_target_pairs={{0,2},{2,0},{4,6},{6,4},{8,10},{10,8},{12,14},{14,12},{16,18},{18,... | collective-permute-start | bytes 442376 | tf_op jit(solution)/shard_map/ppermute | solution.py:767
  246.8 8.8 %collective-permute-start.55 = (bf16[104,768]{1,0:T(8,128)(2,1)S(1)}, bf16[104,768]{1,0:T(8,128)(2,1)S(1)}, u32[]{:S(2)}, u32[]{:S(2)}) collective-permute-start(bf16[104,768]{1,0:T(8,128)(2,1)S(1)} %add_convert_fusion.32), channel_id=1, source_target_pairs={{0,2},{2,0},{4,6},{6,4},{8,10},{10,8},{12,14},{14,12},{16,18},{18,... | collective-permute-start | bytes 479240 | tf_op jit(solution)/shard_map/ppermute | solution.py:767
  262.2 26.4 %collective-permute-start.66 = (bf16[2,192,768]{2,1,0:T(8,128)(2,1)S(1)}, bf16[2,192,768]{2,1,0:T(8,128)(2,1)S(1)}, u32[]{:S(2)}, u32[]{:S(2)}) collective-permute-start(bf16[2,192,768]{2,1,0:T(8,128)(2,1)S(1)} %pad_maximum_fusion.3), channel_id=1, source_target_pairs={{0,4},{2,6},{4,0},{6,2},{8,12},{10,14},{12,8},{14,10},{16,20},{18,... | collective-permute-start | bytes 1769480 | tf_op jit(solution)/shard_map/ppermute | solution.py:767
  267.9 17.0 %collective-permute-start.62 = (bf16[104,768]{1,0:T(8,128)(2,1)S(1)}, bf16[104,768]{1,0:T(8,128)(2,1)S(1)}, u32[]{:S(2)}, u32[]{:S(2)}) collective-permute-start(bf16[104,768]{1,0:T(8,128)(2,1)S(1)} %add_convert_fusion.29), channel_id=1, source_target_pairs={{0,16},{2,18},{4,20},{6,22},{8,24},{10,26},{12,28},{14,30},{16,0},... | collective-permute-start | bytes 479240 | tf_op jit(solution)/shard_map/ppermute | solution.py:767
  278.6 9.9 %collective-permute-start.67 = (bf16[2,96,768]{2,1,0:T(8,128)(2,1)S(1)}, bf16[2,96,768]{2,1,0:T(8,128)(2,1)S(1)}, u32[]{:S(2)}, u32[]{:S(2)}) collective-permute-start(bf16[2,96,768]{2,1,0:T(8,128)(2,1)S(1)} %pad_maximum_fusion.9), channel_id=1, source_target_pairs={{0,4},{2,6},{4,0},{6,2},{8,12},{10,14},{12,8},{14,10},{16,20},{18,... | collective-permute-start | bytes 884744 | tf_op jit(solution)/shard_map/ppermute | solution.py:767
  279.0 13.8 %collective-permute-start.65 = (bf16[2,96,768]{2,1,0:T(8,128)(2,1)S(1)}, bf16[2,96,768]{2,1,0:T(8,128)(2,1)S(1)}, u32[]{:S(2)}, u32[]{:S(2)}) collective-permute-start(bf16[2,96,768]{2,1,0:T(8,128)(2,1)S(1)} %pad_maximum_fusion.10), channel_id=1, source_target_pairs={{0,4},{2,6},{4,0},{6,2},{8,12},{10,14},{12,8},{14,10},{16,20},{18,... | collective-permute-start | bytes 884744 | tf_op jit(solution)/shard_map/ppermute | solution.py:767
  280.7 13.3 %collective-permute-start.64 = (bf16[2,48,3072]{2,1,0:T(8,128)(2,1)S(1)}, bf16[2,48,3072]{2,1,0:T(8,128)(2,1)S(1)}, u32[]{:S(2)}, u32[]{:S(2)}) collective-permute-start(bf16[2,48,3072]{2,1,0:T(8,128)(2,1)S(1)} %pad_maximum_fusion.4), channel_id=1, source_target_pairs={{0,8},{2,10},{4,12},{6,14},{8,0},{10,2},{12,4},{14,6},{16,24},{18,... | collective-permute-start | bytes 1769480 | tf_op jit(solution)/shard_map/ppermute | solution.py:767
  289.7 7.6 %collective-permute-start.74 = (bf16[4,192,768]{2,1,0:T(8,128)(2,1)S(1)}, bf16[4,192,768]{2,1,0:T(8,128)(2,1)S(1)}, u32[]{:S(2)}, u32[]{:S(2)}) collective-permute-start(bf16[4,192,768]{2,1,0:T(8,128)(2,1)S(1)} %pad_maximum_fusion.1.own_ref), channel_id=1, source_target_pairs={{0,1},{1,0},{2,3},{3,2},{4,5},{5,4},{6,7},{7,6},{8,9},{9,8},{10,11... | collective-permute-start | bytes 3538952 | tf_op jit(solution)/shard_map/ppermute | solution.py:762
  290.4 28.0 %collective-permute-start.70 = (bf16[4,192,768]{2,1,0:T(8,128)(2,1)S(1)}, bf16[4,192,768]{2,1,0:T(8,128)(2,1)S(1)}, u32[]{:S(2)}, u32[]{:S(2)}) collective-permute-start(bf16[4,192,768]{2,1,0:T(8,128)(2,1)S(1)} %pad_maximum_fusion.1.own_ref), channel_id=1, source_target_pairs={{0,2},{2,0},{4,6},{6,4},{8,10},{10,8},{12,14},{14,12},{16,18},{18,... | collective-permute-start | bytes 3538952 | tf_op jit(solution)/shard_map/ppermute | solution.py:767
  294.1 12.1 %collective-permute-start.72 = (bf16[4,48,3072]{2,1,0:T(8,128)(2,1)S(1)}, bf16[4,48,3072]{2,1,0:T(8,128)(2,1)S(1)}, u32[]{:S(2)}, u32[]{:S(2)}) collective-permute-start(bf16[4,48,3072]{2,1,0:T(8,128)(2,1)S(1)} %pad_maximum_fusion.2.own_ref), channel_id=1, source_target_pairs={{0,1},{1,0},{2,3},{3,2},{4,5},{5,4},{6,7},{7,6},{8,9},{9,8},{10,11... | collective-permute-start | bytes 3538952 | tf_op jit(solution)/shard_map/ppermute | solution.py:762
  294.2 29.3 %collective-permute-start.68 = (bf16[4,48,3072]{2,1,0:T(8,128)(2,1)S(1)}, bf16[4,48,3072]{2,1,0:T(8,128)(2,1)S(1)}, u32[]{:S(2)}, u32[]{:S(2)}) collective-permute-start(bf16[4,48,3072]{2,1,0:T(8,128)(2,1)S(1)} %pad_maximum_fusion.2.own_ref), channel_id=1, source_target_pairs={{0,4},{2,6},{4,0},{6,2},{8,12},{10,14},{12,8},{14,10},{16,20},{18,... | collective-permute-start | bytes 3538952 | tf_op jit(solution)/shard_map/ppermute | solution.py:767
  295.8 16.3 %collective-permute-start.71 = (bf16[4,96,768]{2,1,0:T(8,128)(2,1)S(1)}, bf16[4,96,768]{2,1,0:T(8,128)(2,1)}, u32[]{:S(2)}, u32[]{:S(2)}) collective-permute-start(bf16[4,96,768]{2,1,0:T(8,128)(2,1)S(1)} %pad_maximum_fusion.5.own_ref), channel_id=1, source_target_pairs={{0,8},{2,10},{4,12},{6,14},{8,0},{10,2},{12,4},{14,6},{16,24},{18,... | collective-permute-start | bytes 1769480 | tf_op jit(solution)/shard_map/ppermute | solution.py:767
  297.3 26.2 %collective-permute-start.69 = (bf16[4,96,768]{2,1,0:T(8,128)(2,1)S(1)}, bf16[4,96,768]{2,1,0:T(8,128)(2,1)}, u32[]{:S(2)}, u32[]{:S(2)}) collective-permute-start(bf16[4,96,768]{2,1,0:T(8,128)(2,1)S(1)} %pad_maximum_fusion.6.own_ref), channel_id=1, source_target_pairs={{0,8},{2,10},{4,12},{6,14},{8,0},{10,2},{12,4},{14,6},{16,24},{18,... | collective-permute-start | bytes 1769480 | tf_op jit(solution)/shard_map/ppermute | solution.py:767
  318.4 13.5 %collective-permute-start.78 = (bf16[4,192,768]{2,1,0:T(8,128)(2,1)S(1)}, bf16[4,192,768]{2,1,0:T(8,128)(2,1)}, u32[]{:S(2)}, u32[]{:S(2)}) collective-permute-start(bf16[4,192,768]{2,1,0:T(8,128)(2,1)S(1)} %collective-permute-done.70.own_ref), channel_id=1, source_target_pairs={{0,1},{1,0},{2,3},{3,2},{4,5},{5,4},{6,7},{7,6},{8,9},{9,8},{10,11... | collective-permute-start | bytes 3538952 | tf_op jit(solution)/shard_map/ppermute | solution.py:762
  323.6 17.3 %collective-permute-start.76 = (bf16[4,48,3072]{2,1,0:T(8,128)(2,1)S(1)}, bf16[4,48,3072]{2,1,0:T(8,128)(2,1)S(1)}, u32[]{:S(2)}, u32[]{:S(2)}) collective-permute-start(bf16[4,48,3072]{2,1,0:T(8,128)(2,1)S(1)} %collective-permute-done.68.own_ref), channel_id=1, source_target_pairs={{0,1},{1,0},{2,3},{3,2},{4,5},{5,4},{6,7},{7,6},{8,9},{9,8},{10,11... | collective-permute-start | bytes 3538952 | tf_op jit(solution)/shard_map/ppermute | solution.py:762
  324.1 12.6 %collective-permute-start.77 = (bf16[4,96,768]{2,1,0:T(8,128)(2,1)}, bf16[4,96,768]{2,1,0:T(8,128)(2,1)}, u32[]{:S(2)}, u32[]{:S(2)}) collective-permute-start(bf16[4,96,768]{2,1,0:T(8,128)(2,1)} %collective-permute-done.69.own_ref), channel_id=1, source_target_pairs={{0,1},{1,0},{2,3},{3,2},{4,5},{5,4},{6,7},{7,6},{8,9},{9,8},{10,11... | collective-permute-start | bytes 1769480 | tf_op jit(solution)/shard_map/ppermute | solution.py:762
  325.4 18.7 %collective-permute-start.63 = (bf16[104,768]{1,0:T(8,128)(2,1)S(1)}, bf16[104,768]{1,0:T(8,128)(2,1)S(1)}, u32[]{:S(2)}, u32[]{:S(2)}) collective-permute-start(bf16[104,768]{1,0:T(8,128)(2,1)S(1)} %copy-done.62), channel_id=1, source_target_pairs={{0,1},{1,0},{2,3},{3,2},{4,5},{5,4},{6,7},{7,6},{8,9},{9,8},{10,11... | collective-permute-start | bytes 479240 | tf_op jit(solution)/shard_map/ppermute | solution.py:762
  (98 other events, 982.8 us)
